TPU v7x, 128 devices: a whole 4x4x4 slice. The times are simulated.
128 devices in a mesh: seq: 8 (over z, core), dp: 16 (over y, x).
Axes of the slice: x: 4, y: 4, z: 4, core: 2. Of those that a mesh axis runs over, the one named last changes fastest.
Arguments:
- qkv: bfloat16 [16, 3, 1024, 16, 128], P('dp', None, 'seq'), may hold values from -14 to 14
- cotangent: bfloat16 [16, 1024, 3072], P('dp', 'seq'), may hold values from -6 to 6
- w_proj: bfloat16 [2048, 3072], replicated, may hold values from -0.125 to 0.125
- clip_levels: float32 [3072], replicated, may hold values from 0.03 to 0.3
Outputs:
- grad_qkv: bfloat16 [16, 3, 1024, 16, 128], P('dp', None, 'seq')
- d_smooth: float32 [2048], replicated
- d_clip: float32 [3072], replicated
All inputs are finite; a program needn't handle non-finite values. Where the computation divides by a largest or mean magnitude, that divisor is 1e-20 or more.
Results may differ from a plain program's by a relative error of at most 0.03.
Values may be sent and summed in bfloat16 or wider, within the bound.
No kernel may reach another device: no remote copies, remote signals or barrier semaphores. Data moves between devices by JAX's collectives and lax.ppermute only.
A program may use at most 64 MiB of HBM per device.

v0:
```python
import math

import jax
import jax.numpy as jnp
from jax import lax
from jax.sharding import PartitionSpec as P

HEADS = 16
HEAD_DIM = 128


epsilon = 1e-05
act_fraction = 0.5


def block_weights(q_block, key_rows):
    scaling = HEAD_DIM ** (-0.5)
    scores = (
        jnp.einsum("hqd,hkd->hqk", q_block, key_rows, preferred_element_type=jnp.float32) * scaling
    )
    row_top = jnp.max(scores, axis=-1, keepdims=True)
    exponent = jnp.exp(scores - row_top)
    return exponent / jnp.sum(exponent, axis=-1, keepdims=True)


def block_count(length):
    return length // math.gcd(length, 512)


def to_blocks(tensor, number):
    return tensor.reshape(
        tensor.shape[0], number, tensor.shape[1] // number, tensor.shape[2]
    ).transpose(1, 0, 2, 3)


def from_blocks(tensor):
    return tensor.transpose(1, 0, 2, 3).reshape(
        tensor.shape[1], tensor.shape[0] * tensor.shape[2], tensor.shape[3]
    )


def attend_forward(queries, key_rows, values):
    number = block_count(queries.shape[1])

    def one_block(q_block):
        weights = block_weights(q_block, key_rows)
        mixed = jnp.einsum(
            "hqk,hkd->hqd", weights.astype(jnp.bfloat16), values, preferred_element_type=jnp.float32
        )
        return mixed.astype(jnp.bfloat16)

    return from_blocks(lax.map(one_block, to_blocks(queries, number)))


def attend_backward(queries, key_rows, values, outputs, cot_heads):
    scaling = HEAD_DIM ** (-0.5)
    number = block_count(queries.shape[1])

    def one_block(running, block_items):
        q_block, out_block, cot_block = block_items
        weights = block_weights(q_block, key_rows)
        grad_weights = jnp.einsum(
            "hqd,hkd->hqk", cot_block, values, preferred_element_type=jnp.float32
        )
        row_delta = jnp.sum(
            cot_block.astype(jnp.float32) * out_block.astype(jnp.float32), axis=-1, keepdims=True
        )
        grad_scores = (weights * (grad_weights - row_delta)).astype(jnp.bfloat16)
        grad_query = scaling * jnp.einsum(
            "hqk,hkd->hqd", grad_scores, key_rows, preferred_element_type=jnp.float32
        )
        key_sum = running[0] + jnp.einsum(
            "hqk,hqd->hkd", grad_scores, q_block, preferred_element_type=jnp.float32
        )
        value_sum = running[1] + jnp.einsum(
            "hqk,hqd->hkd",
            weights.astype(jnp.bfloat16),
            cot_block,
            preferred_element_type=jnp.float32,
        )
        return ((key_sum, value_sum), grad_query.astype(jnp.bfloat16))

    zero_sums = jnp.zeros(key_rows.shape, jnp.float32)
    block_items = (
        to_blocks(queries, number),
        to_blocks(outputs, number),
        to_blocks(cot_heads, number),
    )
    (key_sum, value_sum), grad_blocks = lax.scan(one_block, (zero_sums, zero_sums), block_items)
    return (
        from_blocks(grad_blocks),
        (scaling * key_sum).astype(jnp.bfloat16),
        value_sum.astype(jnp.bfloat16),
    )


def smoothing(out_float, weight_float, act_max, act_clip_of):
    weight_max = jnp.max(jnp.abs(weight_float), axis=1)
    smooth = jnp.sqrt((act_max + epsilon) / (weight_max + epsilon))
    bound = jnp.max(jnp.sqrt((act_max + epsilon) * (weight_max + epsilon)))
    act_clip = act_fraction * act_clip_of(bound)
    act_tanh = jnp.tanh(out_float / smooth / act_clip)
    act_quant = (act_clip * act_tanh).astype(jnp.bfloat16)
    return (smooth, act_tanh, act_quant)


def weight_side(weight_float, smooth, clip_levels):
    ratio = smooth[:, None] * weight_float / clip_levels[None, :]
    weight_tanh = jnp.tanh(ratio)
    weight_quant = (clip_levels[None, :] * weight_tanh).astype(jnp.bfloat16)
    return (ratio, weight_tanh, weight_quant)


def gradient_terms(
    grad_act, grad_weight, out_float, weight_float, smooth, act_tanh, ratio, weight_tanh
):
    weight_slope = 1.0 - weight_tanh * weight_tanh
    clip_part = jnp.sum(grad_weight * (weight_tanh - ratio * weight_slope), axis=0)
    grad_smoothed = grad_act * (1.0 - act_tanh * act_tanh)
    weight_part = jnp.sum(grad_weight * weight_slope * weight_float, axis=1)
    act_part = jnp.sum(grad_smoothed * out_float, axis=0) / (smooth * smooth)
    grad_out = (grad_smoothed / smooth).astype(jnp.bfloat16)
    return (weight_part - act_part, clip_part, grad_out)


def per_device(qkv, cotangent, w_proj, clip_levels):
    heads_layout = lax.all_to_all(qkv, "seq", split_axis=3, concat_axis=2, tiled=True)
    local_heads = heads_layout[0].transpose(0, 2, 1, 3)
    queries = local_heads[0]
    key_rows = local_heads[1]
    values = local_heads[2]
    outputs = attend_forward(queries, key_rows, values)
    token_layout = lax.all_to_all(
        outputs.transpose(1, 0, 2)[None], "seq", split_axis=1, concat_axis=2, tiled=True
    )
    token_count = token_layout.shape[1]
    out_float = token_layout[0].reshape(token_count, HEADS * HEAD_DIM).astype(jnp.float32)
    act_max = lax.pmax(jnp.max(jnp.abs(out_float), axis=0), ("seq", "dp"))
    weight_float = w_proj.astype(jnp.float32)
    smooth, act_tanh, act_quant = smoothing(out_float, weight_float, act_max, lambda bound: bound)
    ratio, weight_tanh, weight_quant = weight_side(weight_float, smooth, clip_levels)
    cot_rows = cotangent[0]
    grad_act = lax.dot_general(
        cot_rows, weight_quant, (((1,), (1,)), ((), ())), preferred_element_type=jnp.float32
    )
    grad_weight = lax.dot_general(
        act_quant, cot_rows, (((0,), (0,)), ((), ())), preferred_element_type=jnp.float32
    )
    smooth_part, clip_part, grad_out = gradient_terms(
        grad_act, grad_weight, out_float, weight_float, smooth, act_tanh, ratio, weight_tanh
    )
    d_smooth, d_clip = lax.psum((smooth_part, clip_part), ("seq", "dp"))
    grad_tokens = grad_out.reshape(1, token_count, HEADS, HEAD_DIM)
    grad_heads = lax.all_to_all(grad_tokens, "seq", split_axis=2, concat_axis=1, tiled=True)
    cot_heads = grad_heads[0].transpose(1, 0, 2)
    grad_query, grad_key, grad_value = attend_backward(
        queries, key_rows, values, outputs, cot_heads
    )
    stacked = jnp.stack((grad_query, grad_key, grad_value), axis=0).transpose(0, 2, 1, 3)[None]
    grad_qkv = lax.all_to_all(stacked, "seq", split_axis=2, concat_axis=3, tiled=True)
    return (grad_qkv, d_smooth, d_clip)


def solution(mesh):
    in_specs = (P("dp", None, "seq", None, None), P("dp", "seq", None), P(), P())
    out_specs = (P("dp", None, "seq", None, None), P(), P())
    return jax.shard_map(
        per_device, mesh=mesh, in_specs=in_specs, out_specs=out_specs, check_vma=False
    )
```

profile of v0, /device:TPU:0, one launch (start us, length us, event | category | flops | bytes accessed | tf_op | source)
XLA Modules:
  0.0 269.7 jit_solution(16431919477965766835)
XLA Ops:
  0.6 0.0 copy-start
  0.6 3.0 %copy.53 = bf16[1,3,128,16,128]{4,2,1,0,3:T(8,128)(2,1)} copy(bf16[1,3,128,16,128]{4,3,2,1,0:T(8,128)(2,1)} %param.8) | data formatting | bytes 3145728 | tf_op args[0]
  3.7 5.4 %all-to-all-start = ((bf16[1,3,128,16,128]{4,2,1,0,3:T(8,128)(2,1)}), bf16[1,3,128,16,128]{4,2,1,0,3:T(8,128)(2,1)S(1)}, u32[]{:S(2)}, u32[]{:S(2)}) async-start(bf16[1,3,128,16,128]{4,2,1,0,3:T(8,128)(2,1)} %copy.53), calls=%async_computation | async-start | bytes 3145728 | tf_op jit(solution)/shard_map/all_to_all | solution.py:127
  9.1 21.6 %all-to-all-done = bf16[1,3,128,16,128]{4,2,1,0,3:T(8,128)(2,1)S(1)} async-done(((bf16[1,3,128,16,128]{4,2,1,0,3:T(8,128)(2,1)}), bf16[1,3,128,16,128]{4,2,1,0,3:T(8,128)(2,1)S(1)}, u32[]{:S(2)}, u32[]{:S(2)}) %all-to-all-start) | async-done | bytes 1572896 | tf_op jit(solution)/shard_map/all_to_all | solution.py:127
  30.7 0.2 copy.54
  30.8 0.1 slice_bitcast_fusion
  31.0 12.6 %while.25 = (s32[]{:T(128)}, bf16[2,2,512,128]{3,2,1,0:T(8,128)(2,1)S(1)}, bf16[2,2,512,128]{3,2,1,0:T(8,128)(2,1)S(1)}, bf16[2,1024,128]{2,1,0:T(8,128)(2,1)S(1)}, bf16[2,1024,128]{2,1,0:T(8,128)(2,1)S(1)}, /*index=5*/s32[]{:T(128)}) while((s32[]{:T(128)}, bf16[2,2,512,128]{3,2,1,0:T(8,128)(2,1)S(1)}, bf16[2,2,512,128]{3,2,1,0:T(8,128)(2,1)S(1)}, ...), condition=%wide.region_3.4_spmd, body=%wide.region_0.3_spmd.sunk | while | flops 542245888 | bytes 9969741 | solution.py:52
  31.0 3.3 %fusion.132 = (f32[2,512]{1,0:T(2,128)S(1)}, f32[2,512,1024]{2,1,0:T(8,128)}) fusion(bf16[2,1024,128]{2,1,0:T(8,128)(2,1)S(1)} %get-tuple-element.305, bf16[2,2,512,128]{3,2,1,0:T(8,128)(2,1)S(1)} %get-tuple-element.304, s32[]{:T(128)} %get-tuple-element.296), kind=kOutput, calls=%fused_computation.96.clone.1 | convolution fusion | flops 271582208 | bytes 4984836 | tf_op jit(solution)/shard_map/while/body/eval_jaxpr/sub | solution.py:22
  34.3 3.0 %fusion.133 = bf16[2,2,512,128]{3,2,1,0:T(8,128)(2,1)S(1)} fusion(bf16[2,2,512,128]{3,2,1,0:T(8,128)(2,1)S(1)} %get-tuple-element.297, s32[]{:T(128)} %get-tuple-element.296, bf16[2,1024,128]{2,1,0:T(8,128)(2,1)S(1)} %get-tuple-element.306, f32[2,512,1024]{2,1,0:T(8,128)} %get-tuple-element.277, f32[2,512]{1,0:T(2,128)S(1)} %get-tuple-element.278), kind=kOutput, calls=%fused_computation.9.clone.1 | convolution fusion | flops 270663680 | bytes 4984836 | tf_op jit(solution)/shard_map/while/body/eval_jaxpr/hqk,hkd->hqd/dot_general | solution.py:47
  37.3 3.3 %fusion.132 = (f32[2,512]{1,0:T(2,128)S(1)}, f32[2,512,1024]{2,1,0:T(8,128)}) fusion(bf16[2,1024,128]{2,1,0:T(8,128)(2,1)S(1)} %get-tuple-element.305, bf16[2,2,512,128]{3,2,1,0:T(8,128)(2,1)S(1)} %get-tuple-element.304, s32[]{:T(128)} %get-tuple-element.296), kind=kOutput, calls=%fused_computation.96.clone.1 | convolution fusion | flops 271582208 | bytes 4984836 | tf_op jit(solution)/shard_map/while/body/eval_jaxpr/sub | solution.py:22
  40.6 3.0 %fusion.133 = bf16[2,2,512,128]{3,2,1,0:T(8,128)(2,1)S(1)} fusion(bf16[2,2,512,128]{3,2,1,0:T(8,128)(2,1)S(1)} %get-tuple-element.297, s32[]{:T(128)} %get-tuple-element.296, bf16[2,1024,128]{2,1,0:T(8,128)(2,1)S(1)} %get-tuple-element.306, f32[2,512,1024]{2,1,0:T(8,128)} %get-tuple-element.277, f32[2,512]{1,0:T(2,128)S(1)} %get-tuple-element.278), kind=kOutput, calls=%fused_computation.9.clone.1 | convolution fusion | flops 270663680 | bytes 4984836 | tf_op jit(solution)/shard_map/while/body/eval_jaxpr/hqk,hkd->hqd/dot_general | solution.py:47
  43.7 1.3 copy.57
  45.0 3.5 %all-to-all-start.1 = ((bf16[1,1024,2,128]{3,2,0,1:T(2,128)(2,1)}), bf16[1,1024,2,128]{3,2,0,1:T(2,128)(2,1)S(1)}, u32[]{:S(2)}, u32[]{:S(2)}) async-start(bf16[1,1024,2,128]{3,2,0,1:T(2,128)(2,1)} %copy.57), calls=%async_computation.1 | async-start | bytes 1048576 | tf_op jit(solution)/shard_map/all_to_all | solution.py:133
  48.5 7.1 %fusion.68 = f32[2048]{0:T(1024)S(1)} fusion(bf16[2048,3072]{1,0:T(8,128)(2,1)} %param.10), kind=kLoop, calls=%fused_computation.57 | loop fusion | flops 18872320 | bytes 12591104 | tf_op jit(solution)/shard_map/reduce_max | solution.py:98
  55.6 3.2 %all-to-all-done.1 = bf16[1,1024,2,128]{3,2,0,1:T(2,128)(2,1)S(1)} async-done(((bf16[1,1024,2,128]{3,2,0,1:T(2,128)(2,1)}), bf16[1,1024,2,128]{3,2,0,1:T(2,128)(2,1)S(1)}, u32[]{:S(2)}, u32[]{:S(2)}) %all-to-all-start.1) | async-done | bytes 524320 | tf_op jit(solution)/shard_map/all_to_all | solution.py:133
  58.8 0.1 fusion.99
  58.9 0.1 fusion.75
  59.1 65.0 %pmax.7 = f32[2048]{0:T(1024)S(1)} all-reduce(f32[2048]{0:T(1024)S(1)} %bitcast.185), channel_id=1, replica_groups=mesh['seq'=8,'dp'=16] {'seq','dp'}, use_global_device_ids=true, to_apply=%region_5.6 | all-reduce | flops 2048 | bytes 16384 | tf_op jit(solution)/shard_map/pmax | solution.py:138
  124.0 0.6 sqrt_reduce_fusion
  125.3 1.3 copy.60
  126.6 1.6 fusion.81
  128.2 8.1 %fusion.82 = (f32[2048]{0:T(1024)S(1)}, bf16[128,2048]{0,1:T(8,128)(2,1)S(1)}) fusion(f32[1,128,8,2,128]{1,4,3,2,0:T(8,128)} %copy.60, f32[2048]{0:T(1024)S(1)} %get-tuple-element.182, f32[128,2048]{0,1:T(8,128)S(1)} %fusion.81, bf16[1,128,3072]{2,1,0:T(8,128)(2,1)S(1)} %copy-done, f32[3072]{0:T(1024)S(1)} %copy-done.6, bf16[2048,3072]{1,0:T(8,128)(2,1)} %param.10), kind=kOutput, calls=%fused_computation.80 | convolution fusion | flops 1643378688 | bytes 16019456 | tf_op jit(solution)/shard_map/dot_general | solution.py:143
  136.3 1.0 copy.61
  137.4 4.3 %all-to-all-start.2 = ((bf16[1,128,16,128]{3,1,0,2:T(8,128)(2,1)}), bf16[1,128,16,128]{3,1,0,2:T(8,128)(2,1)}, u32[]{:S(2)}, u32[]{:S(2)}) async-start(bf16[1,128,16,128]{3,1,0,2:T(8,128)(2,1)} %copy.61), calls=%async_computation.2 | async-start | bytes 1048576 | tf_op jit(solution)/shard_map/all_to_all | solution.py:154
  141.7 1.0 fusion.87
  142.7 2.1 copy.68
  144.8 7.1 %all-to-all-done.2 = bf16[1,128,16,128]{3,1,0,2:T(8,128)(2,1)} async-done(((bf16[1,128,16,128]{3,1,0,2:T(8,128)(2,1)}), bf16[1,128,16,128]{3,1,0,2:T(8,128)(2,1)}, u32[]{:S(2)}, u32[]{:S(2)}) %all-to-all-start.2) | async-done | bytes 524320 | tf_op jit(solution)/shard_map/all_to_all | solution.py:154
  151.9 1.1 copy.62
  152.9 25.2 %while.26 = (s32[]{:T(128)}, f32[2,1024,128]{2,1,0:T(8,128)S(1)}, f32[2,1024,128]{2,1,0:T(8,128)}, bf16[2,2,512,128]{3,2,0,1:T(8,128)(2,1)}, bf16[2,2,512,128]{3...) while((s32[]{:T(128)}, f32[2,1024,128]{2,1,0:T(8,128)S(1)}, ...), condition=%wide.region_12.13_spmd.clone, body=%wide.region_8.12_spmd.clone.sunk | while | flops 1353449472 | bytes 47469276 | solution.py:89
  153.0 4.3 %fusion.145 = (f32[2,512]{1,0:T(2,128)S(1)}, f32[2,512,1024]{2,1,0:T(8,128)}) fusion(bf16[2,1024,128]{2,1,0:T(8,128)(2,1)} %get-tuple-element.335, bf16[2,2,512,128]{3,2,1,0:T(8,128)(2,1)S(1)} %get-tuple-element.334, s32[]{:T(128)} %get-tuple-element.319), kind=kOutput, calls=%fused_computation.97.clone.1 | convolution fusion | flops 271582208 | bytes 4984836 | tf_op jit(solution)/shard_map/while/body/eval_jaxpr/sub | solution.py:22
  157.3 4.3 %fusion.146 = f32[2,1024,128]{2,1,0:T(8,128)} fusion(f32[2,512,1024]{2,1,0:T(8,128)} %get-tuple-element.288, f32[2,512]{1,0:T(2,128)S(1)} %get-tuple-element.289, f32[2,1024,128]{2,1,0:T(8,128)} %get-tuple-element.321, pred[]{:T(512)S(6)} %compare.3, bf16[2,2,512,128]{3,2,0,1:T(8,128)(2,1)S(1)} %get-tuple-element.336, s32[]{:T(128)} %get-tuple-element.319), kind=kOutput, calls=%fused_computation.29.clone.1 | convolution fusion | flops 271056896 | bytes 6557701 | tf_op jit(solution)/shard_map/while/body/eval_jaxpr/hqk,hqd->hkd/dot_general | solution.py:75
  161.6 0.2 fusion.144
  161.9 0.8 multiply_convert_fusion.9
  162.7 1.3 convolution_add_fusion.2
  164.0 1.4 fusion.147
  165.4 4.3 %fusion.145 = (f32[2,512]{1,0:T(2,128)S(1)}, f32[2,512,1024]{2,1,0:T(8,128)}) fusion(bf16[2,1024,128]{2,1,0:T(8,128)(2,1)} %get-tuple-element.335, bf16[2,2,512,128]{3,2,1,0:T(8,128)(2,1)S(1)} %get-tuple-element.334, s32[]{:T(128)} %get-tuple-element.319), kind=kOutput, calls=%fused_computation.97.clone.1 | convolution fusion | flops 271582208 | bytes 4984836 | tf_op jit(solution)/shard_map/while/body/eval_jaxpr/sub | solution.py:22
  169.7 4.6 %fusion.146 = f32[2,1024,128]{2,1,0:T(8,128)} fusion(f32[2,512,1024]{2,1,0:T(8,128)} %get-tuple-element.288, f32[2,512]{1,0:T(2,128)S(1)} %get-tuple-element.289, f32[2,1024,128]{2,1,0:T(8,128)} %get-tuple-element.321, pred[]{:T(512)S(6)} %compare.3, bf16[2,2,512,128]{3,2,0,1:T(8,128)(2,1)S(1)} %get-tuple-element.336, s32[]{:T(128)} %get-tuple-element.319), kind=kOutput, calls=%fused_computation.29.clone.1 | convolution fusion | flops 271056896 | bytes 6557701 | tf_op jit(solution)/shard_map/while/body/eval_jaxpr/hqk,hqd->hkd/dot_general | solution.py:75
  174.4 0.2 fusion.144
  174.6 0.8 multiply_convert_fusion.9
  175.4 1.3 convolution_add_fusion.2
  176.7 1.4 fusion.147
  178.2 1.4 fusion.86
  179.6 1.2 maximum_bitcast_fusion
  180.8 2.8 %copy.65 = bf16[1,3,1024,2,128]{4,3,1,0,2:T(2,128)(2,1)} copy(bf16[1,3,1024,2,128]{4,2,3,1,0:T(8,128)(2,1)S(1)} %maximum_bitcast_fusion) | data formatting | bytes 3145728 | tf_op jit(solution)/shard_map/broadcast_in_dim | solution.py:159
  183.6 3.6 %all-to-all-start.3 = ((bf16[1,3,1024,2,128]{4,3,1,0,2:T(2,128)(2,1)}), bf16[1,3,1024,2,128]{4,3,1,0,2:T(2,128)(2,1)S(1)}, u32[]{:S(2)}, u32[]{:S(2)}) async-start(bf16[1,3,1024,2,128]{4,3,1,0,2:T(2,128)(2,1)} %copy.65), calls=%async_computation.3 | async-start | bytes 3145728 | tf_op jit(solution)/shard_map/all_to_all | solution.py:160
  187.2 14.7 %multiply_reduce_fusion.2 = (f32[3072]{0:T(1024)S(1)}, f32[2048]{0:T(1024)S(1)}) fusion(f32[3072]{0:T(1024)S(1)} %copy-done.6, bf16[2048,3072]{1,0:T(8,128)(2,1)} %param.10, f32[2048]{0:T(1024)S(1)} %get-tuple-element.182, bf16[128,2048]{0,1:T(8,128)(2,1)S(1)} %bitcast.182, bf16[1,128,3072]{2,1,0:T(8,128)(2,1)S(1)} %copy-done), kind=kOutput, calls=%fused_computation.60 | convolution fusion | flops 1686105088 | bytes 13934592 | tf_op jit(solution)/shard_map/dot_general | solution.py:146
  201.9 65.6 %all-reduce = (f32[2048]{0:T(1024)}, f32[3072]{0:T(1024)}) all-reduce(f32[2048]{0:T(1024)S(1)} %divide_subtract_fusion, f32[3072]{0:T(1024)S(1)} %get-tuple-element.149), channel_id=1, replica_groups=mesh['seq'=8,'dp'=16] {'seq','dp'}, use_global_device_ids=true, to_apply=%region_15.16 | all-reduce | flops 5120 | bytes 40960 | tf_op jit(solution)/shard_map/psum | solution.py:152
  267.5 2.2 copy.66
  (32 shorter events, 0.2 us)
Async XLA Ops:
  0.6 127.6 %copy-start = (bf16[1,128,3072]{2,1,0:T(8,128)(2,1)S(1)}, bf16[1,128,3072]{2,1,0:T(8,128)(2,1)}, u32[]{:S(2)}) copy-start(bf16[1,128,3072]{2,1,0:T(8,128)(2,1)} %param.9) | copy-start | bytes 2359300
  3.7 27.0 %all-to-all-start = ((bf16[1,3,128,16,128]{4,2,1,0,3:T(8,128)(2,1)}), bf16[1,3,128,16,128]{4,2,1,0,3:T(8,128)(2,1)S(1)}, u32[]{:S(2)}, u32[]{:S(2)}) async-start(bf16[1,3,128,16,128]{4,2,1,0,3:T(8,128)(2,1)} %copy.53), calls=%async_computation | async-start | bytes 3145728 | tf_op jit(solution)/shard_map/all_to_all | solution.py:127
  43.6 12.0 %copy-start.2 = (bf16[2,1024,128]{2,1,0:T(8,128)(2,1)}, bf16[2,1024,128]{2,1,0:T(8,128)(2,1)S(1)}, u32[]{:S(2)}) copy-start(bf16[2,1024,128]{2,1,0:T(8,128)(2,1)S(1)} %get-tuple-element.349) | copy-start | bytes 1572868
  43.6 12.0 %copy-start.4 = (bf16[2,1024,128]{2,1,0:T(8,128)(2,1)}, bf16[2,1024,128]{2,1,0:T(8,128)(2,1)S(1)}, u32[]{:S(2)}) copy-start(bf16[2,1024,128]{2,1,0:T(8,128)(2,1)S(1)} %get-tuple-element.350) | copy-start | bytes 1572868
  45.0 13.8 %all-to-all-start.1 = ((bf16[1,1024,2,128]{3,2,0,1:T(2,128)(2,1)}), bf16[1,1024,2,128]{3,2,0,1:T(2,128)(2,1)S(1)}, u32[]{:S(2)}, u32[]{:S(2)}) async-start(bf16[1,1024,2,128]{3,2,0,1:T(2,128)(2,1)} %copy.57), calls=%async_computation.1 | async-start | bytes 1048576 | tf_op jit(solution)/shard_map/all_to_all | solution.py:133
  55.6 72.6 %copy-start.6 = (f32[3072]{0:T(1024)S(1)}, f32[3072]{0:T(1024)}, u32[]{:S(2)}) copy-start(f32[3072]{0:T(1024)} %param.11) | copy-start | bytes 36868
  137.4 14.5 %all-to-all-start.2 = ((bf16[1,128,16,128]{3,1,0,2:T(8,128)(2,1)}), bf16[1,128,16,128]{3,1,0,2:T(8,128)(2,1)}, u32[]{:S(2)}, u32[]{:S(2)}) async-start(bf16[1,128,16,128]{3,1,0,2:T(8,128)(2,1)} %copy.61), calls=%async_computation.2 | async-start | bytes 1048576 | tf_op jit(solution)/shard_map/all_to_all | solution.py:154
  157.3 4.6 %copy-start.3 = (bf16[2,1024,128]{2,1,0:T(8,128)(2,1)S(1)}, bf16[2,1024,128]{2,1,0:T(8,128)(2,1)}, u32[]{:S(2)}) copy-start(bf16[2,1024,128]{2,1,0:T(8,128)(2,1)} %get-tuple-element.337) | copy-start | bytes 1572868 | tf_op jit(solution)/shard_map/while
  157.3 4.6 %copy-start.7 = (f32[2,512,1024]{2,1,0:T(8,128)S(1)}, f32[2,512,1024]{2,1,0:T(8,128)}, u32[]{:S(2)}) copy-start(f32[2,512,1024]{2,1,0:T(8,128)} %get-tuple-element.288) | copy-start | bytes 12582916 | tf_op jit(solution)/shard_map/while
  162.7 1.3 copy-start.5
  169.7 4.9 %copy-start.3 = (bf16[2,1024,128]{2,1,0:T(8,128)(2,1)S(1)}, bf16[2,1024,128]{2,1,0:T(8,128)(2,1)}, u32[]{:S(2)}) copy-start(bf16[2,1024,128]{2,1,0:T(8,128)(2,1)} %get-tuple-element.337) | copy-start | bytes 1572868 | tf_op jit(solution)/shard_map/while
  169.7 4.9 %copy-start.7 = (f32[2,512,1024]{2,1,0:T(8,128)S(1)}, f32[2,512,1024]{2,1,0:T(8,128)}, u32[]{:S(2)}) copy-start(f32[2,512,1024]{2,1,0:T(8,128)} %get-tuple-element.288) | copy-start | bytes 12582916 | tf_op jit(solution)/shard_map/while
  175.4 1.3 copy-start.5
  180.8 6.4 %copy-start.1 = (bf16[1,128,8,2,128]{1,4,3,2,0:T(8,128)(2,1)S(1)}, bf16[1,128,8,2,128]{1,4,3,2,0:T(8,128)(2,1)}, u32[]{:S(2)}) copy-start(bf16[1,128,8,2,128]{1,4,3,2,0:T(8,128)(2,1)} %copy.68) | copy-start | bytes 1572868
  183.6 83.9 %all-to-all-start.3 = ((bf16[1,3,1024,2,128]{4,3,1,0,2:T(2,128)(2,1)}), bf16[1,3,1024,2,128]{4,3,1,0,2:T(2,128)(2,1)S(1)}, u32[]{:S(2)}, u32[]{:S(2)}) async-start(bf16[1,3,1024,2,128]{4,3,1,0,2:T(2,128)(2,1)} %copy.65), calls=%async_computation.3 | async-start | bytes 3145728 | tf_op jit(solution)/shard_map/all_to_all | solution.py:160
where the time goes:
time: 271 us; the launch traced here: 270 us
  blocking collectives  131 us (48%)
  matrix products  60.1 us (22%)
  waiting for transfers between devices  31.8 us (12%)
  starting transfers between devices  16.8 us (6%)
  local copies, waits for them, and re-layouts  15.2 us (6%)
  other arithmetic  13.6 us (5%)
    psum x1, blocking collectives, per_device(): d_smooth, d_clip = lax.psum((smooth_part, clip_part), ('seq', 'dp'))  65.6 us
    pmax x1, blocking collectives, per_device(): act_max = lax.pmax(jnp.max(jnp.abs(out_float), axis=0), ('seq', 'dp'))  65 us
    all_to_all x1, waiting for transfers between devices, per_device(): lax.all_to_all(qkv, 'seq', split_axis=3, concat_axis=2, tiled=True)  21.6 us
    sub x4, matrix products, block_weights(): exponent = jnp.exp(scores - row_top)  15.3 us
    dot_general x1, matrix products, per_device(): lax.dot_general(act_quant, cot_rows, (((0,), (0,)), ((), ())), preferred_...  14.7 us
    dot_general x2, matrix products, one_block(): jnp.einsum('hqk,hqd->hkd', weights.astype(jnp.bfloat16), cot_block, prefe...  8.98 us
    dot_general x1, matrix products, per_device(): lax.dot_general(cot_rows, weight_quant, (((1,), (1,)), ((), ())), preferr...  8.13 us
    reduce_max x1, other arithmetic, smoothing(): weight_max = jnp.max(jnp.abs(weight_float), axis=1)  7.07 us
  transfers between devices with their start and end apart: 4, of which 3 were waited for; matrix products, arithmetic and copies ran while one was open for 9% of the time, Pallas kernels for 0%

commit v1 on v0

v1 whole, which is shorter than its diff:
```python
import math

import jax
import jax.numpy as jnp
from jax import lax
from jax.experimental import pallas as pl
from jax.experimental.pallas import tpu as pltpu
from jax.sharding import PartitionSpec as P

HEADS = 16
HEAD_DIM = 128
SEQ = 8
DP = 16
LOCAL_HEADS = 2
CHANNELS = LOCAL_HEADS * HEAD_DIM
TOKENS = 128
LEN = 1024
D = 3072
BLOCK = 256
NUM_BLOCKS = LEN // BLOCK
epsilon = 1e-05
act_fraction = 0.5
SCALE = HEAD_DIM ** (-0.5)
EXP2_SCALE = SCALE * math.log2(math.e)

NN = (((1,), (0,)), ((), ()))
NT = (((1,), (1,)), ((), ()))
TN = (((0,), (0,)), ((), ()))
MIB = 1 << 20


def dot(lhs, rhs, dims):
    return lax.dot_general(lhs, rhs, dims, preferred_element_type=jnp.float32)


def to_row(column):
    return jnp.broadcast_to(column, (column.shape[0], 128)).T[0:1]


def to_column(row):
    return jnp.broadcast_to(row, (128, row.shape[1])).T[:, 0:1]


def forward_kernel(y_ref, weight_max_ref, p_ref, out_ref, message_ref):
    keys = y_ref[:, 0, 1].reshape(LEN, HEAD_DIM)
    values = y_ref[:, 0, 2].reshape(LEN, HEAD_DIM)
    top = None
    for b in range(NUM_BLOCKS):
        queries = y_ref[2 * b : 2 * b + 2, 0, 0].reshape(BLOCK, HEAD_DIM)
        scores = dot(keys, queries, NT)
        row_top = jnp.max(scores, axis=0, keepdims=True)
        exponent = jnp.exp2((scores - row_top) * EXP2_SCALE)
        total = jnp.sum(exponent, axis=0, keepdims=True)
        weights = (exponent * (1.0 / total)).astype(jnp.bfloat16)
        columns = pl.ds(b * BLOCK, BLOCK)
        p_ref[0, :, columns] = weights
        mixed = dot(values, weights, TN).astype(jnp.bfloat16)
        out_ref[0, :, columns] = mixed
        block_top = jnp.max(jnp.abs(mixed.astype(jnp.float32)), axis=1, keepdims=True)
        top = block_top if top is None else jnp.maximum(top, block_top)
    act_row = to_row(top)
    bound = jnp.max(
        jnp.sqrt((act_row + epsilon) * (weight_max_ref[0] + epsilon)), axis=1, keepdims=True
    )
    message_ref[0, 0:1] = act_row
    message_ref[0, 1:2] = jnp.broadcast_to(bound, (1, 128))


def forward(heads, weight_max):
    return pl.pallas_call(
        forward_kernel,
        grid=(LOCAL_HEADS,),
        in_specs=[
            pl.BlockSpec((SEQ, 1, 3, TOKENS, HEAD_DIM), lambda h: (0, h, 0, 0, 0)),
            pl.BlockSpec((1, 1, 128), lambda h: (h, 0, 0)),
        ],
        out_specs=[
            pl.BlockSpec((1, LEN, LEN), lambda h: (h, 0, 0)),
            pl.BlockSpec((1, HEAD_DIM, LEN), lambda h: (h, 0, 0)),
            pl.BlockSpec((1, 2, 128), lambda h: (h, 0, 0)),
        ],
        out_shape=[
            jax.ShapeDtypeStruct((LOCAL_HEADS, LEN, LEN), jnp.bfloat16),
            jax.ShapeDtypeStruct((LOCAL_HEADS, HEAD_DIM, LEN), jnp.bfloat16),
            jax.ShapeDtypeStruct((LOCAL_HEADS, 2, 128), jnp.float32),
        ],
        compiler_params=pltpu.CompilerParams(vmem_limit_bytes=28 * MIB),
        cost_estimate=pl.CostEstimate(
            flops=2 * 2 * LOCAL_HEADS * LEN * LEN * HEAD_DIM,
            bytes_accessed=6 * MIB,
            transcendentals=LOCAL_HEADS * LEN * LEN,
        ),
        name="attend_forward",
    )(heads, weight_max)


def projection_kernel(
    place_ref,
    messages_ref,
    w_ref,
    clip_ref,
    cot_ref,
    out_ref,
    grad_ref,
    quant_ref,
    part_ref,
    smooth_ref,
    wq_ref,
    scale_ref,
):
    step = pl.program_id(0)

    @pl.when(step == 0)
    def _():
        everyone = messages_ref[...]
        bound = jnp.max(everyone[:, :, 1, :], axis=0)
        bound = jnp.max(bound, axis=0, keepdims=True)
        first = pl.multiple_of(place_ref[0] * DP, DP)
        mine = messages_ref[pl.ds(first, DP)]
        act_max = jnp.max(mine[:, :, 0, :], axis=0)
        act_column = jnp.concatenate(
            [to_column(act_max[0:1]), to_column(act_max[1:2])], axis=0
        )
        weight = w_ref[...].astype(jnp.float32)
        weight_max = jnp.max(jnp.abs(weight), axis=1, keepdims=True)
        smooth = jnp.sqrt((act_column + epsilon) / (weight_max + epsilon))
        smooth_ref[...] = jnp.broadcast_to(smooth, (CHANNELS, 128))
        scale_ref[...] = jnp.broadcast_to(act_fraction * bound, (8, 128))
        clip = clip_ref[...]
        tanh = jnp.tanh((smooth * weight) * (1.0 / clip))
        wq_ref[...] = (clip * tanh).astype(jnp.bfloat16)
        part_ref[...] = jnp.zeros((CHANNELS, 128), jnp.float32)

    smooth = smooth_ref[:, 0:1]
    act_clip = scale_ref[0:1, 0:1]
    cot = cot_ref[...].reshape(BLOCK, D)
    grad_act = dot(wq_ref[...], cot, NT)
    out = out_ref[...].reshape(CHANNELS, BLOCK).astype(jnp.float32)
    inverse = 1.0 / smooth
    tanh = jnp.tanh(out * (inverse / act_clip))
    quant_ref[...] = (act_clip * tanh).astype(jnp.bfloat16)
    smoothed = grad_act * (1.0 - tanh * tanh)
    part = jnp.sum(smoothed * out, axis=1, keepdims=True) * (inverse * inverse)
    part_ref[...] += jnp.broadcast_to(part, (CHANNELS, 128))
    grad_ref[...] = (
        (smoothed * inverse).astype(jnp.bfloat16).reshape(LOCAL_HEADS, HEAD_DIM, BLOCK)
    )


def projection(place, messages, w_proj, clip, cot, out):
    return pl.pallas_call(
        projection_kernel,
        grid_spec=pltpu.PrefetchScalarGridSpec(
            num_scalar_prefetch=1,
            grid=(NUM_BLOCKS,),
            in_specs=[
                pl.BlockSpec((SEQ * DP, LOCAL_HEADS, 2, 128), lambda t, place: (0, 0, 0, 0)),
                pl.BlockSpec((CHANNELS, D), lambda t, place: (place[0], 0)),
                pl.BlockSpec((1, D), lambda t, place: (0, 0)),
                pl.BlockSpec((2, TOKENS, D), lambda t, place: (t, 0, 0)),
                pl.BlockSpec((LOCAL_HEADS, HEAD_DIM, BLOCK), lambda t, place: (0, 0, t)),
            ],
            out_specs=[
                pl.BlockSpec((LOCAL_HEADS, HEAD_DIM, BLOCK), lambda t, place: (0, 0, t)),
                pl.BlockSpec((CHANNELS, BLOCK), lambda t, place: (0, t)),
                pl.BlockSpec((CHANNELS, 128), lambda t, place: (0, 0)),
                pl.BlockSpec((CHANNELS, 128), lambda t, place: (0, 0)),
            ],
            scratch_shapes=[
                pltpu.VMEM((CHANNELS, D), jnp.bfloat16),
                pltpu.VMEM((8, 128), jnp.float32),
            ],
        ),
        out_shape=[
            jax.ShapeDtypeStruct((LOCAL_HEADS, HEAD_DIM, LEN), jnp.bfloat16),
            jax.ShapeDtypeStruct((CHANNELS, LEN), jnp.bfloat16),
            jax.ShapeDtypeStruct((CHANNELS, 128), jnp.float32),
            jax.ShapeDtypeStruct((CHANNELS, 128), jnp.float32),
        ],
        compiler_params=pltpu.CompilerParams(vmem_limit_bytes=28 * MIB),
        cost_estimate=pl.CostEstimate(
            flops=2 * CHANNELS * LEN * D, bytes_accessed=9 * MIB, transcendentals=CHANNELS * D
        ),
        name="projection_backward",
    )(place, messages, w_proj, clip, cot, out)


def backward_kernel(y_ref, p_ref, out_ref, grad_ref, z_ref, ds_ref):
    keys = y_ref[:, 0, 1].reshape(LEN, HEAD_DIM)
    values = y_ref[:, 0, 2].reshape(LEN, HEAD_DIM)
    for b in range(NUM_BLOCKS):
        columns = pl.ds(b * BLOCK, BLOCK)
        grad_out = grad_ref[0, :, columns]
        delta = jnp.sum(
            grad_out.astype(jnp.float32) * out_ref[0, :, columns].astype(jnp.float32),
            axis=0,
            keepdims=True,
        )
        grad_weights = dot(values, grad_out, NN)
        weights = p_ref[0, :, columns].astype(jnp.float32)
        grad_scores = (weights * (grad_weights - delta)).astype(jnp.bfloat16)
        ds_ref[:, columns] = grad_scores
        grad_query = dot(keys, grad_scores, TN) * SCALE
        z_ref[2 * b : 2 * b + 2, 0, 0] = (
            grad_query.T.astype(jnp.bfloat16).reshape(2, TOKENS, HEAD_DIM)
        )
    queries = y_ref[:, 0, 0].reshape(LEN, HEAD_DIM)
    grad_value = dot(p_ref[0], grad_ref[0], NT)
    z_ref[:, 0, 2] = grad_value.astype(jnp.bfloat16).reshape(SEQ, TOKENS, HEAD_DIM)
    grad_key = dot(ds_ref[...], queries, NN) * SCALE
    z_ref[:, 0, 1] = grad_key.astype(jnp.bfloat16).reshape(SEQ, TOKENS, HEAD_DIM)


def backward(heads, weights, out, grad_out):
    return pl.pallas_call(
        backward_kernel,
        grid=(LOCAL_HEADS,),
        in_specs=[
            pl.BlockSpec((SEQ, 1, 3, TOKENS, HEAD_DIM), lambda h: (0, h, 0, 0, 0)),
            pl.BlockSpec((1, LEN, LEN), lambda h: (h, 0, 0)),
            pl.BlockSpec((1, HEAD_DIM, LEN), lambda h: (h, 0, 0)),
            pl.BlockSpec((1, HEAD_DIM, LEN), lambda h: (h, 0, 0)),
        ],
        out_specs=pl.BlockSpec((SEQ, 1, 3, TOKENS, HEAD_DIM), lambda h: (0, h, 0, 0, 0)),
        out_shape=jax.ShapeDtypeStruct(
            (SEQ, LOCAL_HEADS, 3, TOKENS, HEAD_DIM), jnp.bfloat16
        ),
        scratch_shapes=[pltpu.VMEM((LEN, LEN), jnp.bfloat16)],
        compiler_params=pltpu.CompilerParams(vmem_limit_bytes=28 * MIB),
        cost_estimate=pl.CostEstimate(
            flops=4 * 2 * LOCAL_HEADS * LEN * LEN * HEAD_DIM,
            bytes_accessed=8 * MIB,
            transcendentals=0,
        ),
        name="attend_backward",
    )(heads, weights, out, grad_out)


WIDTH = 512


def weight_kernel(place_ref, w_ref, clip_ref, cot_ref, quant_ref, part_ref, smooth_ref, vec_ref, acc_ref):
    step = pl.program_id(0)
    smooth = smooth_ref[:, 0:1]

    @pl.when(step == 0)
    def _():
        vec_ref[...] = jnp.zeros_like(vec_ref)
        acc_ref[...] = -part_ref[...]

    weight = w_ref[...].astype(jnp.float32)
    grad_weight = dot(quant_ref[...], cot_ref[...].reshape(LEN, WIDTH), NN)
    ratio = (smooth * weight) * (1.0 / clip_ref[...])
    tanh = jnp.tanh(ratio)
    slope = 1.0 - tanh * tanh
    clip_part = jnp.sum(grad_weight * (tanh - ratio * slope), axis=0, keepdims=True)
    column = pl.multiple_of(HEADS * HEAD_DIM + step * WIDTH, WIDTH)
    vec_ref[:, pl.ds(column, WIDTH)] = clip_part
    smooth_part = jnp.sum(grad_weight * slope * weight, axis=1, keepdims=True)
    acc_ref[...] += jnp.broadcast_to(smooth_part, (CHANNELS, 128))

    @pl.when(step == D // WIDTH - 1)
    def _():
        row = acc_ref[...].T[0:1]
        first = pl.multiple_of(place_ref[0] * CHANNELS, CHANNELS)
        vec_ref[:, pl.ds(first, CHANNELS)] = row


def weight_side(place, w_proj, clip, cot, quant, part, smooth):
    return pl.pallas_call(
        weight_kernel,
        grid_spec=pltpu.PrefetchScalarGridSpec(
            num_scalar_prefetch=1,
            grid=(D // WIDTH,),
            in_specs=[
                pl.BlockSpec((CHANNELS, WIDTH), lambda j, place: (place[0], j)),
                pl.BlockSpec((1, WIDTH), lambda j, place: (0, j)),
                pl.BlockSpec((SEQ, TOKENS, WIDTH), lambda j, place: (0, 0, j)),
                pl.BlockSpec((CHANNELS, LEN), lambda j, place: (0, 0)),
                pl.BlockSpec((CHANNELS, 128), lambda j, place: (0, 0)),
                pl.BlockSpec((CHANNELS, 128), lambda j, place: (0, 0)),
            ],
            out_specs=pl.BlockSpec((1, HEADS * HEAD_DIM + D), lambda j, place: (0, 0)),
            scratch_shapes=[pltpu.VMEM((CHANNELS, 128), jnp.float32)],
        ),
        out_shape=jax.ShapeDtypeStruct((1, HEADS * HEAD_DIM + D), jnp.float32),
        compiler_params=pltpu.CompilerParams(vmem_limit_bytes=28 * MIB),
        cost_estimate=pl.CostEstimate(
            flops=2 * CHANNELS * LEN * D, bytes_accessed=9 * MIB, transcendentals=CHANNELS * D
        ),
        name="weight_side",
    )(place, w_proj, clip, cot, quant, part, smooth)


def total_over_devices(vector):
    for axis, size, bit in (
        ("seq", SEQ, 1),
        ("seq", SEQ, 2),
        ("seq", SEQ, 4),
        ("dp", DP, 1),
        ("dp", DP, 2),
        ("dp", DP, 4),
        ("dp", DP, 8),
    ):
        pairs = [(i, i ^ bit) for i in range(size)]
        vector = vector + lax.ppermute(vector, axis, pairs)
    return vector


def per_device(qkv, cotangent, w_proj, clip_levels):
    place = lax.axis_index("seq")
    place_vector = place.astype(jnp.int32).reshape(1)
    clip = clip_levels.reshape(1, D)
    cot = lax.all_gather(cotangent[0], "seq")
    send = qkv[0].reshape(3, TOKENS, SEQ, LOCAL_HEADS, HEAD_DIM).transpose(2, 3, 0, 1, 4)
    heads = lax.all_to_all(send, "seq", split_axis=0, concat_axis=0, tiled=True)
    own_rows = lax.dynamic_slice_in_dim(w_proj, place * CHANNELS, CHANNELS, axis=0)
    weight_max = jnp.max(jnp.abs(own_rows), axis=1).astype(jnp.float32)
    weights, out, message = forward(heads, weight_max.reshape(LOCAL_HEADS, 1, 128))
    messages = lax.all_to_all(
        jnp.broadcast_to(message[None], (SEQ * DP, LOCAL_HEADS, 2, 128)),
        ("seq", "dp"),
        split_axis=0,
        concat_axis=0,
        tiled=True,
    )
    grad_out, quant, part, smooth = projection(
        place_vector, messages, w_proj, clip, cot, out
    )
    back = backward(heads, weights, out, grad_out)
    back, quant = lax.optimization_barrier((back, quant))
    received = lax.all_to_all(back, "seq", split_axis=0, concat_axis=0, tiled=True)
    vector = weight_side(place_vector, w_proj, clip, cot, quant, part, smooth)
    vector = total_over_devices(vector)[0]
    grad_qkv = received.transpose(2, 3, 0, 1, 4).reshape(1, 3, TOKENS, HEADS, HEAD_DIM)
    return (grad_qkv, vector[: HEADS * HEAD_DIM], vector[HEADS * HEAD_DIM :])


def solution(mesh):
    in_specs = (P("dp", None, "seq", None, None), P("dp", "seq", None), P(), P())
    out_specs = (P("dp", None, "seq", None, None), P(), P())
    return jax.shard_map(
        per_device, mesh=mesh, in_specs=in_specs, out_specs=out_specs, check_vma=False
    )
```

time: 271 us -> 155 us (0.57)
  blocking collectives: 131 us -> 18.7 us
  matrix products: 60.1 us -> 0 us
  waiting for transfers between devices: 31.8 us -> 56.6 us
  Pallas kernels: 0 us -> 22.7 us
  between operations: 1.55 us -> 14.1 us
  other arithmetic: 13.6 us -> 1.95 us
  local copies, waits for them, and re-layouts: 15.2 us -> 23.2 us
    psum x1 -> x0, blocking collectives: 65.6 us -> none  [per_device(): d_smooth, d_clip = lax.psum((smooth_part, clip_part), ('seq', 'dp'))]
    pmax x1 -> x0, blocking collectives: 65 us -> none  [per_device(): act_max = lax.pmax(jnp.max(jnp.abs(out_float), axis=0), ('seq', 'dp'))]
    dot_general x12 -> x0, matrix products: 44.8 us -> none  [the longest x1 14.7 us: per_device(): lax.dot_general(act_quant, cot_rows, (((0,), (0,)), ((), ())), preferred_...]
    ppermute x0 -> x7, waiting for transfers between devices: none -> 24.4 us  [total_over_devices(): vector = vector + lax.ppermute(vector, axis, pairs)]
    pallas_call x0 -> x4, Pallas kernels: none -> 22.7 us  [the longest x1 7.26 us: forward(): pl.pallas_call(forward_kernel, grid=(LOCAL_HEADS,), in_specs=[pl.BlockSpe...]
    unnamed x11 -> x16, local copies, waits for them, and re-layouts: 3.06 us -> 21.9 us
    all_to_all x0 -> x1, blocking collectives: none -> 18.7 us  [per_device(): lax.all_to_all(jnp.broadcast_to(message[None], (SEQ * DP, LOCAL_HEADS, 2,...]
    sub x4 -> x0, matrix products: 15.3 us -> none  [block_weights(): exponent = jnp.exp(scores - row_top)]
  transfers between devices with their start and end apart: 4 -> 10, of which waited for: 3 -> 8; matrix products, arithmetic and copies ran while one was open for 9% -> 4% of each run, Pallas kernels for 0% -> 8%
where the time goes in v1:
time: 155 us
  waiting for transfers between devices  56.6 us (37%)
  local copies, waits for them, and re-layouts  23.2 us (15%)
  Pallas kernels  22.7 us (15%)
  blocking collectives  18.7 us (12%)
  starting transfers between devices  17.3 us (11%)
  between operations  14.1 us (9%)
  other arithmetic  1.95 us (1%)
    all_to_all x1, waiting for transfers between devices, per_device(): heads = lax.all_to_all(send, 'seq', split_axis=0, concat_axis=0, tiled=True)  31.5 us
    ppermute x7, waiting for transfers between devices, total_over_devices(): vector = vector + lax.ppermute(vector, axis, pairs)  24.4 us
    unnamed x16, local copies, waits for them, and re-layouts  21.9 us
    all_to_all x1, blocking collectives, per_device(): lax.all_to_all(jnp.broadcast_to(message[None], (SEQ * DP, LOCAL_HEADS, 2,...  18.7 us
    ppermute x7, starting transfers between devices, total_over_devices(): vector = vector + lax.ppermute(vector, axis, pairs)  8.25 us
    pallas_call x1, Pallas kernels, forward(): pl.pallas_call(forward_kernel, grid=(LOCAL_HEADS,), in_specs=[pl.BlockSpe...  7.26 us
    pallas_call x1, Pallas kernels, backward(): pl.pallas_call(backward_kernel, grid=(LOCAL_HEADS,), in_specs=[pl.BlockSp...  6.96 us
    all_to_all x1, starting transfers between devices, per_device(): heads = lax.all_to_all(send, 'seq', split_axis=0, concat_axis=0, tiled=True)  5.4 us
  transfers between devices with their start and end apart: 10, of which 8 were waited for; matrix products, arithmetic and copies ran while one was open for 4% of the time, Pallas kernels for 8%

profile of v1, /device:TPU:0, one launch (start us, length us, event | category | flops | bytes accessed | tf_op | source)
XLA Modules:
  0.0 154.5 jit_solution(12140984352697723982)
XLA Ops:
  7.2 0.0 all-gather.2.cloned.1.call-start
  7.2 0.7 all-gather.2.cloned.1.call-update
  7.9 3.0 %copy.9 = bf16[1,3,128,16,128]{4,2,1,3,0:T(8,128)(2,1)} copy(bf16[1,3,128,16,128]{4,3,2,1,0:T(8,128)(2,1)} %param.4) | data formatting | bytes 3145728 | tf_op args[0]
  10.9 5.4 %all-to-all-start = ((bf16[8,2,3,128,128]{4,3,2,1,0:T(8,128)(2,1)}), bf16[8,2,3,128,128]{4,3,2,1,0:T(8,128)(2,1)S(1)}, u32[]{:S(2)}, u32[]{:S(2)}) async-start(bf16[8,2,3,128,128]{4,3,2,1,0:T(8,128)(2,1)} %bitcast.1), calls=%async_computation | async-start | bytes 3145728 | tf_op jit(solution)/shard_map/all_to_all | solution.py:316
  16.3 1.8 %abs_reduce_fusion = bf16[256]{0:T(256)(128)(2,1)S(1)} fusion(bf16[2048,3072]{1,0:T(8,128)(2,1)} %w_ref.3, s32[]{:T(128)S(6)} %select_n.3), kind=kLoop, calls=%fused_computation | loop fusion | flops 3145472 | bytes 1573380 | tf_op jit(solution)/shard_map/reduce_max | solution.py:318
  18.0 31.5 %all-to-all-done.y_ref = bf16[8,2,3,128,128]{4,3,2,1,0:T(8,128)(2,1)S(1)} async-done(((bf16[8,2,3,128,128]{4,3,2,1,0:T(8,128)(2,1)}), bf16[8,2,3,128,128]{4,3,2,1,0:T(8,128)(2,1)S(1)}, u32[]{:S(2)}, u32[]{:S(2)}) %all-to-all-start) | async-done | bytes 1572896 | tf_op jit(solution)/shard_map/all_to_all | solution.py:316
  49.5 0.0 copy-start.6
  49.5 7.3 %attend_forward.1 = (bf16[2,1024,1024]{2,1,0:T(8,128)(2,1)S(1)}, bf16[2,128,1024]{2,1,0:T(8,128)(2,1)S(1)}, f32[2,2,128]{2,1,0:T(2,128)S(1)}) custom-call(bf16[8,2,3,128,128]{4,3,2,1,0:T(8,128)(2,1)S(1)} %all-to-all-done.y_ref, f32[2,1,128]{2,1,0:T(1,128)S(1)} %bitcast.13), custom_call_target="tpu_custom_call" | custom-call | flops 1073741824 | bytes 6291456 | tf_op jit(solution)/shard_map/attend_forward/pallas_call | solution.py:70
  56.8 0.0 copy-start.4
  56.8 2.1 %copy-done.4 = bf16[2,1024,1024]{2,1,0:T(8,128)(2,1)} copy-done((bf16[2,1024,1024]{2,1,0:T(8,128)(2,1)}, bf16[2,1024,1024]{2,1,0:T(8,128)(2,1)S(1)}, u32[]{:S(2)}) %copy-start.4) | copy-done | bytes 4194328
  58.9 0.1 broadcast_in_dim.2
  58.9 18.7 %all_to_all.15.messages_ref = f32[128,2,2,128]{3,2,1,0:T(2,128)S(1)} all-to-all(f32[128,2,2,128]{3,2,1,0:T(2,128)S(1)} %broadcast_in_dim.2), channel_id=1, replica_groups=mesh['seq'=8,'dp'=16] {'seq','dp'}, dimensions={0} | all-to-all | bytes 524288 | tf_op jit(solution)/shard_map/all_to_all | solution.py:320
  77.6 0.0 all-gather.2.cloned.1.call-done.cot_ref
  77.7 0.0 copy-done.6
  77.7 0.0 copy-start
  77.7 4.6 %copy-done = bf16[2048,3072]{1,0:T(8,128)(2,1)S(1)} copy-done((bf16[2048,3072]{1,0:T(8,128)(2,1)S(1)}, bf16[2048,3072]{1,0:T(8,128)(2,1)}, u32[]{:S(2)}) %copy-start) | copy-done | bytes 12582936
  82.2 0.0 copy-start.2
  82.2 2.8 %copy-done.2 = bf16[8,128,3072]{2,1,0:T(8,128)(2,1)S(1)} copy-done((bf16[8,128,3072]{2,1,0:T(8,128)(2,1)S(1)}, bf16[8,128,3072]{2,1,0:T(8,128)(2,1)}, u32[]{:S(2)}) %copy-start.2) | copy-done | bytes 6291480
  85.0 0.0 copy-start.5
  85.0 4.1 %projection_backward.1 = (bf16[2,128,1024]{2,1,0:T(8,128)(2,1)S(1)}, bf16[256,1024]{1,0:T(8,128)(2,1)S(1)}, f32[256,128]{1,0:T(8,128)S(1)}, f32[256,128]{1,0:T(8,128)S(1)}) custom-call(s32[1]{0:T(128)} %bitcast.3.place_ref, f32[128,2,2,128]{3,2,1,0:T(2,128)S(1)} %all_to_all.15.messages_ref, bf16[2048,3072]{1,0:T(8,128)(2,1)S(1)} %copy-done, ...), custom_call_target="tpu_custom_call" | custom-call | flops 1610612736 | bytes 9437184 | tf_op jit(solution)/shard_map/projection_backward/pallas_call | solution.py:151
  89.2 0.0 copy-done.5
  89.2 7.0 %attend_backward.1 = bf16[8,2,3,128,128]{4,3,2,1,0:T(8,128)(2,1)} custom-call(bf16[8,2,3,128,128]{4,3,2,1,0:T(8,128)(2,1)S(1)} %all-to-all-done.y_ref, bf16[2,1024,1024]{2,1,0:T(8,128)(2,1)S(1)} %copy-done.5, bf16[2,128,1024]{2,1,0:T(8,128)(2,1)S(1)} %get-tuple-element.13.out_ref, bf16[2,128,1024]{2,1,0:T(8,128)(2,1)S(1)} %get-tuple-element.15.grad_ref), custom_call_target="tpu_custom_call" | custom-call | flops 2147483648 | bytes 8388608 | tf_op jit(solution)/shard_map/attend_backward/pallas_call | solution.py:215
  96.1 3.6 %all-to-all-start.2 = ((bf16[8,2,3,128,128]{4,3,2,1,0:T(8,128)(2,1)}), bf16[8,2,3,128,128]{4,3,2,1,0:T(8,128)(2,1)S(1)}, u32[]{:S(2)}, u32[]{:S(2)}) async-start(bf16[8,2,3,128,128]{4,3,2,1,0:T(8,128)(2,1)} %attend_backward.1), calls=%async_computation.2 | async-start | bytes 3145728 | tf_op jit(solution)/shard_map/all_to_all | solution.py:332
  99.7 0.0 copy-start.1
  99.7 4.6 %copy-done.1 = bf16[2048,3072]{1,0:T(8,128)(2,1)S(1)} copy-done((bf16[2048,3072]{1,0:T(8,128)(2,1)S(1)}, bf16[2048,3072]{1,0:T(8,128)(2,1)}, u32[]{:S(2)}) %copy-start.1) | copy-done | bytes 12582936
  104.3 0.0 copy-start.3
  104.3 2.8 %copy-done.3 = bf16[8,128,3072]{2,1,0:T(8,128)(2,1)S(1)} copy-done((bf16[8,128,3072]{2,1,0:T(8,128)(2,1)S(1)}, bf16[8,128,3072]{2,1,0:T(8,128)(2,1)}, u32[]{:S(2)}) %copy-start.3) | copy-done | bytes 6291480
  107.1 4.4 %weight_side.1 = f32[1,5120]{1,0:T(1,128)S(1)} custom-call(s32[1]{0:T(128)} %bitcast.3.place_ref, bf16[2048,3072]{1,0:T(8,128)(2,1)S(1)} %copy-done.1, f32[1,3072]{1,0:T(1,128)S(1)} %bitcast.12, bf16[8,128,3072]{2,1,0:T(8,128)(2,1)S(1)} %copy-done.3, bf16[256,1024]{1,0:T(8,128)(2,1)S(1)} %get-tuple-element.18.quant_ref, ...), custom_call_target="tpu_custom_call" | custom-call | flops 1610612736 | bytes 9437184 | tf_op jit(solution)/shard_map/weight_side/pallas_call | solution.py:270
  111.5 0.5 collective-permute-start
  112.0 0.8 collective-permute-done
  112.8 1.9 %collective-permute-start.1 = (f32[1,5120]{1,0:T(1,128)S(1)}, f32[1,5120]{1,0:T(1,128)S(1)}, u32[]{:S(2)}, u32[]{:S(2)}) collective-permute-start(f32[1,5120]{1,0:T(1,128)S(1)} %add.25), channel_id=1, source_target_pairs={{0,32},{16,48},{32,0},{48,16},{64,96},{80,112},{96,64},{112,80},{1... | collective-permute-start | bytes 61448 | tf_op jit(solution)/shard_map/ppermute | solution.py:306
  114.8 5.4 %collective-permute-done.1 = f32[1,5120]{1,0:T(1,128)S(1)} collective-permute-done((f32[1,5120]{1,0:T(1,128)S(1)}, f32[1,5120]{1,0:T(1,128)S(1)}, u32[]{:S(2)}, u32[]{:S(2)}) %collective-permute-start.1) | collective-permute-done | bytes 20512 | tf_op jit(solution)/shard_map/ppermute | solution.py:306
  120.2 2.8 %collective-permute-start.2 = (f32[1,5120]{1,0:T(1,128)S(1)}, f32[1,5120]{1,0:T(1,128)S(1)}, u32[]{:S(2)}, u32[]{:S(2)}) collective-permute-start(f32[1,5120]{1,0:T(1,128)S(1)} %add.26), channel_id=1, source_target_pairs={{0,64},{16,80},{32,96},{48,112},{64,0},{80,16},{96,32},{112,48},{1... | collective-permute-start | bytes 61448 | tf_op jit(solution)/shard_map/ppermute | solution.py:306
  123.0 2.6 %collective-permute-done.2 = f32[1,5120]{1,0:T(1,128)S(1)} collective-permute-done((f32[1,5120]{1,0:T(1,128)S(1)}, f32[1,5120]{1,0:T(1,128)S(1)}, u32[]{:S(2)}, u32[]{:S(2)}) %collective-permute-start.2) | collective-permute-done | bytes 20512 | tf_op jit(solution)/shard_map/ppermute | solution.py:306
  125.6 0.7 collective-permute-start.3
  126.3 3.4 %collective-permute-done.3 = f32[1,5120]{1,0:T(1,128)S(1)} collective-permute-done((f32[1,5120]{1,0:T(1,128)S(1)}, f32[1,5120]{1,0:T(1,128)S(1)}, u32[]{:S(2)}, u32[]{:S(2)}) %collective-permute-start.3) | collective-permute-done | bytes 20512 | tf_op jit(solution)/shard_map/ppermute | solution.py:306
  129.6 0.6 collective-permute-start.4
  130.2 4.8 %collective-permute-done.4 = f32[1,5120]{1,0:T(1,128)S(1)} collective-permute-done((f32[1,5120]{1,0:T(1,128)S(1)}, f32[1,5120]{1,0:T(1,128)S(1)}, u32[]{:S(2)}, u32[]{:S(2)}) %collective-permute-start.4) | collective-permute-done | bytes 20512 | tf_op jit(solution)/shard_map/ppermute | solution.py:306
  135.0 0.7 collective-permute-start.5
  135.7 3.2 %collective-permute-done.5 = f32[1,5120]{1,0:T(1,128)S(1)} collective-permute-done((f32[1,5120]{1,0:T(1,128)S(1)}, f32[1,5120]{1,0:T(1,128)S(1)}, u32[]{:S(2)}, u32[]{:S(2)}) %collective-permute-start.5) | collective-permute-done | bytes 20512 | tf_op jit(solution)/shard_map/ppermute | solution.py:306
  138.9 1.1 collective-permute-start.6
  140.0 4.3 %collective-permute-done.6 = f32[1,5120]{1,0:T(1,128)S(1)} collective-permute-done((f32[1,5120]{1,0:T(1,128)S(1)}, f32[1,5120]{1,0:T(1,128)S(1)}, u32[]{:S(2)}, u32[]{:S(2)}) %collective-permute-start.6) | collective-permute-done | bytes 20512 | tf_op jit(solution)/shard_map/ppermute | solution.py:306
  144.3 0.6 slice.16
  144.9 0.6 slice.17
  145.5 0.0 all-to-all-done.2
  145.5 2.2 %copy.10 = bf16[1,3,128,16,128]{4,3,2,1,0:T(8,128)(2,1)} copy(bf16[1,3,128,16,128]{4,2,1,3,0:T(8,128)(2,1)S(1)} %bitcast.14) | data formatting | bytes 3145728
  (8 shorter events, 0.2 us)
Async XLA Ops:
  7.2 70.5 %all-gather.2.cloned.1.call-start = ((), (), s32[]{:S(2)}) async-start(), calls=%async_computation.3 | async-start | bytes 7077888 | tf_op jit(solution)/shard_map/all_gather | solution.py:314
  10.9 38.7 %all-to-all-start = ((bf16[8,2,3,128,128]{4,3,2,1,0:T(8,128)(2,1)}), bf16[8,2,3,128,128]{4,3,2,1,0:T(8,128)(2,1)S(1)}, u32[]{:S(2)}, u32[]{:S(2)}) async-start(bf16[8,2,3,128,128]{4,3,2,1,0:T(8,128)(2,1)} %bitcast.1), calls=%async_computation | async-start | bytes 3145728 | tf_op jit(solution)/shard_map/all_to_all | solution.py:316
  49.5 28.1 %copy-start.6 = (f32[3072]{0:T(1024)S(1)}, f32[3072]{0:T(1024)}, u32[]{:S(2)}) copy-start(f32[3072]{0:T(1024)} %param.7) | copy-start | bytes 36868
  56.8 2.1 %copy-start.4 = (bf16[2,1024,1024]{2,1,0:T(8,128)(2,1)}, bf16[2,1024,1024]{2,1,0:T(8,128)(2,1)S(1)}, u32[]{:S(2)}) copy-start(bf16[2,1024,1024]{2,1,0:T(8,128)(2,1)S(1)} %get-tuple-element.12.p_ref) | copy-start | bytes 12582916
  77.7 4.6 %copy-start = (bf16[2048,3072]{1,0:T(8,128)(2,1)S(1)}, bf16[2048,3072]{1,0:T(8,128)(2,1)}, u32[]{:S(2)}) copy-start(bf16[2048,3072]{1,0:T(8,128)(2,1)} %w_ref.3) | copy-start | bytes 37748740
  82.2 2.8 %copy-start.2 = (bf16[8,128,3072]{2,1,0:T(8,128)(2,1)S(1)}, bf16[8,128,3072]{2,1,0:T(8,128)(2,1)}, u32[]{:S(2)}) copy-start(bf16[8,128,3072]{2,1,0:T(8,128)(2,1)} %all-gather.2.cloned.1.call-done.cot_ref) | copy-start | bytes 18874372
  85.0 4.2 %copy-start.5 = (bf16[2,1024,1024]{2,1,0:T(8,128)(2,1)S(1)}, bf16[2,1024,1024]{2,1,0:T(8,128)(2,1)}, u32[]{:S(2)}) copy-start(bf16[2,1024,1024]{2,1,0:T(8,128)(2,1)} %copy-done.4) | copy-start | bytes 12582916
  96.1 49.4 %all-to-all-start.2 = ((bf16[8,2,3,128,128]{4,3,2,1,0:T(8,128)(2,1)}), bf16[8,2,3,128,128]{4,3,2,1,0:T(8,128)(2,1)S(1)}, u32[]{:S(2)}, u32[]{:S(2)}) async-start(bf16[8,2,3,128,128]{4,3,2,1,0:T(8,128)(2,1)} %attend_backward.1), calls=%async_computation.2 | async-start | bytes 3145728 | tf_op jit(solution)/shard_map/all_to_all | solution.py:332
  99.7 4.6 %copy-start.1 = (bf16[2048,3072]{1,0:T(8,128)(2,1)S(1)}, bf16[2048,3072]{1,0:T(8,128)(2,1)}, u32[]{:S(2)}) copy-start(bf16[2048,3072]{1,0:T(8,128)(2,1)} %w_ref.3) | copy-start | bytes 37748740
  104.3 2.8 %copy-start.3 = (bf16[8,128,3072]{2,1,0:T(8,128)(2,1)S(1)}, bf16[8,128,3072]{2,1,0:T(8,128)(2,1)}, u32[]{:S(2)}) copy-start(bf16[8,128,3072]{2,1,0:T(8,128)(2,1)} %all-gather.2.cloned.1.call-done.cot_ref) | copy-start | bytes 18874372
  111.5 1.3 collective-permute-start
  112.8 7.3 %collective-permute-start.1 = (f32[1,5120]{1,0:T(1,128)S(1)}, f32[1,5120]{1,0:T(1,128)S(1)}, u32[]{:S(2)}, u32[]{:S(2)}) collective-permute-start(f32[1,5120]{1,0:T(1,128)S(1)} %add.25), channel_id=1, source_target_pairs={{0,32},{16,48},{32,0},{48,16},{64,96},{80,112},{96,64},{112,80},{1... | collective-permute-start | bytes 61448 | tf_op jit(solution)/shard_map/ppermute | solution.py:306
  120.2 5.4 %collective-permute-start.2 = (f32[1,5120]{1,0:T(1,128)S(1)}, f32[1,5120]{1,0:T(1,128)S(1)}, u32[]{:S(2)}, u32[]{:S(2)}) collective-permute-start(f32[1,5120]{1,0:T(1,128)S(1)} %add.26), channel_id=1, source_target_pairs={{0,64},{16,80},{32,96},{48,112},{64,0},{80,16},{96,32},{112,48},{1... | collective-permute-start | bytes 61448 | tf_op jit(solution)/shard_map/ppermute | solution.py:306
  125.6 4.0 %collective-permute-start.3 = (f32[1,5120]{1,0:T(1,128)S(1)}, f32[1,5120]{1,0:T(1,128)S(1)}, u32[]{:S(2)}, u32[]{:S(2)}) collective-permute-start(f32[1,5120]{1,0:T(1,128)S(1)} %add.27), channel_id=1, source_target_pairs={{0,1},{1,0},{2,3},{3,2},{4,5},{5,4},{6,7},{7,6},{8,9},{9,8},{10,11... | collective-permute-start | bytes 61448 | tf_op jit(solution)/shard_map/ppermute | solution.py:306
  129.6 5.4 %collective-permute-start.4 = (f32[1,5120]{1,0:T(1,128)S(1)}, f32[1,5120]{1,0:T(1,128)S(1)}, u32[]{:S(2)}, u32[]{:S(2)}) collective-permute-start(f32[1,5120]{1,0:T(1,128)S(1)} %add.28), channel_id=1, source_target_pairs={{0,2},{1,3},{2,0},{3,1},{4,6},{5,7},{6,4},{7,5},{8,10},{9,11},{10,... | collective-permute-start | bytes 61448 | tf_op jit(solution)/shard_map/ppermute | solution.py:306
  135.0 3.9 %collective-permute-start.5 = (f32[1,5120]{1,0:T(1,128)S(1)}, f32[1,5120]{1,0:T(1,128)S(1)}, u32[]{:S(2)}, u32[]{:S(2)}) collective-permute-start(f32[1,5120]{1,0:T(1,128)S(1)} %add.29), channel_id=1, source_target_pairs={{0,4},{1,5},{2,6},{3,7},{4,0},{5,1},{6,2},{7,3},{8,12},{9,13},{10,... | collective-permute-start | bytes 61448 | tf_op jit(solution)/shard_map/ppermute | solution.py:306
  138.9 5.4 %collective-permute-start.6 = (f32[1,5120]{1,0:T(1,128)S(1)}, f32[1,5120]{1,0:T(1,128)S(1)}, u32[]{:S(2)}, u32[]{:S(2)}) collective-permute-start(f32[1,5120]{1,0:T(1,128)S(1)} %add.30), channel_id=1, source_target_pairs={{0,8},{1,9},{2,10},{3,11},{4,12},{5,13},{6,14},{7,15},{8,0},{9,1},... | collective-permute-start | bytes 61448 | tf_op jit(solution)/shard_map/ppermute | solution.py:306
Sparse Core Ops, SparseCore 0:
  9.7 54.8 all-gather.1

commit v2 on v1

v2 whole, which is shorter than its diff:
```python
import math

import jax
import jax.numpy as jnp
from jax import lax
from jax.experimental import pallas as pl
from jax.experimental.pallas import tpu as pltpu
from jax.sharding import PartitionSpec as P

HEADS = 16
HEAD_DIM = 128
SEQ = 8
DP = 16
LOCAL_HEADS = 2
CHANNELS = LOCAL_HEADS * HEAD_DIM
TOKENS = 128
LEN = 1024
D = 3072
BLOCK = 256
NUM_BLOCKS = LEN // BLOCK
epsilon = 1e-05
act_fraction = 0.5
SCALE = HEAD_DIM ** (-0.5)
EXP2_SCALE = SCALE * math.log2(math.e)

NN = (((1,), (0,)), ((), ()))
NT = (((1,), (1,)), ((), ()))
TN = (((0,), (0,)), ((), ()))
MIB = 1 << 20
VMEM_LIMIT = 24 * MIB


def dot(lhs, rhs, dims):
    return lax.dot_general(lhs, rhs, dims, preferred_element_type=jnp.float32)


def to_row(column):
    return jnp.broadcast_to(column, (column.shape[0], 128)).T[0:1]


def to_column(row):
    return jnp.broadcast_to(row, (128, row.shape[1])).T[:, 0:1]


def forward_kernel(y_ref, weight_max_ref, p_ref, out_ref, message_ref):
    keys = y_ref[:, 0, 1].reshape(LEN, HEAD_DIM)
    values = y_ref[:, 0, 2].reshape(LEN, HEAD_DIM)
    top = None
    for b in range(NUM_BLOCKS):
        queries = y_ref[2 * b : 2 * b + 2, 0, 0].reshape(BLOCK, HEAD_DIM)
        scores = dot(keys, queries, NT)
        row_top = jnp.max(scores, axis=0, keepdims=True)
        exponent = jnp.exp2((scores - row_top) * EXP2_SCALE)
        total = jnp.sum(exponent, axis=0, keepdims=True)
        weights = (exponent * (1.0 / total)).astype(jnp.bfloat16)
        columns = pl.ds(b * BLOCK, BLOCK)
        p_ref[0, :, columns] = weights
        mixed = dot(values, weights, TN).astype(jnp.bfloat16)
        out_ref[0, :, columns] = mixed
        block_top = jnp.max(jnp.abs(mixed.astype(jnp.float32)), axis=1, keepdims=True)
        top = block_top if top is None else jnp.maximum(top, block_top)
    act_row = to_row(top)
    bound = jnp.max(
        jnp.sqrt((act_row + epsilon) * (weight_max_ref[0] + epsilon)), axis=1, keepdims=True
    )
    message_ref[0, 0:1] = act_row
    message_ref[0, 1:2] = jnp.broadcast_to(bound, (1, 128))


def forward(heads, weight_max):
    return pl.pallas_call(
        forward_kernel,
        grid=(LOCAL_HEADS,),
        in_specs=[
            pl.BlockSpec((SEQ, 1, 3, TOKENS, HEAD_DIM), lambda h: (0, h, 0, 0, 0)),
            pl.BlockSpec((1, 1, 128), lambda h: (h, 0, 0)),
        ],
        out_specs=[
            pl.BlockSpec((1, LEN, LEN), lambda h: (h, 0, 0)),
            pl.BlockSpec((1, HEAD_DIM, LEN), lambda h: (h, 0, 0)),
            pl.BlockSpec((1, 2, 128), lambda h: (h, 0, 0)),
        ],
        out_shape=[
            jax.ShapeDtypeStruct((LOCAL_HEADS, LEN, LEN), jnp.bfloat16),
            jax.ShapeDtypeStruct((LOCAL_HEADS, HEAD_DIM, LEN), jnp.bfloat16),
            jax.ShapeDtypeStruct((LOCAL_HEADS, 2, 128), jnp.float32),
        ],
        compiler_params=pltpu.CompilerParams(vmem_limit_bytes=VMEM_LIMIT),
        cost_estimate=pl.CostEstimate(
            flops=2 * 2 * LOCAL_HEADS * LEN * LEN * HEAD_DIM,
            bytes_accessed=6 * MIB,
            transcendentals=LOCAL_HEADS * LEN * LEN,
        ),
        name="attend_forward",
    )(heads, weight_max)


HALF = TOKENS // 2
WIDTH = 512


def projection_kernel(place_ref, messages_ref, clip_ref, out_ref, own_ref, *rest):
    pieces = rest[:10]
    grad_ref, vec_ref, cot_ref, wq_ref, tanh_ref, quant_ref, sem = rest[10:]
    place = place_ref[0]
    depth = place // 2
    core = place % 2
    copies = []
    for k, piece in enumerate(pieces):
        kind, sibling = k % 5, k // 5
        rows = TOKENS if kind < 3 else HALF
        source = (depth + (0, 3, 1, 2, 2)[kind]) % 4
        first = (source * 2 + (core + sibling) % 2) * TOKENS + (HALF if kind == 4 else 0)
        copy = pltpu.make_async_copy(
            piece, cot_ref.at[pl.ds(pl.multiple_of(first, HALF), rows)], sem.at[k]
        )
        copy.start()
        copies.append(copy)
    bound = jnp.max(messages_ref[:, :, 1, :], axis=0)
    bound = jnp.max(jnp.max(bound, axis=0, keepdims=True), axis=1, keepdims=True)
    act_clip = act_fraction * bound
    mine = messages_ref[pl.ds(pl.multiple_of(place * DP, DP), DP)]
    act_max = jnp.max(mine[:, :, 0, :], axis=0)
    act_column = jnp.concatenate([to_column(act_max[0:1]), to_column(act_max[1:2])], axis=0)
    weight_max = None
    for j in range(D // WIDTH):
        weight = own_ref[:, j * WIDTH : (j + 1) * WIDTH]
        top = jnp.max(jnp.abs(weight.astype(jnp.float32)), axis=1, keepdims=True)
        weight_max = top if weight_max is None else jnp.maximum(weight_max, top)
    smooth = jnp.sqrt((act_column + epsilon) / (weight_max + epsilon))
    for j in range(D // WIDTH):
        columns = slice(j * WIDTH, (j + 1) * WIDTH)
        clip = clip_ref[:, columns]
        weight = own_ref[:, columns].astype(jnp.float32)
        tanh = jnp.tanh((smooth * weight) * (1.0 / clip))
        tanh_ref[:, columns] = tanh
        wq_ref[:, columns] = (clip * tanh).astype(jnp.bfloat16)
    inverse = 1.0 / smooth
    inner = inverse / act_clip
    for copy in copies:
        copy.wait()
    act_part = None
    for t in range(NUM_BLOCKS):
        tokens = slice(t * BLOCK, (t + 1) * BLOCK)
        grad_act = dot(wq_ref[...], cot_ref[tokens], NT)
        out = out_ref[:, :, tokens].reshape(CHANNELS, BLOCK).astype(jnp.float32)
        tanh = jnp.tanh(out * inner)
        quant_ref[:, tokens] = (act_clip * tanh).astype(jnp.bfloat16)
        smoothed = grad_act * (1.0 - tanh * tanh)
        part = jnp.sum(smoothed * out, axis=1, keepdims=True)
        act_part = part if act_part is None else act_part + part
        grad_ref[:, :, tokens] = (
            (smoothed * inverse).astype(jnp.bfloat16).reshape(LOCAL_HEADS, HEAD_DIM, BLOCK)
        )
    smooth_part = -act_part * (inverse * inverse)
    vec_ref[...] = jnp.zeros_like(vec_ref)
    for j in range(D // WIDTH):
        columns = slice(j * WIDTH, (j + 1) * WIDTH)
        weight = own_ref[:, columns].astype(jnp.float32)
        grad_weight = dot(quant_ref[...], cot_ref[:, columns], NN)
        ratio = (smooth * weight) * (1.0 / clip_ref[:, columns])
        tanh = tanh_ref[:, columns]
        slope = 1.0 - tanh * tanh
        vec_ref[:, HEADS * HEAD_DIM + j * WIDTH : HEADS * HEAD_DIM + (j + 1) * WIDTH] = jnp.sum(
            grad_weight * (tanh - ratio * slope), axis=0, keepdims=True
        )
        smooth_part += jnp.sum(grad_weight * slope * weight, axis=1, keepdims=True)
    vec_ref[:, pl.ds(pl.multiple_of(place * CHANNELS, CHANNELS), CHANNELS)] = to_row(smooth_part)


def projection(place, messages, clip, out, own_rows, pieces):
    vmem = pl.BlockSpec(memory_space=pltpu.VMEM)
    hbm = pl.BlockSpec(memory_space=pl.ANY)
    return pl.pallas_call(
        projection_kernel,
        in_specs=[pl.BlockSpec(memory_space=pltpu.SMEM), vmem, vmem, vmem, vmem] + [hbm] * 10,
        out_specs=[vmem, vmem],
        out_shape=[
            jax.ShapeDtypeStruct((LOCAL_HEADS, HEAD_DIM, LEN), jnp.bfloat16),
            jax.ShapeDtypeStruct((1, HEADS * HEAD_DIM + D), jnp.float32),
        ],
        scratch_shapes=[
            pltpu.VMEM((LEN, D), jnp.bfloat16),
            pltpu.VMEM((CHANNELS, D), jnp.bfloat16),
            pltpu.VMEM((CHANNELS, D), jnp.float32),
            pltpu.VMEM((CHANNELS, LEN), jnp.bfloat16),
            pltpu.SemaphoreType.DMA((10,)),
        ],
        compiler_params=pltpu.CompilerParams(vmem_limit_bytes=VMEM_LIMIT),
        cost_estimate=pl.CostEstimate(
            flops=2 * 2 * CHANNELS * LEN * D,
            bytes_accessed=9 * MIB,
            transcendentals=CHANNELS * (D + LEN),
        ),
        name="projection_backward",
    )(place, messages, clip, out, own_rows, *pieces)


def backward_kernel(y_ref, p_ref, out_ref, grad_ref, z_ref, ds_ref):
    keys = y_ref[:, 0, 1].reshape(LEN, HEAD_DIM)
    values = y_ref[:, 0, 2].reshape(LEN, HEAD_DIM)
    for b in range(NUM_BLOCKS):
        columns = pl.ds(b * BLOCK, BLOCK)
        grad_out = grad_ref[0, :, columns]
        delta = jnp.sum(
            grad_out.astype(jnp.float32) * out_ref[0, :, columns].astype(jnp.float32),
            axis=0,
            keepdims=True,
        )
        grad_weights = dot(values, grad_out, NN)
        weights = p_ref[0, :, columns].astype(jnp.float32)
        grad_scores = (weights * (grad_weights - delta)).astype(jnp.bfloat16)
        ds_ref[:, columns] = grad_scores
        grad_query = dot(keys, grad_scores, TN) * SCALE
        z_ref[2 * b : 2 * b + 2, 0, 0] = (
            grad_query.T.astype(jnp.bfloat16).reshape(2, TOKENS, HEAD_DIM)
        )
    queries = y_ref[:, 0, 0].reshape(LEN, HEAD_DIM)
    grad_value = dot(p_ref[0], grad_ref[0], NT)
    z_ref[:, 0, 2] = grad_value.astype(jnp.bfloat16).reshape(SEQ, TOKENS, HEAD_DIM)
    grad_key = dot(ds_ref[...], queries, NN) * SCALE
    z_ref[:, 0, 1] = grad_key.astype(jnp.bfloat16).reshape(SEQ, TOKENS, HEAD_DIM)


def backward(heads, weights, out, grad_out):
    return pl.pallas_call(
        backward_kernel,
        grid=(LOCAL_HEADS,),
        in_specs=[
            pl.BlockSpec((SEQ, 1, 3, TOKENS, HEAD_DIM), lambda h: (0, h, 0, 0, 0)),
            pl.BlockSpec((1, LEN, LEN), lambda h: (h, 0, 0)),
            pl.BlockSpec((1, HEAD_DIM, LEN), lambda h: (h, 0, 0)),
            pl.BlockSpec((1, HEAD_DIM, LEN), lambda h: (h, 0, 0)),
        ],
        out_specs=pl.BlockSpec((SEQ, 1, 3, TOKENS, HEAD_DIM), lambda h: (0, h, 0, 0, 0)),
        out_shape=jax.ShapeDtypeStruct(
            (SEQ, LOCAL_HEADS, 3, TOKENS, HEAD_DIM), jnp.bfloat16
        ),
        scratch_shapes=[pltpu.VMEM((LEN, LEN), jnp.bfloat16)],
        compiler_params=pltpu.CompilerParams(vmem_limit_bytes=VMEM_LIMIT),
        cost_estimate=pl.CostEstimate(
            flops=4 * 2 * LOCAL_HEADS * LEN * LEN * HEAD_DIM,
            bytes_accessed=8 * MIB,
            transcendentals=0,
        ),
        name="attend_backward",
    )(heads, weights, out, grad_out)


def total_over_depth(vector):
    moved = [
        lax.ppermute(vector, "seq", [(i, i ^ bits) for i in range(SEQ)]) for bits in (2, 4, 6)
    ]
    return (vector + moved[0]) + (moved[1] + moved[2])


def total_over_rest(vector):
    for axis, size, bit in (
        ("dp", DP, 1),
        ("dp", DP, 2),
        ("dp", DP, 4),
        ("dp", DP, 8),
        ("seq", SEQ, 1),
    ):
        vector = vector + lax.ppermute(vector, axis, [(i, i ^ bit) for i in range(size)])
    return vector


def shift_depth(tensor, steps):
    return lax.ppermute(tensor, "seq", [(i, (i + 2 * steps) % SEQ) for i in range(SEQ)])


def swap_cores(tensor):
    return lax.ppermute(tensor, "seq", [(i, i ^ 1) for i in range(SEQ)])


def after(tensors, *earlier):
    return lax.optimization_barrier((tensors, earlier))[0]


def per_device(qkv, cotangent, w_proj, clip_levels):
    place = lax.axis_index("seq")
    place_vector = place.astype(jnp.int32).reshape(1)
    clip = clip_levels.reshape(1, D)
    own = cotangent[0]
    own_rows = lax.optimization_barrier(
        lax.dynamic_slice_in_dim(w_proj, place * CHANNELS, CHANNELS, axis=0)
    )
    send = qkv[0].reshape(3, TOKENS, SEQ, LOCAL_HEADS, HEAD_DIM).transpose(2, 3, 0, 1, 4)
    heads = lax.all_to_all(send, "seq", split_axis=0, concat_axis=0, tiled=True)
    weight_max = jnp.max(jnp.abs(own_rows), axis=1).astype(jnp.float32)
    weight_max = weight_max.reshape(LOCAL_HEADS, 1, 128)
    own_swapped = swap_cores(own)
    own_1, weight_max = after((own, weight_max), heads)
    before = shift_depth(own_1, 1)
    behind = shift_depth(own_1, -1)
    weights, out, message = forward(heads, weight_max)
    messages = lax.all_to_all(
        jnp.broadcast_to(message[None], (SEQ * DP, LOCAL_HEADS, 2, 128)),
        ("seq", "dp"),
        split_axis=0,
        concat_axis=0,
        tiled=True,
    )
    before, behind = after((before, behind), message)
    far_low = shift_depth(before[:HALF], 1)
    far_high = shift_depth(behind[HALF:], -1)
    pieces = [own, before, behind, far_low, far_high, own_swapped]
    pieces += [swap_cores(piece) for piece in (before, behind)]
    pieces += [swap_cores(piece) for piece in after((far_low, far_high), messages)]
    grad_out, vector = projection(place_vector, messages, clip, out, own_rows, pieces)
    back = backward(heads, weights, out, grad_out)
    back, vector = lax.optimization_barrier((back, total_over_depth(vector)))
    received = lax.all_to_all(back, "seq", split_axis=0, concat_axis=0, tiled=True)
    vector = total_over_rest(vector)[0]
    grad_qkv = received.transpose(2, 3, 0, 1, 4).reshape(1, 3, TOKENS, HEADS, HEAD_DIM)
    return (grad_qkv, vector[: HEADS * HEAD_DIM], vector[HEADS * HEAD_DIM :])


def solution(mesh):
    in_specs = (P("dp", None, "seq", None, None), P("dp", "seq", None), P(), P())
    out_specs = (P("dp", None, "seq", None, None), P(), P())
    return jax.shard_map(
        per_device, mesh=mesh, in_specs=in_specs, out_specs=out_specs, check_vma=False
    )
```

time: 155 us -> 123 us (0.79)
  local copies, waits for them, and re-layouts: 23.2 us -> 7.96 us
  between operations: 14.1 us -> 0.73 us
  waiting for transfers between devices: 56.6 us -> 50.6 us
  starting transfers between devices: 17.3 us -> 21.4 us
  Pallas kernels: 22.7 us -> 21 us
    unnamed x16 -> x6, local copies, waits for them, and re-layouts: 21.9 us -> 5.12 us
    all_to_all x1, waiting for transfers between devices: 31.5 us -> 19.7 us  [per_device(): heads = lax.all_to_all(send, 'seq', split_axis=0, concat_axis=0, tiled=True)]
    ppermute x7 -> x17, waiting for transfers between devices: 24.4 us -> 30.7 us  [the longest x5 16.8 us: total_over_rest(): lax.ppermute(vector, axis, [(i, i ^ bit) for i in range(size)])]
    ppermute x7 -> x17, starting transfers between devices: 8.25 us -> 12.4 us  [the longest x3 4.17 us: total_over_depth(): lax.ppermute(vector, 'seq', [(i, i ^ bits) for i in range(SEQ)])]
    pallas_call x2 -> x1, Pallas kernels: 8.52 us -> 6.81 us  [projection(): pl.pallas_call(projection_kernel, in_specs=[pl.BlockSpec(memory_space=plt...]
  transfers between devices with their start and end apart: 10 -> 19, of which waited for: 8 -> 11; matrix products, arithmetic and copies ran while one was open for 4% -> 3% of each run, Pallas kernels for 8% -> 12%
where the time goes in v2:
time: 123 us; the launch traced here: 122 us
  waiting for transfers between devices  50.6 us (41%)
  starting transfers between devices  21.4 us (17%)
  Pallas kernels  21 us (17%)
  blocking collectives  19.3 us (16%)
  local copies, waits for them, and re-layouts  7.96 us (6%)
    all_to_all x1, waiting for transfers between devices, per_device(): heads = lax.all_to_all(send, 'seq', split_axis=0, concat_axis=0, tiled=True)  19.7 us
    all_to_all x1, blocking collectives, per_device(): lax.all_to_all(jnp.broadcast_to(message[None], (SEQ * DP, LOCAL_HEADS, 2,...  19.3 us
    ppermute x5, waiting for transfers between devices, total_over_rest(): lax.ppermute(vector, axis, [(i, i ^ bit) for i in range(size)])  16.8 us
    ppermute x4, waiting for transfers between devices, shift_depth(): lax.ppermute(tensor, 'seq', [(i, (i + 2 * steps) % SEQ) for i in range(SE...  12.1 us
    pallas_call x1, Pallas kernels, forward(): pl.pallas_call(forward_kernel, grid=(LOCAL_HEADS,), in_specs=[pl.BlockSpe...  7.26 us
    pallas_call x1, Pallas kernels, backward(): pl.pallas_call(backward_kernel, grid=(LOCAL_HEADS,), in_specs=[pl.BlockSp...  6.95 us
    pallas_call x1, Pallas kernels, projection(): pl.pallas_call(projection_kernel, in_specs=[pl.BlockSpec(memory_space=plt...  6.81 us
    all_to_all x1, starting transfers between devices, per_device(): heads = lax.all_to_all(send, 'seq', split_axis=0, concat_axis=0, tiled=True)  5.4 us
  transfers between devices with their start and end apart: 19, of which 11 were waited for; matrix products, arithmetic and copies ran while one was open for 3% of the time, Pallas kernels for 12%

profile of v2, /device:TPU:0, one launch (start us, length us, event | category | flops | bytes accessed | tf_op | source)
XLA Modules:
  0.0 121.6 jit_solution(7784256101171306531)
XLA Ops:
  0.6 3.0 %copy.7 = bf16[1,3,128,16,128]{4,2,1,3,0:T(8,128)(2,1)} copy(bf16[1,3,128,16,128]{4,3,2,1,0:T(8,128)(2,1)} %param.4) | data formatting | bytes 3145728 | tf_op args[0]
  3.6 5.4 %all-to-all-start = ((bf16[8,2,3,128,128]{4,3,2,1,0:T(8,128)(2,1)}), bf16[8,2,3,128,128]{4,3,2,1,0:T(8,128)(2,1)S(1)}, u32[]{:S(2)}, u32[]{:S(2)}) async-start(bf16[8,2,3,128,128]{4,3,2,1,0:T(8,128)(2,1)} %bitcast.1), calls=%async_computation | async-start | bytes 3145728 | tf_op jit(solution)/shard_map/all_to_all | solution.py:290
  9.0 1.5 %constant_dynamic-slice_fusion.own_ref = bf16[256,3072]{1,0:T(8,128)(2,1)S(1)} fusion(bf16[2048,3072]{1,0:T(8,128)(2,1)} %param.6, s32[]{:T(128)S(6)} %select_n.3), kind=kLoop, calls=%fused_computation.2 | loop fusion | bytes 3145732 | tf_op jit(solution)/shard_map/dynamic_slice | solution.py:287
  10.5 0.4 abs_reduce_fusion
  10.9 19.7 %all-to-all-done.y_ref = bf16[8,2,3,128,128]{4,3,2,1,0:T(8,128)(2,1)S(1)} async-done(((bf16[8,2,3,128,128]{4,3,2,1,0:T(8,128)(2,1)}), bf16[8,2,3,128,128]{4,3,2,1,0:T(8,128)(2,1)S(1)}, u32[]{:S(2)}, u32[]{:S(2)}) %all-to-all-start) | async-done | bytes 1572896 | tf_op jit(solution)/shard_map/all_to_all | solution.py:290
  30.6 1.2 collective-permute-start.1
  31.7 0.9 collective-permute-start
  32.6 7.3 %attend_forward.1 = (bf16[2,1024,1024]{2,1,0:T(8,128)(2,1)S(1)}, bf16[2,128,1024]{2,1,0:T(8,128)(2,1)S(1)}, f32[2,2,128]{2,1,0:T(2,128)S(1)}) custom-call(bf16[8,2,3,128,128]{4,3,2,1,0:T(8,128)(2,1)S(1)} %all-to-all-done.y_ref, f32[2,1,128]{2,1,0:T(1,128)S(1)} %bitcast.17), custom_call_target="tpu_custom_call" | custom-call | flops 1073741824 | bytes 6291456 | tf_op jit(solution)/shard_map/attend_forward/pallas_call | solution.py:71
  39.9 10.0 %collective-permute-done.1.rest_2_ = bf16[128,3072]{1,0:T(8,128)(2,1)S(1)} collective-permute-done((bf16[128,3072]{1,0:T(8,128)(2,1)}, bf16[128,3072]{1,0:T(8,128)(2,1)S(1)}, u32[]{:S(2)}, u32[]{:S(2)}) %collective-permute-start.1) | collective-permute-done | bytes 786464 | tf_op jit(solution)/shard_map/ppermute | solution.py:270
  49.9 2.1 %collective-permute-done.rest_1_ = bf16[128,3072]{1,0:T(8,128)(2,1)S(1)} collective-permute-done((bf16[128,3072]{1,0:T(8,128)(2,1)}, bf16[128,3072]{1,0:T(8,128)(2,1)S(1)}, u32[]{:S(2)}, u32[]{:S(2)}) %collective-permute-start) | collective-permute-done | bytes 786464 | tf_op jit(solution)/shard_map/ppermute | solution.py:270
  52.0 0.4 collective-permute-start.3
  52.4 1.7 %collective-permute-start.2 = (bf16[64,3072]{1,0:T(8,128)(2,1)S(1)}, bf16[64,3072]{1,0:T(8,128)(2,1)S(1)}, u32[]{:S(2)}, u32[]{:S(2)}) collective-permute-start(bf16[64,3072]{1,0:T(8,128)(2,1)S(1)} %slice.18), channel_id=1, source_target_pairs={{0,32},{16,48},{32,64},{48,80},{64,96},{80,112},{96,0},{112,16},{1... | collective-permute-start | bytes 1179656 | tf_op jit(solution)/shard_map/ppermute | solution.py:270
  54.1 0.0 collective-permute-start.4
  54.1 0.5 collective-permute-start.5
  54.6 0.0 collective-permute-start.6
  54.6 0.1 broadcast_in_dim.2
  54.7 19.3 %all_to_all.15.messages_ref = f32[128,2,2,128]{3,2,1,0:T(2,128)S(1)} all-to-all(f32[128,2,2,128]{3,2,1,0:T(2,128)S(1)} %broadcast_in_dim.2), channel_id=1, replica_groups=mesh['seq'=8,'dp'=16] {'seq','dp'}, dimensions={0} | all-to-all | bytes 524288 | tf_op jit(solution)/shard_map/all_to_all | solution.py:298
  74.0 0.0 collective-permute-done.3.rest_4_
  74.0 0.0 collective-permute-done.2.rest_3_
  74.0 0.0 collective-permute-start.7
  74.0 0.5 collective-permute-start.8
  74.6 0.0 collective-permute-done.4.rest_5_
  74.6 1.2 collective-permute-done.7.rest_8_
  75.8 0.6 collective-permute-done.8.rest_9_
  76.3 0.0 collective-permute-done.5.rest_6_
  76.3 6.8 %projection_backward.1 = (bf16[2,128,1024]{2,1,0:T(8,128)(2,1)S(1)}, f32[1,5120]{1,0:T(1,128)S(1)}) custom-call(s32[1]{0:T(128)} %bitcast.4.place_ref, f32[128,2,2,128]{3,2,1,0:T(2,128)S(1)} %all_to_all.15.messages_ref, f32[1,3072]{1,0:T(1,128)S(1)} %bitcast.16, bf16[2,128,1024]{2,1,0:T(8,128)(2,1)S(1)} %get-tuple-element.18.out_ref, ...), custom_call_target="tpu_custom_call" | custom-call | flops 3221225472 | bytes 9437184 | tf_op jit(solution)/shard_map/projection_backward/pallas_call | solution.py:174
  83.2 1.0 collective-permute-start.11
  84.1 2.0 %collective-permute-start.10 = (f32[1,5120]{1,0:T(1,128)S(1)}, f32[1,5120]{1,0:T(1,128)S(1)}, u32[]{:S(2)}, u32[]{:S(2)}) collective-permute-start(f32[1,5120]{1,0:T(1,128)S(1)} %get-tuple-element.26), channel_id=1, source_target_pairs={{0,64},{16,80},{32,96},{48,112},{64,0},{80,16},{96,32},{112,48},{1... | collective-permute-start | bytes 61448 | tf_op jit(solution)/shard_map/ppermute | solution.py:252
  86.1 1.2 collective-permute-start.9
  87.3 7.0 %attend_backward.1 = bf16[8,2,3,128,128]{4,3,2,1,0:T(8,128)(2,1)} custom-call(bf16[8,2,3,128,128]{4,3,2,1,0:T(8,128)(2,1)S(1)} %all-to-all-done.y_ref, bf16[2,1024,1024]{2,1,0:T(8,128)(2,1)S(1)} %get-tuple-element.17.p_ref, bf16[2,128,1024]{2,1,0:T(8,128)(2,1)S(1)} %get-tuple-element.18.out_ref, bf16[2,128,1024]{2,1,0:T(8,128)(2,1)S(1)} %get-tuple-element.25.grad_ref), custom_call_target="tpu_custom_call" | custom-call | flops 2147483648 | bytes 8388608 | tf_op jit(solution)/shard_map/attend_backward/pallas_call | solution.py:226
  94.3 0.0 collective-permute-done.11
  94.3 0.0 collective-permute-done.10
  94.3 0.0 collective-permute-done.9
  94.3 3.6 %all-to-all-start.2 = ((bf16[8,2,3,128,128]{4,3,2,1,0:T(8,128)(2,1)}), bf16[8,2,3,128,128]{4,3,2,1,0:T(8,128)(2,1)S(1)}, u32[]{:S(2)}, u32[]{:S(2)}) async-start(bf16[8,2,3,128,128]{4,3,2,1,0:T(8,128)(2,1)} %attend_backward.1), calls=%async_computation.2 | async-start | bytes 3145728 | tf_op jit(solution)/shard_map/all_to_all | solution.py:314
  97.9 0.7 collective-permute-start.12
  98.6 3.2 %collective-permute-done.12 = f32[1,5120]{1,0:T(1,128)S(1)} collective-permute-done((f32[1,5120]{1,0:T(1,128)S(1)}, f32[1,5120]{1,0:T(1,128)S(1)}, u32[]{:S(2)}, u32[]{:S(2)}) %collective-permute-start.12) | collective-permute-done | bytes 20512 | tf_op jit(solution)/shard_map/ppermute | solution.py:265
  101.8 0.7 collective-permute-start.13
  102.6 4.6 %collective-permute-done.13 = f32[1,5120]{1,0:T(1,128)S(1)} collective-permute-done((f32[1,5120]{1,0:T(1,128)S(1)}, f32[1,5120]{1,0:T(1,128)S(1)}, u32[]{:S(2)}, u32[]{:S(2)}) %collective-permute-start.13) | collective-permute-done | bytes 20512 | tf_op jit(solution)/shard_map/ppermute | solution.py:265
  107.2 0.7 collective-permute-start.14
  107.9 3.3 %collective-permute-done.14 = f32[1,5120]{1,0:T(1,128)S(1)} collective-permute-done((f32[1,5120]{1,0:T(1,128)S(1)}, f32[1,5120]{1,0:T(1,128)S(1)}, u32[]{:S(2)}, u32[]{:S(2)}) %collective-permute-start.14) | collective-permute-done | bytes 20512 | tf_op jit(solution)/shard_map/ppermute | solution.py:265
  111.3 0.9 collective-permute-start.15
  112.2 4.5 %collective-permute-done.15 = f32[1,5120]{1,0:T(1,128)S(1)} collective-permute-done((f32[1,5120]{1,0:T(1,128)S(1)}, f32[1,5120]{1,0:T(1,128)S(1)}, u32[]{:S(2)}, u32[]{:S(2)}) %collective-permute-start.15) | collective-permute-done | bytes 20512 | tf_op jit(solution)/shard_map/ppermute | solution.py:265
  116.7 0.1 collective-permute-start.16
  116.8 1.2 collective-permute-done.16
  118.0 0.6 slice.24
  118.6 0.6 slice.25
  119.2 0.3 all-to-all-done.2
  119.5 2.2 %copy.8 = bf16[1,3,128,16,128]{4,3,2,1,0:T(8,128)(2,1)} copy(bf16[1,3,128,16,128]{4,2,1,3,0:T(8,128)(2,1)S(1)} %bitcast.18) | data formatting | bytes 3145728
  (14 shorter events, 0.2 us)
Async XLA Ops:
  3.6 27.0 %all-to-all-start = ((bf16[8,2,3,128,128]{4,3,2,1,0:T(8,128)(2,1)}), bf16[8,2,3,128,128]{4,3,2,1,0:T(8,128)(2,1)S(1)}, u32[]{:S(2)}, u32[]{:S(2)}) async-start(bf16[8,2,3,128,128]{4,3,2,1,0:T(8,128)(2,1)} %bitcast.1), calls=%async_computation | async-start | bytes 3145728 | tf_op jit(solution)/shard_map/all_to_all | solution.py:290
  30.6 19.3 %collective-permute-start.1 = (bf16[128,3072]{1,0:T(8,128)(2,1)}, bf16[128,3072]{1,0:T(8,128)(2,1)S(1)}, u32[]{:S(2)}, u32[]{:S(2)}) collective-permute-start(bf16[128,3072]{1,0:T(8,128)(2,1)} %bitcast.12), channel_id=1, source_target_pairs={{0,96},{16,112},{32,0},{48,16},{64,32},{80,48},{96,64},{112,80},{1... | collective-permute-start | bytes 2359304 | tf_op jit(solution)/shard_map/ppermute | solution.py:270
  31.7 20.2 %collective-permute-start = (bf16[128,3072]{1,0:T(8,128)(2,1)}, bf16[128,3072]{1,0:T(8,128)(2,1)S(1)}, u32[]{:S(2)}, u32[]{:S(2)}) collective-permute-start(bf16[128,3072]{1,0:T(8,128)(2,1)} %bitcast.13), channel_id=1, source_target_pairs={{0,32},{16,48},{32,64},{48,80},{64,96},{80,112},{96,0},{112,16},{1... | collective-permute-start | bytes 2359304 | tf_op jit(solution)/shard_map/ppermute | solution.py:270
  39.9 14.3 %copy-start = (bf16[1,128,3072]{2,1,0:T(8,128)(2,1)S(1)}, bf16[1,128,3072]{2,1,0:T(8,128)(2,1)}, u32[]{:S(2)}) copy-start(bf16[1,128,3072]{2,1,0:T(8,128)(2,1)} %param.5) | copy-start | bytes 2359300
  39.9 36.5 %copy-start.1 = (f32[3072]{0:T(1024)S(1)}, f32[3072]{0:T(1024)}, u32[]{:S(2)}) copy-start(f32[3072]{0:T(1024)} %param.7) | copy-start | bytes 36868
  52.0 22.0 %collective-permute-start.3 = (bf16[64,3072]{1,0:T(8,128)(2,1)S(1)}, bf16[64,3072]{1,0:T(8,128)(2,1)S(1)}, u32[]{:S(2)}, u32[]{:S(2)}) collective-permute-start(bf16[64,3072]{1,0:T(8,128)(2,1)S(1)} %slice.19), channel_id=1, source_target_pairs={{0,96},{16,112},{32,0},{48,16},{64,32},{80,48},{96,64},{112,80},{1... | collective-permute-start | bytes 1179656 | tf_op jit(solution)/shard_map/ppermute | solution.py:270
  52.4 21.7 %collective-permute-start.2 = (bf16[64,3072]{1,0:T(8,128)(2,1)S(1)}, bf16[64,3072]{1,0:T(8,128)(2,1)S(1)}, u32[]{:S(2)}, u32[]{:S(2)}) collective-permute-start(bf16[64,3072]{1,0:T(8,128)(2,1)S(1)} %slice.18), channel_id=1, source_target_pairs={{0,32},{16,48},{32,64},{48,80},{64,96},{80,112},{96,0},{112,16},{1... | collective-permute-start | bytes 1179656 | tf_op jit(solution)/shard_map/ppermute | solution.py:270
  54.1 20.4 %collective-permute-start.4 = (bf16[128,3072]{1,0:T(8,128)(2,1)S(1)}, bf16[128,3072]{1,0:T(8,128)(2,1)S(1)}, u32[]{:S(2)}, u32[]{:S(2)}) collective-permute-start(bf16[128,3072]{1,0:T(8,128)(2,1)S(1)} %bitcast.14), channel_id=1, source_target_pairs={{0,16},{16,0},{32,48},{48,32},{64,80},{80,64},{96,112},{112,96},{1... | collective-permute-start | bytes 2359304 | tf_op jit(solution)/shard_map/ppermute | solution.py:274
  54.1 22.2 %collective-permute-start.5 = (bf16[128,3072]{1,0:T(8,128)(2,1)S(1)}, bf16[128,3072]{1,0:T(8,128)(2,1)S(1)}, u32[]{:S(2)}, u32[]{:S(2)}) collective-permute-start(bf16[128,3072]{1,0:T(8,128)(2,1)S(1)} %collective-permute-done.rest_1_), channel_id=1, source_target_pairs={{0,16},{16,0},{32,48},{48,32},{64,80},{80,64},{96,112},{112,96},{1... | collective-permute-start | bytes 2359304 | tf_op jit(solution)/shard_map/ppermute | solution.py:274
  54.6 21.7 %collective-permute-start.6 = (bf16[128,3072]{1,0:T(8,128)(2,1)S(1)}, bf16[128,3072]{1,0:T(8,128)(2,1)S(1)}, u32[]{:S(2)}, u32[]{:S(2)}) collective-permute-start(bf16[128,3072]{1,0:T(8,128)(2,1)S(1)} %collective-permute-done.1.rest_2_), channel_id=1, source_target_pairs={{0,16},{16,0},{32,48},{48,32},{64,80},{80,64},{96,112},{112,96},{1... | collective-permute-start | bytes 2359304 | tf_op jit(solution)/shard_map/ppermute | solution.py:274
  74.0 1.7 %collective-permute-start.7 = (bf16[64,3072]{1,0:T(8,128)(2,1)S(1)}, bf16[64,3072]{1,0:T(8,128)(2,1)S(1)}, u32[]{:S(2)}, u32[]{:S(2)}) collective-permute-start(bf16[64,3072]{1,0:T(8,128)(2,1)S(1)} %collective-permute-done.2.rest_3_), channel_id=1, source_target_pairs={{0,16},{16,0},{32,48},{48,32},{64,80},{80,64},{96,112},{112,96},{1... | collective-permute-start | bytes 1179656 | tf_op jit(solution)/shard_map/ppermute | solution.py:274
  74.0 2.3 %collective-permute-start.8 = (bf16[64,3072]{1,0:T(8,128)(2,1)S(1)}, bf16[64,3072]{1,0:T(8,128)(2,1)S(1)}, u32[]{:S(2)}, u32[]{:S(2)}) collective-permute-start(bf16[64,3072]{1,0:T(8,128)(2,1)S(1)} %collective-permute-done.3.rest_4_), channel_id=1, source_target_pairs={{0,16},{16,0},{32,48},{48,32},{64,80},{80,64},{96,112},{112,96},{1... | collective-permute-start | bytes 1179656 | tf_op jit(solution)/shard_map/ppermute | solution.py:274
  83.2 11.1 %collective-permute-start.11 = (f32[1,5120]{1,0:T(1,128)S(1)}, f32[1,5120]{1,0:T(1,128)S(1)}, u32[]{:S(2)}, u32[]{:S(2)}) collective-permute-start(f32[1,5120]{1,0:T(1,128)S(1)} %get-tuple-element.26), channel_id=1, source_target_pairs={{0,96},{16,112},{32,64},{48,80},{64,32},{80,48},{96,0},{112,16},{1... | collective-permute-start | bytes 61448 | tf_op jit(solution)/shard_map/ppermute | solution.py:252
  84.1 10.2 %collective-permute-start.10 = (f32[1,5120]{1,0:T(1,128)S(1)}, f32[1,5120]{1,0:T(1,128)S(1)}, u32[]{:S(2)}, u32[]{:S(2)}) collective-permute-start(f32[1,5120]{1,0:T(1,128)S(1)} %get-tuple-element.26), channel_id=1, source_target_pairs={{0,64},{16,80},{32,96},{48,112},{64,0},{80,16},{96,32},{112,48},{1... | collective-permute-start | bytes 61448 | tf_op jit(solution)/shard_map/ppermute | solution.py:252
  86.1 8.2 %collective-permute-start.9 = (f32[1,5120]{1,0:T(1,128)S(1)}, f32[1,5120]{1,0:T(1,128)S(1)}, u32[]{:S(2)}, u32[]{:S(2)}) collective-permute-start(f32[1,5120]{1,0:T(1,128)S(1)} %get-tuple-element.26), channel_id=1, source_target_pairs={{0,32},{16,48},{32,0},{48,16},{64,96},{80,112},{96,64},{112,80},{1... | collective-permute-start | bytes 61448 | tf_op jit(solution)/shard_map/ppermute | solution.py:252
  94.3 25.1 %all-to-all-start.2 = ((bf16[8,2,3,128,128]{4,3,2,1,0:T(8,128)(2,1)}), bf16[8,2,3,128,128]{4,3,2,1,0:T(8,128)(2,1)S(1)}, u32[]{:S(2)}, u32[]{:S(2)}) async-start(bf16[8,2,3,128,128]{4,3,2,1,0:T(8,128)(2,1)} %attend_backward.1), calls=%async_computation.2 | async-start | bytes 3145728 | tf_op jit(solution)/shard_map/all_to_all | solution.py:314
  97.9 3.9 %collective-permute-start.12 = (f32[1,5120]{1,0:T(1,128)S(1)}, f32[1,5120]{1,0:T(1,128)S(1)}, u32[]{:S(2)}, u32[]{:S(2)}) collective-permute-start(f32[1,5120]{1,0:T(1,128)S(1)} %add_add_fusion), channel_id=1, source_target_pairs={{0,1},{1,0},{2,3},{3,2},{4,5},{5,4},{6,7},{7,6},{8,9},{9,8},{10,11... | collective-permute-start | bytes 61448 | tf_op jit(solution)/shard_map/ppermute | solution.py:265
  101.8 5.4 %collective-permute-start.13 = (f32[1,5120]{1,0:T(1,128)S(1)}, f32[1,5120]{1,0:T(1,128)S(1)}, u32[]{:S(2)}, u32[]{:S(2)}) collective-permute-start(f32[1,5120]{1,0:T(1,128)S(1)} %add.31), channel_id=1, source_target_pairs={{0,2},{1,3},{2,0},{3,1},{4,6},{5,7},{6,4},{7,5},{8,10},{9,11},{10,... | collective-permute-start | bytes 61448 | tf_op jit(solution)/shard_map/ppermute | solution.py:265
  107.2 4.0 %collective-permute-start.14 = (f32[1,5120]{1,0:T(1,128)S(1)}, f32[1,5120]{1,0:T(1,128)S(1)}, u32[]{:S(2)}, u32[]{:S(2)}) collective-permute-start(f32[1,5120]{1,0:T(1,128)S(1)} %add.32), channel_id=1, source_target_pairs={{0,4},{1,5},{2,6},{3,7},{4,0},{5,1},{6,2},{7,3},{8,12},{9,13},{10,... | collective-permute-start | bytes 61448 | tf_op jit(solution)/shard_map/ppermute | solution.py:265
  111.3 5.4 %collective-permute-start.15 = (f32[1,5120]{1,0:T(1,128)S(1)}, f32[1,5120]{1,0:T(1,128)S(1)}, u32[]{:S(2)}, u32[]{:S(2)}) collective-permute-start(f32[1,5120]{1,0:T(1,128)S(1)} %add.33), channel_id=1, source_target_pairs={{0,8},{1,9},{2,10},{3,11},{4,12},{5,13},{6,14},{7,15},{8,0},{9,1},... | collective-permute-start | bytes 61448 | tf_op jit(solution)/shard_map/ppermute | solution.py:265
  116.7 1.3 %collective-permute-start.16 = (f32[1,5120]{1,0:T(1,128)S(1)}, f32[1,5120]{1,0:T(1,128)S(1)}, u32[]{:S(2)}, u32[]{:S(2)}) collective-permute-start(f32[1,5120]{1,0:T(1,128)S(1)} %add.34), channel_id=1, source_target_pairs={{0,16},{16,0},{32,48},{48,32},{64,80},{80,64},{96,112},{112,96},{1... | collective-permute-start | bytes 61448 | tf_op jit(solution)/shard_map/ppermute | solution.py:265

commit v3 on v2

--- a/solution.py
+++ b/solution.py
@@ -63,8 +63,14 @@
     bound = jnp.max(
         jnp.sqrt((act_row + epsilon) * (weight_max_ref[0] + epsilon)), axis=1, keepdims=True
     )
-    message_ref[0, 0:1] = act_row
-    message_ref[0, 1:2] = jnp.broadcast_to(bound, (1, 128))
+    head = pl.program_id(0)
+
+    @pl.when(head == 0)
+    def _():
+        message_ref[...] = jnp.zeros_like(message_ref)
+
+    message_ref[pl.ds(head, 1)] = act_row
+    message_ref[2:3] = jnp.maximum(message_ref[2:3], bound)
 
 
 def forward(heads, weight_max):
@@ -78,12 +84,12 @@
         out_specs=[
             pl.BlockSpec((1, LEN, LEN), lambda h: (h, 0, 0)),
             pl.BlockSpec((1, HEAD_DIM, LEN), lambda h: (h, 0, 0)),
-            pl.BlockSpec((1, 2, 128), lambda h: (h, 0, 0)),
+            pl.BlockSpec((8, 128), lambda h: (0, 0)),
         ],
         out_shape=[
             jax.ShapeDtypeStruct((LOCAL_HEADS, LEN, LEN), jnp.bfloat16),
             jax.ShapeDtypeStruct((LOCAL_HEADS, HEAD_DIM, LEN), jnp.bfloat16),
-            jax.ShapeDtypeStruct((LOCAL_HEADS, 2, 128), jnp.float32),
+            jax.ShapeDtypeStruct((8, 128), jnp.float32),
         ],
         compiler_params=pltpu.CompilerParams(vmem_limit_bytes=VMEM_LIMIT),
         cost_estimate=pl.CostEstimate(
@@ -99,7 +105,7 @@
 WIDTH = 512
 
 
-def projection_kernel(place_ref, messages_ref, clip_ref, out_ref, own_ref, *rest):
+def projection_kernel(place_ref, message_ref, bound_ref, clip_ref, out_ref, own_ref, *rest):
     pieces = rest[:10]
     grad_ref, vec_ref, cot_ref, wq_ref, tanh_ref, quant_ref, sem = rest[10:]
     place = place_ref[0]
@@ -116,12 +122,10 @@
         )
         copy.start()
         copies.append(copy)
-    bound = jnp.max(messages_ref[:, :, 1, :], axis=0)
-    bound = jnp.max(jnp.max(bound, axis=0, keepdims=True), axis=1, keepdims=True)
-    act_clip = act_fraction * bound
-    mine = messages_ref[pl.ds(pl.multiple_of(place * DP, DP), DP)]
-    act_max = jnp.max(mine[:, :, 0, :], axis=0)
-    act_column = jnp.concatenate([to_column(act_max[0:1]), to_column(act_max[1:2])], axis=0)
+    act_clip = act_fraction * bound_ref[2:3, 0:1]
+    act_column = jnp.concatenate(
+        [to_column(message_ref[0:1]), to_column(message_ref[1:2])], axis=0
+    )
     weight_max = None
     for j in range(D // WIDTH):
         weight = own_ref[:, j * WIDTH : (j + 1) * WIDTH]
@@ -168,12 +172,12 @@
     vec_ref[:, pl.ds(pl.multiple_of(place * CHANNELS, CHANNELS), CHANNELS)] = to_row(smooth_part)
 
 
-def projection(place, messages, clip, out, own_rows, pieces):
+def projection(place, message, bound, clip, out, own_rows, pieces):
     vmem = pl.BlockSpec(memory_space=pltpu.VMEM)
     hbm = pl.BlockSpec(memory_space=pl.ANY)
     return pl.pallas_call(
         projection_kernel,
-        in_specs=[pl.BlockSpec(memory_space=pltpu.SMEM), vmem, vmem, vmem, vmem] + [hbm] * 10,
+        in_specs=[pl.BlockSpec(memory_space=pltpu.SMEM), vmem, vmem, vmem, vmem, vmem] + [hbm] * 10,
         out_specs=[vmem, vmem],
         out_shape=[
             jax.ShapeDtypeStruct((LOCAL_HEADS, HEAD_DIM, LEN), jnp.bfloat16),
@@ -193,7 +197,7 @@
             transcendentals=CHANNELS * (D + LEN),
         ),
         name="projection_backward",
-    )(place, messages, clip, out, own_rows, *pieces)
+    )(place, message, bound, clip, out, own_rows, *pieces)
 
 
 def backward_kernel(y_ref, p_ref, out_ref, grad_ref, z_ref, ds_ref):
@@ -247,10 +251,12 @@
     )(heads, weights, out, grad_out)
 
 
+def exchange(tensor, axis, size, bits):
+    return lax.ppermute(tensor, axis, [(i, i ^ bits) for i in range(size)])
+
+
 def total_over_depth(vector):
-    moved = [
-        lax.ppermute(vector, "seq", [(i, i ^ bits) for i in range(SEQ)]) for bits in (2, 4, 6)
-    ]
+    moved = [exchange(vector, "seq", SEQ, bits) for bits in (2, 4, 6)]
     return (vector + moved[0]) + (moved[1] + moved[2])
 
 
@@ -262,7 +268,7 @@
         ("dp", DP, 8),
         ("seq", SEQ, 1),
     ):
-        vector = vector + lax.ppermute(vector, axis, [(i, i ^ bit) for i in range(size)])
+        vector = vector + exchange(vector, axis, size, bit)
     return vector
 
 
@@ -271,7 +277,7 @@
 
 
 def swap_cores(tensor):
-    return lax.ppermute(tensor, "seq", [(i, i ^ 1) for i in range(SEQ)])
+    return exchange(tensor, "seq", SEQ, 1)
 
 
 def after(tensors, *earlier):
@@ -295,20 +301,21 @@
     before = shift_depth(own_1, 1)
     behind = shift_depth(own_1, -1)
     weights, out, message = forward(heads, weight_max)
-    messages = lax.all_to_all(
-        jnp.broadcast_to(message[None], (SEQ * DP, LOCAL_HEADS, 2, 128)),
-        ("seq", "dp"),
-        split_axis=0,
-        concat_axis=0,
-        tiled=True,
-    )
+    for bit in (1, 2, 4):
+        message = jnp.maximum(message, exchange(message, "dp", DP, bit))
     before, behind = after((before, behind), message)
-    far_low = shift_depth(before[:HALF], 1)
-    far_high = shift_depth(behind[HALF:], -1)
+    halves, message = lax.optimization_barrier(((before[:HALF], behind[HALF:]), message))
+    far_low = shift_depth(halves[0], 1)
+    far_high = shift_depth(halves[1], -1)
+    message = jnp.maximum(message, exchange(message, "dp", DP, 8))
     pieces = [own, before, behind, far_low, far_high, own_swapped]
     pieces += [swap_cores(piece) for piece in (before, behind)]
-    pieces += [swap_cores(piece) for piece in after((far_low, far_high), messages)]
-    grad_out, vector = projection(place_vector, messages, clip, out, own_rows, pieces)
+    moved = [exchange(message, "seq", SEQ, bits) for bits in (2, 4, 6)]
+    bound = jnp.maximum(jnp.maximum(message, moved[0]), jnp.maximum(moved[1], moved[2]))
+    far_low, far_high, bound = lax.optimization_barrier((far_low, far_high, bound))
+    pieces += [swap_cores(piece) for piece in (far_low, far_high)]
+    bound = jnp.maximum(bound, exchange(bound, "seq", SEQ, 1))
+    grad_out, vector = projection(place_vector, message, bound, clip, out, own_rows, pieces)
     back = backward(heads, weights, out, grad_out)
     back, vector = lax.optimization_barrier((back, total_over_depth(vector)))
     received = lax.all_to_all(back, "seq", split_axis=0, concat_axis=0, tiled=True)

time: 123 us -> 119 us (0.967)
  blocking collectives: 19.3 us -> 0 us
  starting transfers between devices: 21.4 us -> 40 us
  waiting for transfers between devices: 50.6 us -> 47.9 us
    all_to_all x1 -> x0, blocking collectives: 19.3 us -> none  [per_device(): lax.all_to_all(jnp.broadcast_to(message[None], (SEQ * DP, LOCAL_HEADS, 2,...]
    ppermute x13 -> x21, starting transfers between devices: 8.29 us -> 25.1 us  [exchange(): return lax.ppermute(tensor, axis, [(i, i ^ bits) for i in range(size)])]
    ppermute x4, waiting for transfers between devices: 12.1 us -> 0.01 us  [shift_depth(): lax.ppermute(tensor, 'seq', [(i, (i + 2 * steps) % SEQ) for i in range(SE...]
    ppermute x13 -> x21, waiting for transfers between devices: 18.6 us -> 27.6 us  [exchange(): return lax.ppermute(tensor, axis, [(i, i ^ bits) for i in range(size)])]
  transfers between devices with their start and end apart: 19 -> 27, of which waited for: 11 -> 14; matrix products, arithmetic and copies ran while one was open for 3% -> 3% of each run, Pallas kernels for 12% -> 12%
where the time goes in v3:
time: 119 us; the launch traced here: 118 us
  waiting for transfers between devices  47.9 us (40%)
  starting transfers between devices  40 us (34%)
  Pallas kernels  21 us (18%)
  local copies, waits for them, and re-layouts  7.89 us (7%)
    ppermute x21, waiting for transfers between devices, exchange(): return lax.ppermute(tensor, axis, [(i, i ^ bits) for i in range(size)])  27.6 us
    ppermute x21, starting transfers between devices, exchange(): return lax.ppermute(tensor, axis, [(i, i ^ bits) for i in range(size)])  25.1 us
    all_to_all x1, waiting for transfers between devices, per_device(): heads = lax.all_to_all(send, 'seq', split_axis=0, concat_axis=0, tiled=True)  19.7 us
    pallas_call x1, Pallas kernels, forward(): pl.pallas_call(forward_kernel, grid=(LOCAL_HEADS,), in_specs=[pl.BlockSpe...  7.26 us
    pallas_call x1, Pallas kernels, backward(): pl.pallas_call(backward_kernel, grid=(LOCAL_HEADS,), in_specs=[pl.BlockSp...  6.95 us
    pallas_call x1, Pallas kernels, projection(): pl.pallas_call(projection_kernel, in_specs=[pl.BlockSpec(memory_space=plt...  6.81 us
    all_to_all x1, starting transfers between devices, per_device(): heads = lax.all_to_all(send, 'seq', split_axis=0, concat_axis=0, tiled=True)  5.4 us
    ppermute x4, starting transfers between devices, shift_depth(): lax.ppermute(tensor, 'seq', [(i, (i + 2 * steps) % SEQ) for i in range(SE...  5.26 us
  transfers between devices with their start and end apart: 27, of which 14 were waited for; matrix products, arithmetic and copies ran while one was open for 3% of the time, Pallas kernels for 12%

profile of v3, /device:TPU:0, one launch (start us, length us, event | category | flops | bytes accessed | tf_op | source)
XLA Modules:
  0.0 118.1 jit_solution(14458404948544357781)
XLA Ops:
  0.6 3.0 %copy.7 = bf16[1,3,128,16,128]{4,2,1,3,0:T(8,128)(2,1)} copy(bf16[1,3,128,16,128]{4,3,2,1,0:T(8,128)(2,1)} %param.4) | data formatting | bytes 3145728 | tf_op args[0]
  3.6 5.4 %all-to-all-start = ((bf16[8,2,3,128,128]{4,3,2,1,0:T(8,128)(2,1)}), bf16[8,2,3,128,128]{4,3,2,1,0:T(8,128)(2,1)S(1)}, u32[]{:S(2)}, u32[]{:S(2)}) async-start(bf16[8,2,3,128,128]{4,3,2,1,0:T(8,128)(2,1)} %bitcast.1), calls=%async_computation | async-start | bytes 3145728 | tf_op jit(solution)/shard_map/all_to_all | solution.py:296
  9.0 1.5 %constant_dynamic-slice_fusion.own_ref = bf16[256,3072]{1,0:T(8,128)(2,1)S(1)} fusion(bf16[2048,3072]{1,0:T(8,128)(2,1)} %param.6, s32[]{:T(128)S(6)} %select_n.3), kind=kLoop, calls=%fused_computation.3 | loop fusion | bytes 3145732 | tf_op jit(solution)/shard_map/dynamic_slice | solution.py:293
  10.5 0.4 abs_reduce_fusion
  10.9 19.7 %all-to-all-done.y_ref = bf16[8,2,3,128,128]{4,3,2,1,0:T(8,128)(2,1)S(1)} async-done(((bf16[8,2,3,128,128]{4,3,2,1,0:T(8,128)(2,1)}), bf16[8,2,3,128,128]{4,3,2,1,0:T(8,128)(2,1)S(1)}, u32[]{:S(2)}, u32[]{:S(2)}) %all-to-all-start) | async-done | bytes 1572896 | tf_op jit(solution)/shard_map/all_to_all | solution.py:296
  30.6 1.2 collective-permute-start.1
  31.7 0.9 collective-permute-start
  32.6 7.3 %attend_forward.1 = (bf16[2,1024,1024]{2,1,0:T(8,128)(2,1)S(1)}, bf16[2,128,1024]{2,1,0:T(8,128)(2,1)S(1)}, f32[8,128]{1,0:T(8,128)S(1)}) custom-call(bf16[8,2,3,128,128]{4,3,2,1,0:T(8,128)(2,1)S(1)} %all-to-all-done.y_ref, f32[2,1,128]{2,1,0:T(1,128)S(1)} %bitcast.17), custom_call_target="tpu_custom_call" | custom-call | flops 1073741824 | bytes 6291456 | tf_op jit(solution)/shard_map/attend_forward/pallas_call | solution.py:77
  39.9 1.5 %collective-permute-start.2 = (f32[8,128]{1,0:T(8,128)S(1)}, f32[8,128]{1,0:T(8,128)S(1)}, u32[]{:S(2)}, u32[]{:S(2)}) collective-permute-start(f32[8,128]{1,0:T(8,128)S(1)} %get-tuple-element.24), channel_id=1, source_target_pairs={{0,1},{1,0},{2,3},{3,2},{4,5},{5,4},{6,7},{7,6},{8,9},{9,8},{10,11... | collective-permute-start | bytes 12296 | tf_op jit(solution)/shard_map/ppermute | solution.py:255
  41.4 2.1 %collective-permute-done.2 = f32[8,128]{1,0:T(8,128)S(1)} collective-permute-done((f32[8,128]{1,0:T(8,128)S(1)}, f32[8,128]{1,0:T(8,128)S(1)}, u32[]{:S(2)}, u32[]{:S(2)}) %collective-permute-start.2) | collective-permute-done | bytes 4128 | tf_op jit(solution)/shard_map/ppermute | solution.py:255
  43.5 3.0 %collective-permute-start.3 = (f32[8,128]{1,0:T(8,128)S(1)}, f32[8,128]{1,0:T(8,128)S(1)}, u32[]{:S(2)}, u32[]{:S(2)}) collective-permute-start(f32[8,128]{1,0:T(8,128)S(1)} %max.24), channel_id=1, source_target_pairs={{0,2},{1,3},{2,0},{3,1},{4,6},{5,7},{6,4},{7,5},{8,10},{9,11},{10,... | collective-permute-start | bytes 12296 | tf_op jit(solution)/shard_map/ppermute | solution.py:255
  46.5 2.1 %collective-permute-done.3 = f32[8,128]{1,0:T(8,128)S(1)} collective-permute-done((f32[8,128]{1,0:T(8,128)S(1)}, f32[8,128]{1,0:T(8,128)S(1)}, u32[]{:S(2)}, u32[]{:S(2)}) %collective-permute-start.3) | collective-permute-done | bytes 4128 | tf_op jit(solution)/shard_map/ppermute | solution.py:255
  48.6 1.6 %collective-permute-start.4 = (f32[8,128]{1,0:T(8,128)S(1)}, f32[8,128]{1,0:T(8,128)S(1)}, u32[]{:S(2)}, u32[]{:S(2)}) collective-permute-start(f32[8,128]{1,0:T(8,128)S(1)} %max.25), channel_id=1, source_target_pairs={{0,4},{1,5},{2,6},{3,7},{4,0},{5,1},{6,2},{7,3},{8,12},{9,13},{10,... | collective-permute-start | bytes 12296 | tf_op jit(solution)/shard_map/ppermute | solution.py:255
  50.2 2.0 %collective-permute-done.4 = f32[8,128]{1,0:T(8,128)S(1)} collective-permute-done((f32[8,128]{1,0:T(8,128)S(1)}, f32[8,128]{1,0:T(8,128)S(1)}, u32[]{:S(2)}, u32[]{:S(2)}) %collective-permute-start.4) | collective-permute-done | bytes 4128 | tf_op jit(solution)/shard_map/ppermute | solution.py:255
  52.3 3.3 %collective-permute-start.5 = (f32[8,128]{1,0:T(8,128)S(1)}, f32[8,128]{1,0:T(8,128)S(1)}, u32[]{:S(2)}, u32[]{:S(2)}) collective-permute-start(f32[8,128]{1,0:T(8,128)S(1)} %max.26), channel_id=1, source_target_pairs={{0,8},{1,9},{2,10},{3,11},{4,12},{5,13},{6,14},{7,15},{8,0},{9,1},... | collective-permute-start | bytes 12296 | tf_op jit(solution)/shard_map/ppermute | solution.py:255
  55.6 0.6 collective-permute-start.6
  56.1 2.7 %collective-permute-start.7 = (bf16[64,3072]{1,0:T(8,128)(2,1)S(1)}, bf16[64,3072]{1,0:T(8,128)(2,1)S(1)}, u32[]{:S(2)}, u32[]{:S(2)}) collective-permute-start(bf16[64,3072]{1,0:T(8,128)(2,1)S(1)} %slice.19), channel_id=1, source_target_pairs={{0,96},{16,112},{32,0},{48,16},{64,32},{80,48},{96,64},{112,80},{1... | collective-permute-start | bytes 1179656 | tf_op jit(solution)/shard_map/ppermute | solution.py:276
  58.8 1.2 collective-permute-start.10
  60.0 0.3 collective-permute-start.9
  60.2 2.7 %collective-permute-start.8 = (f32[8,128]{1,0:T(8,128)S(1)}, f32[8,128]{1,0:T(8,128)S(1)}, u32[]{:S(2)}, u32[]{:S(2)}) collective-permute-start(f32[8,128]{1,0:T(8,128)S(1)} %max.27.message_ref), channel_id=1, source_target_pairs={{0,32},{16,48},{32,0},{48,16},{64,96},{80,112},{96,64},{112,80},{1... | collective-permute-start | bytes 12296 | tf_op jit(solution)/shard_map/ppermute | solution.py:255
  62.9 2.9 %collective-permute-done.10 = f32[8,128]{1,0:T(8,128)S(1)} collective-permute-done((f32[8,128]{1,0:T(8,128)S(1)}, f32[8,128]{1,0:T(8,128)S(1)}, u32[]{:S(2)}, u32[]{:S(2)}) %collective-permute-start.10) | collective-permute-done | bytes 4128 | tf_op jit(solution)/shard_map/ppermute | solution.py:255
  65.9 0.5 collective-permute-start.13
  66.4 0.1 collective-permute-start.14
  66.5 0.5 collective-permute-start.11
  67.0 0.1 collective-permute-start.15
  67.1 3.3 %collective-permute-done.11 = f32[8,128]{1,0:T(8,128)S(1)} collective-permute-done((f32[8,128]{1,0:T(8,128)S(1)}, f32[8,128]{1,0:T(8,128)S(1)}, u32[]{:S(2)}, u32[]{:S(2)}) %collective-permute-start.11) | collective-permute-done | bytes 4128 | tf_op jit(solution)/shard_map/ppermute | solution.py:255
  70.4 0.1 collective-permute-start.16
  70.6 0.4 collective-permute-done.15.rest_8_
  71.0 1.2 collective-permute-done.16.rest_9_
  72.1 6.8 %projection_backward.1 = (bf16[2,128,1024]{2,1,0:T(8,128)(2,1)S(1)}, f32[1,5120]{1,0:T(1,128)S(1)}) custom-call(s32[1]{0:T(128)} %bitcast.4.place_ref, f32[8,128]{1,0:T(8,128)S(1)} %max.27.message_ref, f32[8,128]{1,0:T(8,128)S(1)} %max.31.bound_ref, f32[1,3072]{1,0:T(1,128)S(1)} %bitcast.16, bf16[2,128,1024]{2,1,0:T(8,128)(2,1)S(1)} %get-tuple-element.22.out_ref, ...), custom_call_target="tpu_custom_call" | custom-call | flops 3221225472 | bytes 9437184 | tf_op jit(solution)/shard_map/projection_backward/pallas_call | solution.py:178
  79.0 3.0 %collective-permute-start.19 = (f32[1,5120]{1,0:T(1,128)S(1)}, f32[1,5120]{1,0:T(1,128)S(1)}, u32[]{:S(2)}, u32[]{:S(2)}) collective-permute-start(f32[1,5120]{1,0:T(1,128)S(1)} %get-tuple-element.34), channel_id=1, source_target_pairs={{0,96},{16,112},{32,64},{48,80},{64,32},{80,48},{96,0},{112,16},{1... | collective-permute-start | bytes 61448 | tf_op jit(solution)/shard_map/ppermute | solution.py:255
  82.0 1.1 collective-permute-start.17
  83.1 6.9 %attend_backward.1 = bf16[8,2,3,128,128]{4,3,2,1,0:T(8,128)(2,1)} custom-call(bf16[8,2,3,128,128]{4,3,2,1,0:T(8,128)(2,1)S(1)} %all-to-all-done.y_ref, bf16[2,1024,1024]{2,1,0:T(8,128)(2,1)S(1)} %get-tuple-element.21.p_ref, bf16[2,128,1024]{2,1,0:T(8,128)(2,1)S(1)} %get-tuple-element.22.out_ref, bf16[2,128,1024]{2,1,0:T(8,128)(2,1)S(1)} %get-tuple-element.33.grad_ref), custom_call_target="tpu_custom_call" | custom-call | flops 2147483648 | bytes 8388608 | tf_op jit(solution)/shard_map/attend_backward/pallas_call | solution.py:230
  90.1 4.2 %all-to-all-start.1 = ((bf16[8,2,3,128,128]{4,3,2,1,0:T(8,128)(2,1)}), bf16[8,2,3,128,128]{4,3,2,1,0:T(8,128)(2,1)S(1)}, u32[]{:S(2)}, u32[]{:S(2)}) async-start(bf16[8,2,3,128,128]{4,3,2,1,0:T(8,128)(2,1)} %attend_backward.1), calls=%async_computation.1 | async-start | bytes 3145728 | tf_op jit(solution)/shard_map/all_to_all | solution.py:321
  94.4 1.5 %collective-permute-start.20 = (f32[1,5120]{1,0:T(1,128)S(1)}, f32[1,5120]{1,0:T(1,128)S(1)}, u32[]{:S(2)}, u32[]{:S(2)}) collective-permute-start(f32[1,5120]{1,0:T(1,128)S(1)} %add_add_fusion), channel_id=1, source_target_pairs={{0,1},{1,0},{2,3},{3,2},{4,5},{5,4},{6,7},{7,6},{8,9},{9,8},{10,11... | collective-permute-start | bytes 61448 | tf_op jit(solution)/shard_map/ppermute | solution.py:255
  95.9 2.3 %collective-permute-done.20 = f32[1,5120]{1,0:T(1,128)S(1)} collective-permute-done((f32[1,5120]{1,0:T(1,128)S(1)}, f32[1,5120]{1,0:T(1,128)S(1)}, u32[]{:S(2)}, u32[]{:S(2)}) %collective-permute-start.20) | collective-permute-done | bytes 20512 | tf_op jit(solution)/shard_map/ppermute | solution.py:255
  98.2 3.1 %collective-permute-start.21 = (f32[1,5120]{1,0:T(1,128)S(1)}, f32[1,5120]{1,0:T(1,128)S(1)}, u32[]{:S(2)}, u32[]{:S(2)}) collective-permute-start(f32[1,5120]{1,0:T(1,128)S(1)} %add.31), channel_id=1, source_target_pairs={{0,2},{1,3},{2,0},{3,1},{4,6},{5,7},{6,4},{7,5},{8,10},{9,11},{10,... | collective-permute-start | bytes 61448 | tf_op jit(solution)/shard_map/ppermute | solution.py:255
  101.3 2.3 %collective-permute-done.21 = f32[1,5120]{1,0:T(1,128)S(1)} collective-permute-done((f32[1,5120]{1,0:T(1,128)S(1)}, f32[1,5120]{1,0:T(1,128)S(1)}, u32[]{:S(2)}, u32[]{:S(2)}) %collective-permute-start.21) | collective-permute-done | bytes 20512 | tf_op jit(solution)/shard_map/ppermute | solution.py:255
  103.6 0.8 collective-permute-start.22
  104.4 3.1 %collective-permute-done.22 = f32[1,5120]{1,0:T(1,128)S(1)} collective-permute-done((f32[1,5120]{1,0:T(1,128)S(1)}, f32[1,5120]{1,0:T(1,128)S(1)}, u32[]{:S(2)}, u32[]{:S(2)}) %collective-permute-start.22) | collective-permute-done | bytes 20512 | tf_op jit(solution)/shard_map/ppermute | solution.py:255
  107.5 0.7 collective-permute-start.23
  108.2 4.7 %collective-permute-done.23 = f32[1,5120]{1,0:T(1,128)S(1)} collective-permute-done((f32[1,5120]{1,0:T(1,128)S(1)}, f32[1,5120]{1,0:T(1,128)S(1)}, u32[]{:S(2)}, u32[]{:S(2)}) %collective-permute-start.23) | collective-permute-done | bytes 20512 | tf_op jit(solution)/shard_map/ppermute | solution.py:255
  112.9 0.1 collective-permute-start.24
  113.0 1.2 collective-permute-done.24
  114.2 0.6 slice.24
  114.8 0.6 slice.25
  115.4 0.6 all-to-all-done.1
  116.0 2.2 %copy.8 = bf16[1,3,128,16,128]{4,3,2,1,0:T(8,128)(2,1)} copy(bf16[1,3,128,16,128]{4,2,1,3,0:T(8,128)(2,1)S(1)} %bitcast.18) | data formatting | bytes 3145728
  (34 shorter events, 0.3 us)
Async XLA Ops:
  3.6 27.0 %all-to-all-start = ((bf16[8,2,3,128,128]{4,3,2,1,0:T(8,128)(2,1)}), bf16[8,2,3,128,128]{4,3,2,1,0:T(8,128)(2,1)S(1)}, u32[]{:S(2)}, u32[]{:S(2)}) async-start(bf16[8,2,3,128,128]{4,3,2,1,0:T(8,128)(2,1)} %bitcast.1), calls=%async_computation | async-start | bytes 3145728 | tf_op jit(solution)/shard_map/all_to_all | solution.py:296
  30.6 21.7 %collective-permute-start.1 = (bf16[128,3072]{1,0:T(8,128)(2,1)}, bf16[128,3072]{1,0:T(8,128)(2,1)S(1)}, u32[]{:S(2)}, u32[]{:S(2)}) collective-permute-start(bf16[128,3072]{1,0:T(8,128)(2,1)} %bitcast.12), channel_id=1, source_target_pairs={{0,96},{16,112},{32,0},{48,16},{64,32},{80,48},{96,64},{112,80},{1... | collective-permute-start | bytes 2359304 | tf_op jit(solution)/shard_map/ppermute | solution.py:276
  31.7 20.5 %collective-permute-start = (bf16[128,3072]{1,0:T(8,128)(2,1)}, bf16[128,3072]{1,0:T(8,128)(2,1)S(1)}, u32[]{:S(2)}, u32[]{:S(2)}) collective-permute-start(bf16[128,3072]{1,0:T(8,128)(2,1)} %bitcast.13), channel_id=1, source_target_pairs={{0,32},{16,48},{32,64},{48,80},{64,96},{80,112},{96,0},{112,16},{1... | collective-permute-start | bytes 2359304 | tf_op jit(solution)/shard_map/ppermute | solution.py:276
  39.9 26.0 %copy-start = (bf16[1,128,3072]{2,1,0:T(8,128)(2,1)S(1)}, bf16[1,128,3072]{2,1,0:T(8,128)(2,1)}, u32[]{:S(2)}) copy-start(bf16[1,128,3072]{2,1,0:T(8,128)(2,1)} %param.5) | copy-start | bytes 2359300
  39.9 32.3 %copy-start.1 = (f32[3072]{0:T(1024)S(1)}, f32[3072]{0:T(1024)}, u32[]{:S(2)}) copy-start(f32[3072]{0:T(1024)} %param.7) | copy-start | bytes 36868
  39.9 3.6 %collective-permute-start.2 = (f32[8,128]{1,0:T(8,128)S(1)}, f32[8,128]{1,0:T(8,128)S(1)}, u32[]{:S(2)}, u32[]{:S(2)}) collective-permute-start(f32[8,128]{1,0:T(8,128)S(1)} %get-tuple-element.24), channel_id=1, source_target_pairs={{0,1},{1,0},{2,3},{3,2},{4,5},{5,4},{6,7},{7,6},{8,9},{9,8},{10,11... | collective-permute-start | bytes 12296 | tf_op jit(solution)/shard_map/ppermute | solution.py:255
  43.5 5.1 %collective-permute-start.3 = (f32[8,128]{1,0:T(8,128)S(1)}, f32[8,128]{1,0:T(8,128)S(1)}, u32[]{:S(2)}, u32[]{:S(2)}) collective-permute-start(f32[8,128]{1,0:T(8,128)S(1)} %max.24), channel_id=1, source_target_pairs={{0,2},{1,3},{2,0},{3,1},{4,6},{5,7},{6,4},{7,5},{8,10},{9,11},{10,... | collective-permute-start | bytes 12296 | tf_op jit(solution)/shard_map/ppermute | solution.py:255
  48.6 3.6 %collective-permute-start.4 = (f32[8,128]{1,0:T(8,128)S(1)}, f32[8,128]{1,0:T(8,128)S(1)}, u32[]{:S(2)}, u32[]{:S(2)}) collective-permute-start(f32[8,128]{1,0:T(8,128)S(1)} %max.25), channel_id=1, source_target_pairs={{0,4},{1,5},{2,6},{3,7},{4,0},{5,1},{6,2},{7,3},{8,12},{9,13},{10,... | collective-permute-start | bytes 12296 | tf_op jit(solution)/shard_map/ppermute | solution.py:255
  52.3 6.5 %collective-permute-start.5 = (f32[8,128]{1,0:T(8,128)S(1)}, f32[8,128]{1,0:T(8,128)S(1)}, u32[]{:S(2)}, u32[]{:S(2)}) collective-permute-start(f32[8,128]{1,0:T(8,128)S(1)} %max.26), channel_id=1, source_target_pairs={{0,8},{1,9},{2,10},{3,11},{4,12},{5,13},{6,14},{7,15},{8,0},{9,1},... | collective-permute-start | bytes 12296 | tf_op jit(solution)/shard_map/ppermute | solution.py:255
  55.6 10.9 %collective-permute-start.6 = (bf16[64,3072]{1,0:T(8,128)(2,1)S(1)}, bf16[64,3072]{1,0:T(8,128)(2,1)S(1)}, u32[]{:S(2)}, u32[]{:S(2)}) collective-permute-start(bf16[64,3072]{1,0:T(8,128)(2,1)S(1)} %slice.18), channel_id=1, source_target_pairs={{0,32},{16,48},{32,64},{48,80},{64,96},{80,112},{96,0},{112,16},{1... | collective-permute-start | bytes 1179656 | tf_op jit(solution)/shard_map/ppermute | solution.py:276
  56.1 10.3 %collective-permute-start.7 = (bf16[64,3072]{1,0:T(8,128)(2,1)S(1)}, bf16[64,3072]{1,0:T(8,128)(2,1)S(1)}, u32[]{:S(2)}, u32[]{:S(2)}) collective-permute-start(bf16[64,3072]{1,0:T(8,128)(2,1)S(1)} %slice.19), channel_id=1, source_target_pairs={{0,96},{16,112},{32,0},{48,16},{64,32},{80,48},{96,64},{112,80},{1... | collective-permute-start | bytes 1179656 | tf_op jit(solution)/shard_map/ppermute | solution.py:276
  58.8 7.0 %collective-permute-start.10 = (f32[8,128]{1,0:T(8,128)S(1)}, f32[8,128]{1,0:T(8,128)S(1)}, u32[]{:S(2)}, u32[]{:S(2)}) collective-permute-start(f32[8,128]{1,0:T(8,128)S(1)} %max.27.message_ref), channel_id=1, source_target_pairs={{0,96},{16,112},{32,64},{48,80},{64,32},{80,48},{96,0},{112,16},{1... | collective-permute-start | bytes 12296 | tf_op jit(solution)/shard_map/ppermute | solution.py:255
  60.0 5.9 %collective-permute-start.9 = (f32[8,128]{1,0:T(8,128)S(1)}, f32[8,128]{1,0:T(8,128)S(1)}, u32[]{:S(2)}, u32[]{:S(2)}) collective-permute-start(f32[8,128]{1,0:T(8,128)S(1)} %max.27.message_ref), channel_id=1, source_target_pairs={{0,64},{16,80},{32,96},{48,112},{64,0},{80,16},{96,32},{112,48},{1... | collective-permute-start | bytes 12296 | tf_op jit(solution)/shard_map/ppermute | solution.py:255
  60.2 6.1 %collective-permute-start.8 = (f32[8,128]{1,0:T(8,128)S(1)}, f32[8,128]{1,0:T(8,128)S(1)}, u32[]{:S(2)}, u32[]{:S(2)}) collective-permute-start(f32[8,128]{1,0:T(8,128)S(1)} %max.27.message_ref), channel_id=1, source_target_pairs={{0,32},{16,48},{32,0},{48,16},{64,96},{80,112},{96,64},{112,80},{1... | collective-permute-start | bytes 12296 | tf_op jit(solution)/shard_map/ppermute | solution.py:255
  65.9 4.7 %collective-permute-start.12 = (bf16[128,3072]{1,0:T(8,128)(2,1)S(1)}, bf16[128,3072]{1,0:T(8,128)(2,1)S(1)}, u32[]{:S(2)}, u32[]{:S(2)}) collective-permute-start(bf16[128,3072]{1,0:T(8,128)(2,1)S(1)} %bitcast.14), channel_id=1, source_target_pairs={{0,16},{16,0},{32,48},{48,32},{64,80},{80,64},{96,112},{112,96},{1... | collective-permute-start | bytes 2359304 | tf_op jit(solution)/shard_map/ppermute | solution.py:255
  65.9 6.3 %collective-permute-start.13 = (bf16[128,3072]{1,0:T(8,128)(2,1)S(1)}, bf16[128,3072]{1,0:T(8,128)(2,1)S(1)}, u32[]{:S(2)}, u32[]{:S(2)}) collective-permute-start(bf16[128,3072]{1,0:T(8,128)(2,1)S(1)} %collective-permute-done.rest_1_), channel_id=1, source_target_pairs={{0,16},{16,0},{32,48},{48,32},{64,80},{80,64},{96,112},{112,96},{1... | collective-permute-start | bytes 2359304 | tf_op jit(solution)/shard_map/ppermute | solution.py:255
  66.4 5.8 %collective-permute-start.14 = (bf16[128,3072]{1,0:T(8,128)(2,1)S(1)}, bf16[128,3072]{1,0:T(8,128)(2,1)S(1)}, u32[]{:S(2)}, u32[]{:S(2)}) collective-permute-start(bf16[128,3072]{1,0:T(8,128)(2,1)S(1)} %collective-permute-done.1.rest_2_), channel_id=1, source_target_pairs={{0,16},{16,0},{32,48},{48,32},{64,80},{80,64},{96,112},{112,96},{1... | collective-permute-start | bytes 2359304 | tf_op jit(solution)/shard_map/ppermute | solution.py:255
  66.5 3.9 %collective-permute-start.11 = (f32[8,128]{1,0:T(8,128)S(1)}, f32[8,128]{1,0:T(8,128)S(1)}, u32[]{:S(2)}, u32[]{:S(2)}) collective-permute-start(f32[8,128]{1,0:T(8,128)S(1)} %maximum_maximum_fusion), channel_id=1, source_target_pairs={{0,16},{16,0},{32,48},{48,32},{64,80},{80,64},{96,112},{112,96},{1... | collective-permute-start | bytes 12296 | tf_op jit(solution)/shard_map/ppermute | solution.py:255
  67.0 4.0 %collective-permute-start.15 = (bf16[64,3072]{1,0:T(8,128)(2,1)S(1)}, bf16[64,3072]{1,0:T(8,128)(2,1)S(1)}, u32[]{:S(2)}, u32[]{:S(2)}) collective-permute-start(bf16[64,3072]{1,0:T(8,128)(2,1)S(1)} %collective-permute-done.6.rest_3_), channel_id=1, source_target_pairs={{0,16},{16,0},{32,48},{48,32},{64,80},{80,64},{96,112},{112,96},{1... | collective-permute-start | bytes 1179656 | tf_op jit(solution)/shard_map/ppermute | solution.py:255
  70.4 1.7 %collective-permute-start.16 = (bf16[64,3072]{1,0:T(8,128)(2,1)S(1)}, bf16[64,3072]{1,0:T(8,128)(2,1)S(1)}, u32[]{:S(2)}, u32[]{:S(2)}) collective-permute-start(bf16[64,3072]{1,0:T(8,128)(2,1)S(1)} %collective-permute-done.7.rest_4_), channel_id=1, source_target_pairs={{0,16},{16,0},{32,48},{48,32},{64,80},{80,64},{96,112},{112,96},{1... | collective-permute-start | bytes 1179656 | tf_op jit(solution)/shard_map/ppermute | solution.py:255
  79.0 11.1 %collective-permute-start.19 = (f32[1,5120]{1,0:T(1,128)S(1)}, f32[1,5120]{1,0:T(1,128)S(1)}, u32[]{:S(2)}, u32[]{:S(2)}) collective-permute-start(f32[1,5120]{1,0:T(1,128)S(1)} %get-tuple-element.34), channel_id=1, source_target_pairs={{0,96},{16,112},{32,64},{48,80},{64,32},{80,48},{96,0},{112,16},{1... | collective-permute-start | bytes 61448 | tf_op jit(solution)/shard_map/ppermute | solution.py:255
  82.0 8.1 %collective-permute-start.18 = (f32[1,5120]{1,0:T(1,128)S(1)}, f32[1,5120]{1,0:T(1,128)S(1)}, u32[]{:S(2)}, u32[]{:S(2)}) collective-permute-start(f32[1,5120]{1,0:T(1,128)S(1)} %get-tuple-element.34), channel_id=1, source_target_pairs={{0,64},{16,80},{32,96},{48,112},{64,0},{80,16},{96,32},{112,48},{1... | collective-permute-start | bytes 61448 | tf_op jit(solution)/shard_map/ppermute | solution.py:255
  82.0 8.1 %collective-permute-start.17 = (f32[1,5120]{1,0:T(1,128)S(1)}, f32[1,5120]{1,0:T(1,128)S(1)}, u32[]{:S(2)}, u32[]{:S(2)}) collective-permute-start(f32[1,5120]{1,0:T(1,128)S(1)} %get-tuple-element.34), channel_id=1, source_target_pairs={{0,32},{16,48},{32,0},{48,16},{64,96},{80,112},{96,64},{112,80},{1... | collective-permute-start | bytes 61448 | tf_op jit(solution)/shard_map/ppermute | solution.py:255
  90.1 25.8 %all-to-all-start.1 = ((bf16[8,2,3,128,128]{4,3,2,1,0:T(8,128)(2,1)}), bf16[8,2,3,128,128]{4,3,2,1,0:T(8,128)(2,1)S(1)}, u32[]{:S(2)}, u32[]{:S(2)}) async-start(bf16[8,2,3,128,128]{4,3,2,1,0:T(8,128)(2,1)} %attend_backward.1), calls=%async_computation.1 | async-start | bytes 3145728 | tf_op jit(solution)/shard_map/all_to_all | solution.py:321
  94.4 3.8 %collective-permute-start.20 = (f32[1,5120]{1,0:T(1,128)S(1)}, f32[1,5120]{1,0:T(1,128)S(1)}, u32[]{:S(2)}, u32[]{:S(2)}) collective-permute-start(f32[1,5120]{1,0:T(1,128)S(1)} %add_add_fusion), channel_id=1, source_target_pairs={{0,1},{1,0},{2,3},{3,2},{4,5},{5,4},{6,7},{7,6},{8,9},{9,8},{10,11... | collective-permute-start | bytes 61448 | tf_op jit(solution)/shard_map/ppermute | solution.py:255
  98.2 5.4 %collective-permute-start.21 = (f32[1,5120]{1,0:T(1,128)S(1)}, f32[1,5120]{1,0:T(1,128)S(1)}, u32[]{:S(2)}, u32[]{:S(2)}) collective-permute-start(f32[1,5120]{1,0:T(1,128)S(1)} %add.31), channel_id=1, source_target_pairs={{0,2},{1,3},{2,0},{3,1},{4,6},{5,7},{6,4},{7,5},{8,10},{9,11},{10,... | collective-permute-start | bytes 61448 | tf_op jit(solution)/shard_map/ppermute | solution.py:255
  103.6 3.9 %collective-permute-start.22 = (f32[1,5120]{1,0:T(1,128)S(1)}, f32[1,5120]{1,0:T(1,128)S(1)}, u32[]{:S(2)}, u32[]{:S(2)}) collective-permute-start(f32[1,5120]{1,0:T(1,128)S(1)} %add.32), channel_id=1, source_target_pairs={{0,4},{1,5},{2,6},{3,7},{4,0},{5,1},{6,2},{7,3},{8,12},{9,13},{10,... | collective-permute-start | bytes 61448 | tf_op jit(solution)/shard_map/ppermute | solution.py:255
  107.5 5.4 %collective-permute-start.23 = (f32[1,5120]{1,0:T(1,128)S(1)}, f32[1,5120]{1,0:T(1,128)S(1)}, u32[]{:S(2)}, u32[]{:S(2)}) collective-permute-start(f32[1,5120]{1,0:T(1,128)S(1)} %add.33), channel_id=1, source_target_pairs={{0,8},{1,9},{2,10},{3,11},{4,12},{5,13},{6,14},{7,15},{8,0},{9,1},... | collective-permute-start | bytes 61448 | tf_op jit(solution)/shard_map/ppermute | solution.py:255
  112.9 1.3 %collective-permute-start.24 = (f32[1,5120]{1,0:T(1,128)S(1)}, f32[1,5120]{1,0:T(1,128)S(1)}, u32[]{:S(2)}, u32[]{:S(2)}) collective-permute-start(f32[1,5120]{1,0:T(1,128)S(1)} %add.34), channel_id=1, source_target_pairs={{0,16},{16,0},{32,48},{48,32},{64,80},{80,64},{96,112},{112,96},{1... | collective-permute-start | bytes 61448 | tf_op jit(solution)/shard_map/ppermute | solution.py:255

commit v4 on v3

--- a/solution.py
+++ b/solution.py
@@ -45,20 +45,16 @@
 def forward_kernel(y_ref, weight_max_ref, p_ref, out_ref, message_ref):
     keys = y_ref[:, 0, 1].reshape(LEN, HEAD_DIM)
     values = y_ref[:, 0, 2].reshape(LEN, HEAD_DIM)
-    top = None
-    for b in range(NUM_BLOCKS):
-        queries = y_ref[2 * b : 2 * b + 2, 0, 0].reshape(BLOCK, HEAD_DIM)
-        scores = dot(keys, queries, NT)
-        row_top = jnp.max(scores, axis=0, keepdims=True)
-        exponent = jnp.exp2((scores - row_top) * EXP2_SCALE)
-        total = jnp.sum(exponent, axis=0, keepdims=True)
-        weights = (exponent * (1.0 / total)).astype(jnp.bfloat16)
-        columns = pl.ds(b * BLOCK, BLOCK)
-        p_ref[0, :, columns] = weights
-        mixed = dot(values, weights, TN).astype(jnp.bfloat16)
-        out_ref[0, :, columns] = mixed
-        block_top = jnp.max(jnp.abs(mixed.astype(jnp.float32)), axis=1, keepdims=True)
-        top = block_top if top is None else jnp.maximum(top, block_top)
+    queries = y_ref[:, 0, 0].reshape(LEN, HEAD_DIM)
+    scores = dot(keys, queries, NT)
+    row_top = jnp.max(scores, axis=0, keepdims=True)
+    exponent = jnp.exp2((scores - row_top) * EXP2_SCALE)
+    total = jnp.sum(exponent, axis=0, keepdims=True)
+    weights = (exponent * (1.0 / total)).astype(jnp.bfloat16)
+    p_ref[0] = weights
+    mixed = dot(values, weights, TN).astype(jnp.bfloat16)
+    out_ref[0] = mixed
+    top = jnp.max(jnp.abs(mixed.astype(jnp.float32)), axis=1, keepdims=True)
     act_row = to_row(top)
     bound = jnp.max(
         jnp.sqrt((act_row + epsilon) * (weight_max_ref[0] + epsilon)), axis=1, keepdims=True
@@ -203,8 +199,8 @@
 def backward_kernel(y_ref, p_ref, out_ref, grad_ref, z_ref, ds_ref):
     keys = y_ref[:, 0, 1].reshape(LEN, HEAD_DIM)
     values = y_ref[:, 0, 2].reshape(LEN, HEAD_DIM)
-    for b in range(NUM_BLOCKS):
-        columns = pl.ds(b * BLOCK, BLOCK)
+    for b in range(LEN // WIDTH):
+        columns = pl.ds(b * WIDTH, WIDTH)
         grad_out = grad_ref[0, :, columns]
         delta = jnp.sum(
             grad_out.astype(jnp.float32) * out_ref[0, :, columns].astype(jnp.float32),
@@ -213,13 +209,10 @@
         )
         grad_weights = dot(values, grad_out, NN)
         weights = p_ref[0, :, columns].astype(jnp.float32)
-        grad_scores = (weights * (grad_weights - delta)).astype(jnp.bfloat16)
-        ds_ref[:, columns] = grad_scores
-        grad_query = dot(keys, grad_scores, TN) * SCALE
-        z_ref[2 * b : 2 * b + 2, 0, 0] = (
-            grad_query.T.astype(jnp.bfloat16).reshape(2, TOKENS, HEAD_DIM)
-        )
+        ds_ref[:, columns] = (weights * (grad_weights - delta)).astype(jnp.bfloat16)
     queries = y_ref[:, 0, 0].reshape(LEN, HEAD_DIM)
+    grad_query = (dot(keys, ds_ref[...], TN) * SCALE).astype(jnp.bfloat16)
+    z_ref[:, 0, 0] = grad_query.T.reshape(SEQ, TOKENS, HEAD_DIM)
     grad_value = dot(p_ref[0], grad_ref[0], NT)
     z_ref[:, 0, 2] = grad_value.astype(jnp.bfloat16).reshape(SEQ, TOKENS, HEAD_DIM)
     grad_key = dot(ds_ref[...], queries, NN) * SCALE
@@ -301,21 +294,24 @@
     before = shift_depth(own_1, 1)
     behind = shift_depth(own_1, -1)
     weights, out, message = forward(heads, weight_max)
+    is_bound = lax.broadcasted_iota(jnp.int32, message.shape, 0) == 2
     for bit in (1, 2, 4):
         message = jnp.maximum(message, exchange(message, "dp", DP, bit))
     before, behind = after((before, behind), message)
     halves, message = lax.optimization_barrier(((before[:HALF], behind[HALF:]), message))
     far_low = shift_depth(halves[0], 1)
     far_high = shift_depth(halves[1], -1)
-    message = jnp.maximum(message, exchange(message, "dp", DP, 8))
-    pieces = [own, before, behind, far_low, far_high, own_swapped]
-    pieces += [swap_cores(piece) for piece in (before, behind)]
     moved = [exchange(message, "seq", SEQ, bits) for bits in (2, 4, 6)]
     bound = jnp.maximum(jnp.maximum(message, moved[0]), jnp.maximum(moved[1], moved[2]))
-    far_low, far_high, bound = lax.optimization_barrier((far_low, far_high, bound))
-    pieces += [swap_cores(piece) for piece in (far_low, far_high)]
-    bound = jnp.maximum(bound, exchange(bound, "seq", SEQ, 1))
-    grad_out, vector = projection(place_vector, message, bound, clip, out, own_rows, pieces)
+    message = jnp.where(is_bound, bound, message)
+    for bit in (8,):
+        message = jnp.maximum(message, exchange(message, "dp", DP, bit))
+    far_low, far_high, message = lax.optimization_barrier((far_low, far_high, message))
+    pair = jnp.maximum(message, exchange(message, "seq", SEQ, 1))
+    message = jnp.where(is_bound, pair, message)
+    pieces = [own, before, behind, far_low, far_high, own_swapped]
+    pieces += [swap_cores(piece) for piece in (before, behind, far_low, far_high)]
+    grad_out, vector = projection(place_vector, message, message, clip, out, own_rows, pieces)
     back = backward(heads, weights, out, grad_out)
     back, vector = lax.optimization_barrier((back, total_over_depth(vector)))
     received = lax.all_to_all(back, "seq", split_axis=0, concat_axis=0, tiled=True)

time: 119 us -> 114 us (0.958)
  Pallas kernels: 21 us -> 16.5 us
  waiting for transfers between devices: 47.9 us -> 44.1 us
  starting transfers between devices: 40 us -> 43.3 us
    ppermute x21, waiting for transfers between devices: 27.6 us -> 19.9 us  [exchange(): return lax.ppermute(tensor, axis, [(i, i ^ bits) for i in range(size)])]
    ppermute x4, waiting for transfers between devices: 0.01 us -> 3.86 us  [shift_depth(): lax.ppermute(tensor, 'seq', [(i, (i + 2 * steps) % SEQ) for i in range(SE...]
    ppermute x21, starting transfers between devices: 25.1 us -> 28.5 us  [exchange(): return lax.ppermute(tensor, axis, [(i, i ^ bits) for i in range(size)])]
    pallas_call x1, Pallas kernels: 7.26 us -> 4.49 us  [forward(): pl.pallas_call(forward_kernel, grid=(LOCAL_HEADS,), in_specs=[pl.BlockSpe...]
    pallas_call x1, Pallas kernels: 6.95 us -> 5.23 us  [backward(): pl.pallas_call(backward_kernel, grid=(LOCAL_HEADS,), in_specs=[pl.BlockSp...]
  transfers between devices with their start and end apart: 27 -> 27, of which waited for: 14 -> 17; matrix products, arithmetic and copies ran while one was open for 3% -> 3% of each run, Pallas kernels for 12% -> 9%
where the time goes in v4:
time: 114 us; the launch traced here: 113 us
  waiting for transfers between devices  44.1 us (39%)
  starting transfers between devices  43.3 us (38%)
  Pallas kernels  16.5 us (14%)
  local copies, waits for them, and re-layouts  7.89 us (7%)
    ppermute x21, starting transfers between devices, exchange(): return lax.ppermute(tensor, axis, [(i, i ^ bits) for i in range(size)])  28.5 us
    ppermute x21, waiting for transfers between devices, exchange(): return lax.ppermute(tensor, axis, [(i, i ^ bits) for i in range(size)])  19.9 us
    all_to_all x1, waiting for transfers between devices, per_device(): heads = lax.all_to_all(send, 'seq', split_axis=0, concat_axis=0, tiled=True)  19.7 us
    pallas_call x1, Pallas kernels, projection(): pl.pallas_call(projection_kernel, in_specs=[pl.BlockSpec(memory_space=plt...  6.82 us
    all_to_all x1, starting transfers between devices, per_device(): heads = lax.all_to_all(send, 'seq', split_axis=0, concat_axis=0, tiled=True)  5.4 us
    ppermute x4, starting transfers between devices, shift_depth(): lax.ppermute(tensor, 'seq', [(i, (i + 2 * steps) % SEQ) for i in range(SE...  5.26 us
    pallas_call x1, Pallas kernels, backward(): pl.pallas_call(backward_kernel, grid=(LOCAL_HEADS,), in_specs=[pl.BlockSp...  5.23 us
    unnamed x6, local copies, waits for them, and re-layouts  5.12 us
  transfers between devices with their start and end apart: 27, of which 17 were waited for; matrix products, arithmetic and copies ran while one was open for 3% of the time, Pallas kernels for 9%

profile of v4, /device:TPU:0, one launch (start us, length us, event | category | flops | bytes accessed | tf_op | source)
XLA Modules:
  0.0 113.2 jit_solution(9655382643021257029)
XLA Ops:
  0.6 3.0 %copy.7 = bf16[1,3,128,16,128]{4,2,1,3,0:T(8,128)(2,1)} copy(bf16[1,3,128,16,128]{4,3,2,1,0:T(8,128)(2,1)} %param.4) | data formatting | bytes 3145728 | tf_op args[0]
  3.6 5.4 %all-to-all-start = ((bf16[8,2,3,128,128]{4,3,2,1,0:T(8,128)(2,1)}), bf16[8,2,3,128,128]{4,3,2,1,0:T(8,128)(2,1)S(1)}, u32[]{:S(2)}, u32[]{:S(2)}) async-start(bf16[8,2,3,128,128]{4,3,2,1,0:T(8,128)(2,1)} %bitcast.1), calls=%async_computation | async-start | bytes 3145728 | tf_op jit(solution)/shard_map/all_to_all | solution.py:289
  9.0 1.5 %constant_dynamic-slice_fusion.own_ref = bf16[256,3072]{1,0:T(8,128)(2,1)S(1)} fusion(bf16[2048,3072]{1,0:T(8,128)(2,1)} %param.6, s32[]{:T(128)S(6)} %select_n.10), kind=kLoop, calls=%fused_computation.5 | loop fusion | bytes 3145732 | tf_op jit(solution)/shard_map/dynamic_slice | solution.py:286
  10.5 0.4 abs_reduce_fusion
  10.9 19.7 %all-to-all-done.y_ref = bf16[8,2,3,128,128]{4,3,2,1,0:T(8,128)(2,1)S(1)} async-done(((bf16[8,2,3,128,128]{4,3,2,1,0:T(8,128)(2,1)}), bf16[8,2,3,128,128]{4,3,2,1,0:T(8,128)(2,1)S(1)}, u32[]{:S(2)}, u32[]{:S(2)}) %all-to-all-start) | async-done | bytes 1572896 | tf_op jit(solution)/shard_map/all_to_all | solution.py:289
  30.6 1.2 %collective-permute-start.1 = (bf16[128,3072]{1,0:T(8,128)(2,1)}, bf16[128,3072]{1,0:T(8,128)(2,1)S(1)}, u32[]{:S(2)}, u32[]{:S(2)}) collective-permute-start(bf16[128,3072]{1,0:T(8,128)(2,1)} %bitcast.12), channel_id=1, source_target_pairs={{0,96},{16,112},{32,0},{48,16},{64,32},{80,48},{96,64},{112,80},{1... | collective-permute-start | bytes 2359304 | tf_op jit(solution)/shard_map/ppermute | solution.py:269
  31.7 0.9 collective-permute-start
  32.6 4.5 %attend_forward.1 = (bf16[2,1024,1024]{2,1,0:T(8,128)(2,1)S(1)}, bf16[2,128,1024]{2,1,0:T(8,128)(2,1)S(1)}, f32[8,128]{1,0:T(8,128)S(1)}) custom-call(bf16[8,2,3,128,128]{4,3,2,1,0:T(8,128)(2,1)S(1)} %all-to-all-done.y_ref, f32[2,1,128]{2,1,0:T(1,128)S(1)} %bitcast.17), custom_call_target="tpu_custom_call" | custom-call | flops 1073741824 | bytes 6291456 | tf_op jit(solution)/shard_map/attend_forward/pallas_call | solution.py:73
  37.1 1.5 %collective-permute-start.2 = (f32[8,128]{1,0:T(8,128)S(1)}, f32[8,128]{1,0:T(8,128)S(1)}, u32[]{:S(2)}, u32[]{:S(2)}) collective-permute-start(f32[8,128]{1,0:T(8,128)S(1)} %get-tuple-element.24), channel_id=1, source_target_pairs={{0,1},{1,0},{2,3},{3,2},{4,5},{5,4},{6,7},{7,6},{8,9},{9,8},{10,11... | collective-permute-start | bytes 12296 | tf_op jit(solution)/shard_map/ppermute | solution.py:248
  38.6 2.1 %collective-permute-done.2 = f32[8,128]{1,0:T(8,128)S(1)} collective-permute-done((f32[8,128]{1,0:T(8,128)S(1)}, f32[8,128]{1,0:T(8,128)S(1)}, u32[]{:S(2)}, u32[]{:S(2)}) %collective-permute-start.2) | collective-permute-done | bytes 4128 | tf_op jit(solution)/shard_map/ppermute | solution.py:248
  40.7 3.0 %collective-permute-start.3 = (f32[8,128]{1,0:T(8,128)S(1)}, f32[8,128]{1,0:T(8,128)S(1)}, u32[]{:S(2)}, u32[]{:S(2)}) collective-permute-start(f32[8,128]{1,0:T(8,128)S(1)} %max.24), channel_id=1, source_target_pairs={{0,2},{1,3},{2,0},{3,1},{4,6},{5,7},{6,4},{7,5},{8,10},{9,11},{10,... | collective-permute-start | bytes 12296 | tf_op jit(solution)/shard_map/ppermute | solution.py:248
  43.8 2.1 %collective-permute-done.3 = f32[8,128]{1,0:T(8,128)S(1)} collective-permute-done((f32[8,128]{1,0:T(8,128)S(1)}, f32[8,128]{1,0:T(8,128)S(1)}, u32[]{:S(2)}, u32[]{:S(2)}) %collective-permute-start.3) | collective-permute-done | bytes 4128 | tf_op jit(solution)/shard_map/ppermute | solution.py:248
  45.9 1.6 %collective-permute-start.4 = (f32[8,128]{1,0:T(8,128)S(1)}, f32[8,128]{1,0:T(8,128)S(1)}, u32[]{:S(2)}, u32[]{:S(2)}) collective-permute-start(f32[8,128]{1,0:T(8,128)S(1)} %max.25), channel_id=1, source_target_pairs={{0,4},{1,5},{2,6},{3,7},{4,0},{5,1},{6,2},{7,3},{8,12},{9,13},{10,... | collective-permute-start | bytes 12296 | tf_op jit(solution)/shard_map/ppermute | solution.py:248
  47.4 2.0 %collective-permute-done.4 = f32[8,128]{1,0:T(8,128)S(1)} collective-permute-done((f32[8,128]{1,0:T(8,128)S(1)}, f32[8,128]{1,0:T(8,128)S(1)}, u32[]{:S(2)}, u32[]{:S(2)}) %collective-permute-start.4) | collective-permute-done | bytes 4128 | tf_op jit(solution)/shard_map/ppermute | solution.py:248
  49.5 0.4 collective-permute-done.1.rest_2_
  49.9 2.1 %collective-permute-done.rest_1_ = bf16[128,3072]{1,0:T(8,128)(2,1)S(1)} collective-permute-done((bf16[128,3072]{1,0:T(8,128)(2,1)}, bf16[128,3072]{1,0:T(8,128)(2,1)S(1)}, u32[]{:S(2)}, u32[]{:S(2)}) %collective-permute-start) | collective-permute-done | bytes 786464 | tf_op jit(solution)/shard_map/ppermute | solution.py:269
  52.0 0.4 collective-permute-start.9
  52.4 1.4 %collective-permute-start.8 = (f32[8,128]{1,0:T(8,128)S(1)}, f32[8,128]{1,0:T(8,128)S(1)}, u32[]{:S(2)}, u32[]{:S(2)}) collective-permute-start(f32[8,128]{1,0:T(8,128)S(1)} %max.26), channel_id=1, source_target_pairs={{0,64},{16,80},{32,96},{48,112},{64,0},{80,16},{96,32},{112,48},{1... | collective-permute-start | bytes 12296 | tf_op jit(solution)/shard_map/ppermute | solution.py:248
  53.8 2.4 %collective-permute-start.7 = (f32[8,128]{1,0:T(8,128)S(1)}, f32[8,128]{1,0:T(8,128)S(1)}, u32[]{:S(2)}, u32[]{:S(2)}) collective-permute-start(f32[8,128]{1,0:T(8,128)S(1)} %max.26), channel_id=1, source_target_pairs={{0,32},{16,48},{32,0},{48,16},{64,96},{80,112},{96,64},{112,80},{1... | collective-permute-start | bytes 12296 | tf_op jit(solution)/shard_map/ppermute | solution.py:248
  56.2 3.2 %collective-permute-start.6 = (bf16[64,3072]{1,0:T(8,128)(2,1)S(1)}, bf16[64,3072]{1,0:T(8,128)(2,1)S(1)}, u32[]{:S(2)}, u32[]{:S(2)}) collective-permute-start(bf16[64,3072]{1,0:T(8,128)(2,1)S(1)} %slice.19), channel_id=1, source_target_pairs={{0,96},{16,112},{32,0},{48,16},{64,32},{80,48},{96,64},{112,80},{1... | collective-permute-start | bytes 1179656 | tf_op jit(solution)/shard_map/ppermute | solution.py:269
  59.5 3.2 %collective-permute-start.10 = (f32[8,128]{1,0:T(8,128)S(1)}, f32[8,128]{1,0:T(8,128)S(1)}, u32[]{:S(2)}, u32[]{:S(2)}) collective-permute-start(f32[8,128]{1,0:T(8,128)S(1)} %maximum_select_fusion.1), channel_id=1, source_target_pairs={{0,8},{1,9},{2,10},{3,11},{4,12},{5,13},{6,14},{7,15},{8,0},{9,1},... | collective-permute-start | bytes 12296 | tf_op jit(solution)/shard_map/ppermute | solution.py:248
  62.8 0.5 collective-permute-start.13
  63.3 1.4 %collective-permute-done.10 = f32[8,128]{1,0:T(8,128)S(1)} collective-permute-done((f32[8,128]{1,0:T(8,128)S(1)}, f32[8,128]{1,0:T(8,128)S(1)}, u32[]{:S(2)}, u32[]{:S(2)}) %collective-permute-start.10) | collective-permute-done | bytes 4128 | tf_op jit(solution)/shard_map/ppermute | solution.py:248
  64.7 1.4 %collective-permute-done.5.rest_3_ = bf16[64,3072]{1,0:T(8,128)(2,1)S(1)} collective-permute-done((bf16[64,3072]{1,0:T(8,128)(2,1)S(1)}, bf16[64,3072]{1,0:T(8,128)(2,1)S(1)}, u32[]{:S(2)}, u32[]{:S(2)}) %collective-permute-start.5) | collective-permute-done | bytes 393248 | tf_op jit(solution)/shard_map/ppermute | solution.py:269
  66.0 0.5 collective-permute-start.15
  66.6 0.7 collective-permute-done.11
  67.3 0.1 collective-permute-start.16
  67.5 0.4 collective-permute-done.15.rest_8_
  67.9 1.1 collective-permute-done.16.rest_9_
  69.0 6.8 %projection_backward.1 = (bf16[2,128,1024]{2,1,0:T(8,128)(2,1)S(1)}, f32[1,5120]{1,0:T(1,128)S(1)}) custom-call(s32[1]{0:T(128)} %bitcast.4.place_ref, f32[8,128]{1,0:T(8,128)S(1)} %maximum_select_fusion.message_ref.bound_ref, f32[8,128]{1,0:T(8,128)S(1)} %maximum_select_fusion.message_ref.bound_ref, f32[1,3072]{1,0:T(1,128)S(1)} %bitcast.16, ...), custom_call_target="tpu_custom_call" | custom-call | flops 3221225472 | bytes 9437184 | tf_op jit(solution)/shard_map/projection_backward/pallas_call | solution.py:174
  75.9 2.9 %collective-permute-start.19 = (f32[1,5120]{1,0:T(1,128)S(1)}, f32[1,5120]{1,0:T(1,128)S(1)}, u32[]{:S(2)}, u32[]{:S(2)}) collective-permute-start(f32[1,5120]{1,0:T(1,128)S(1)} %get-tuple-element.34), channel_id=1, source_target_pairs={{0,96},{16,112},{32,64},{48,80},{64,32},{80,48},{96,0},{112,16},{1... | collective-permute-start | bytes 61448 | tf_op jit(solution)/shard_map/ppermute | solution.py:248
  78.8 1.2 %collective-permute-start.17 = (f32[1,5120]{1,0:T(1,128)S(1)}, f32[1,5120]{1,0:T(1,128)S(1)}, u32[]{:S(2)}, u32[]{:S(2)}) collective-permute-start(f32[1,5120]{1,0:T(1,128)S(1)} %get-tuple-element.34), channel_id=1, source_target_pairs={{0,32},{16,48},{32,0},{48,16},{64,96},{80,112},{96,64},{112,80},{1... | collective-permute-start | bytes 61448 | tf_op jit(solution)/shard_map/ppermute | solution.py:248
  80.0 5.2 %attend_backward.1 = bf16[8,2,3,128,128]{4,3,2,1,0:T(8,128)(2,1)} custom-call(bf16[8,2,3,128,128]{4,3,2,1,0:T(8,128)(2,1)S(1)} %all-to-all-done.y_ref, bf16[2,1024,1024]{2,1,0:T(8,128)(2,1)S(1)} %get-tuple-element.21.p_ref, bf16[2,128,1024]{2,1,0:T(8,128)(2,1)S(1)} %get-tuple-element.22.out_ref, bf16[2,128,1024]{2,1,0:T(8,128)(2,1)S(1)} %get-tuple-element.33.grad_ref), custom_call_target="tpu_custom_call" | custom-call | flops 2147483648 | bytes 8388608 | tf_op jit(solution)/shard_map/attend_backward/pallas_call | solution.py:223
  85.3 4.2 %all-to-all-start.1 = ((bf16[8,2,3,128,128]{4,3,2,1,0:T(8,128)(2,1)}), bf16[8,2,3,128,128]{4,3,2,1,0:T(8,128)(2,1)S(1)}, u32[]{:S(2)}, u32[]{:S(2)}) async-start(bf16[8,2,3,128,128]{4,3,2,1,0:T(8,128)(2,1)} %attend_backward.1), calls=%async_computation.1 | async-start | bytes 3145728 | tf_op jit(solution)/shard_map/all_to_all | solution.py:317
  89.5 1.5 %collective-permute-start.20 = (f32[1,5120]{1,0:T(1,128)S(1)}, f32[1,5120]{1,0:T(1,128)S(1)}, u32[]{:S(2)}, u32[]{:S(2)}) collective-permute-start(f32[1,5120]{1,0:T(1,128)S(1)} %add_add_fusion), channel_id=1, source_target_pairs={{0,1},{1,0},{2,3},{3,2},{4,5},{5,4},{6,7},{7,6},{8,9},{9,8},{10,11... | collective-permute-start | bytes 61448 | tf_op jit(solution)/shard_map/ppermute | solution.py:248
  91.0 2.3 %collective-permute-done.20 = f32[1,5120]{1,0:T(1,128)S(1)} collective-permute-done((f32[1,5120]{1,0:T(1,128)S(1)}, f32[1,5120]{1,0:T(1,128)S(1)}, u32[]{:S(2)}, u32[]{:S(2)}) %collective-permute-start.20) | collective-permute-done | bytes 20512 | tf_op jit(solution)/shard_map/ppermute | solution.py:248
  93.3 3.1 %collective-permute-start.21 = (f32[1,5120]{1,0:T(1,128)S(1)}, f32[1,5120]{1,0:T(1,128)S(1)}, u32[]{:S(2)}, u32[]{:S(2)}) collective-permute-start(f32[1,5120]{1,0:T(1,128)S(1)} %add.31), channel_id=1, source_target_pairs={{0,2},{1,3},{2,0},{3,1},{4,6},{5,7},{6,4},{7,5},{8,10},{9,11},{10,... | collective-permute-start | bytes 61448 | tf_op jit(solution)/shard_map/ppermute | solution.py:248
  96.4 2.3 %collective-permute-done.21 = f32[1,5120]{1,0:T(1,128)S(1)} collective-permute-done((f32[1,5120]{1,0:T(1,128)S(1)}, f32[1,5120]{1,0:T(1,128)S(1)}, u32[]{:S(2)}, u32[]{:S(2)}) %collective-permute-start.21) | collective-permute-done | bytes 20512 | tf_op jit(solution)/shard_map/ppermute | solution.py:248
  98.7 1.7 %collective-permute-start.22 = (f32[1,5120]{1,0:T(1,128)S(1)}, f32[1,5120]{1,0:T(1,128)S(1)}, u32[]{:S(2)}, u32[]{:S(2)}) collective-permute-start(f32[1,5120]{1,0:T(1,128)S(1)} %add.32), channel_id=1, source_target_pairs={{0,4},{1,5},{2,6},{3,7},{4,0},{5,1},{6,2},{7,3},{8,12},{9,13},{10,... | collective-permute-start | bytes 61448 | tf_op jit(solution)/shard_map/ppermute | solution.py:248
  100.3 2.2 %collective-permute-done.22 = f32[1,5120]{1,0:T(1,128)S(1)} collective-permute-done((f32[1,5120]{1,0:T(1,128)S(1)}, f32[1,5120]{1,0:T(1,128)S(1)}, u32[]{:S(2)}, u32[]{:S(2)}) %collective-permute-start.22) | collective-permute-done | bytes 20512 | tf_op jit(solution)/shard_map/ppermute | solution.py:248
  102.6 3.3 %collective-permute-start.23 = (f32[1,5120]{1,0:T(1,128)S(1)}, f32[1,5120]{1,0:T(1,128)S(1)}, u32[]{:S(2)}, u32[]{:S(2)}) collective-permute-start(f32[1,5120]{1,0:T(1,128)S(1)} %add.33), channel_id=1, source_target_pairs={{0,8},{1,9},{2,10},{3,11},{4,12},{5,13},{6,14},{7,15},{8,0},{9,1},... | collective-permute-start | bytes 61448 | tf_op jit(solution)/shard_map/ppermute | solution.py:248
  105.8 2.1 %collective-permute-done.23 = f32[1,5120]{1,0:T(1,128)S(1)} collective-permute-done((f32[1,5120]{1,0:T(1,128)S(1)}, f32[1,5120]{1,0:T(1,128)S(1)}, u32[]{:S(2)}, u32[]{:S(2)}) %collective-permute-start.23) | collective-permute-done | bytes 20512 | tf_op jit(solution)/shard_map/ppermute | solution.py:248
  108.0 0.1 collective-permute-start.24
  108.1 1.2 %collective-permute-done.24 = f32[1,5120]{1,0:T(1,128)S(1)} collective-permute-done((f32[1,5120]{1,0:T(1,128)S(1)}, f32[1,5120]{1,0:T(1,128)S(1)}, u32[]{:S(2)}, u32[]{:S(2)}) %collective-permute-start.24) | collective-permute-done | bytes 20512 | tf_op jit(solution)/shard_map/ppermute | solution.py:248
  109.3 0.6 slice.24
  109.9 0.6 slice.25
  110.5 0.6 all-to-all-done.1
  111.1 2.2 %copy.8 = bf16[1,3,128,16,128]{4,3,2,1,0:T(8,128)(2,1)} copy(bf16[1,3,128,16,128]{4,2,1,3,0:T(8,128)(2,1)S(1)} %bitcast.18) | data formatting | bytes 3145728
  (35 shorter events, 0.5 us)
Async XLA Ops:
  3.6 27.0 %all-to-all-start = ((bf16[8,2,3,128,128]{4,3,2,1,0:T(8,128)(2,1)}), bf16[8,2,3,128,128]{4,3,2,1,0:T(8,128)(2,1)S(1)}, u32[]{:S(2)}, u32[]{:S(2)}) async-start(bf16[8,2,3,128,128]{4,3,2,1,0:T(8,128)(2,1)} %bitcast.1), calls=%async_computation | async-start | bytes 3145728 | tf_op jit(solution)/shard_map/all_to_all | solution.py:289
  30.6 19.3 %collective-permute-start.1 = (bf16[128,3072]{1,0:T(8,128)(2,1)}, bf16[128,3072]{1,0:T(8,128)(2,1)S(1)}, u32[]{:S(2)}, u32[]{:S(2)}) collective-permute-start(bf16[128,3072]{1,0:T(8,128)(2,1)} %bitcast.12), channel_id=1, source_target_pairs={{0,96},{16,112},{32,0},{48,16},{64,32},{80,48},{96,64},{112,80},{1... | collective-permute-start | bytes 2359304 | tf_op jit(solution)/shard_map/ppermute | solution.py:269
  31.7 20.2 %collective-permute-start = (bf16[128,3072]{1,0:T(8,128)(2,1)}, bf16[128,3072]{1,0:T(8,128)(2,1)S(1)}, u32[]{:S(2)}, u32[]{:S(2)}) collective-permute-start(bf16[128,3072]{1,0:T(8,128)(2,1)} %bitcast.13), channel_id=1, source_target_pairs={{0,32},{16,48},{32,64},{48,80},{64,96},{80,112},{96,0},{112,16},{1... | collective-permute-start | bytes 2359304 | tf_op jit(solution)/shard_map/ppermute | solution.py:269
  37.1 25.7 %copy-start = (bf16[1,128,3072]{2,1,0:T(8,128)(2,1)S(1)}, bf16[1,128,3072]{2,1,0:T(8,128)(2,1)}, u32[]{:S(2)}) copy-start(bf16[1,128,3072]{2,1,0:T(8,128)(2,1)} %param.5) | copy-start | bytes 2359300
  37.1 31.9 %copy-start.1 = (f32[3072]{0:T(1024)S(1)}, f32[3072]{0:T(1024)}, u32[]{:S(2)}) copy-start(f32[3072]{0:T(1024)} %param.7) | copy-start | bytes 36868
  37.1 3.6 %collective-permute-start.2 = (f32[8,128]{1,0:T(8,128)S(1)}, f32[8,128]{1,0:T(8,128)S(1)}, u32[]{:S(2)}, u32[]{:S(2)}) collective-permute-start(f32[8,128]{1,0:T(8,128)S(1)} %get-tuple-element.24), channel_id=1, source_target_pairs={{0,1},{1,0},{2,3},{3,2},{4,5},{5,4},{6,7},{7,6},{8,9},{9,8},{10,11... | collective-permute-start | bytes 12296 | tf_op jit(solution)/shard_map/ppermute | solution.py:248
  40.7 5.1 %collective-permute-start.3 = (f32[8,128]{1,0:T(8,128)S(1)}, f32[8,128]{1,0:T(8,128)S(1)}, u32[]{:S(2)}, u32[]{:S(2)}) collective-permute-start(f32[8,128]{1,0:T(8,128)S(1)} %max.24), channel_id=1, source_target_pairs={{0,2},{1,3},{2,0},{3,1},{4,6},{5,7},{6,4},{7,5},{8,10},{9,11},{10,... | collective-permute-start | bytes 12296 | tf_op jit(solution)/shard_map/ppermute | solution.py:248
  45.9 3.6 %collective-permute-start.4 = (f32[8,128]{1,0:T(8,128)S(1)}, f32[8,128]{1,0:T(8,128)S(1)}, u32[]{:S(2)}, u32[]{:S(2)}) collective-permute-start(f32[8,128]{1,0:T(8,128)S(1)} %max.25), channel_id=1, source_target_pairs={{0,4},{1,5},{2,6},{3,7},{4,0},{5,1},{6,2},{7,3},{8,12},{9,13},{10,... | collective-permute-start | bytes 12296 | tf_op jit(solution)/shard_map/ppermute | solution.py:248
  52.0 7.4 %collective-permute-start.9 = (f32[8,128]{1,0:T(8,128)S(1)}, f32[8,128]{1,0:T(8,128)S(1)}, u32[]{:S(2)}, u32[]{:S(2)}) collective-permute-start(f32[8,128]{1,0:T(8,128)S(1)} %max.26), channel_id=1, source_target_pairs={{0,96},{16,112},{32,64},{48,80},{64,32},{80,48},{96,0},{112,16},{1... | collective-permute-start | bytes 12296 | tf_op jit(solution)/shard_map/ppermute | solution.py:248
  52.4 7.1 %collective-permute-start.8 = (f32[8,128]{1,0:T(8,128)S(1)}, f32[8,128]{1,0:T(8,128)S(1)}, u32[]{:S(2)}, u32[]{:S(2)}) collective-permute-start(f32[8,128]{1,0:T(8,128)S(1)} %max.26), channel_id=1, source_target_pairs={{0,64},{16,80},{32,96},{48,112},{64,0},{80,16},{96,32},{112,48},{1... | collective-permute-start | bytes 12296 | tf_op jit(solution)/shard_map/ppermute | solution.py:248
  53.8 5.6 %collective-permute-start.7 = (f32[8,128]{1,0:T(8,128)S(1)}, f32[8,128]{1,0:T(8,128)S(1)}, u32[]{:S(2)}, u32[]{:S(2)}) collective-permute-start(f32[8,128]{1,0:T(8,128)S(1)} %max.26), channel_id=1, source_target_pairs={{0,32},{16,48},{32,0},{48,16},{64,96},{80,112},{96,64},{112,80},{1... | collective-permute-start | bytes 12296 | tf_op jit(solution)/shard_map/ppermute | solution.py:248
  56.2 9.8 %collective-permute-start.5 = (bf16[64,3072]{1,0:T(8,128)(2,1)S(1)}, bf16[64,3072]{1,0:T(8,128)(2,1)S(1)}, u32[]{:S(2)}, u32[]{:S(2)}) collective-permute-start(bf16[64,3072]{1,0:T(8,128)(2,1)S(1)} %slice.18), channel_id=1, source_target_pairs={{0,32},{16,48},{32,64},{48,80},{64,96},{80,112},{96,0},{112,16},{1... | collective-permute-start | bytes 1179656 | tf_op jit(solution)/shard_map/ppermute | solution.py:269
  56.2 9.8 %collective-permute-start.6 = (bf16[64,3072]{1,0:T(8,128)(2,1)S(1)}, bf16[64,3072]{1,0:T(8,128)(2,1)S(1)}, u32[]{:S(2)}, u32[]{:S(2)}) collective-permute-start(bf16[64,3072]{1,0:T(8,128)(2,1)S(1)} %slice.19), channel_id=1, source_target_pairs={{0,96},{16,112},{32,0},{48,16},{64,32},{80,48},{96,64},{112,80},{1... | collective-permute-start | bytes 1179656 | tf_op jit(solution)/shard_map/ppermute | solution.py:269
  59.5 5.1 %collective-permute-start.10 = (f32[8,128]{1,0:T(8,128)S(1)}, f32[8,128]{1,0:T(8,128)S(1)}, u32[]{:S(2)}, u32[]{:S(2)}) collective-permute-start(f32[8,128]{1,0:T(8,128)S(1)} %maximum_select_fusion.1), channel_id=1, source_target_pairs={{0,8},{1,9},{2,10},{3,11},{4,12},{5,13},{6,14},{7,15},{8,0},{9,1},... | collective-permute-start | bytes 12296 | tf_op jit(solution)/shard_map/ppermute | solution.py:248
  62.8 4.8 %collective-permute-start.12 = (bf16[128,3072]{1,0:T(8,128)(2,1)S(1)}, bf16[128,3072]{1,0:T(8,128)(2,1)S(1)}, u32[]{:S(2)}, u32[]{:S(2)}) collective-permute-start(bf16[128,3072]{1,0:T(8,128)(2,1)S(1)} %bitcast.14), channel_id=1, source_target_pairs={{0,16},{16,0},{32,48},{48,32},{64,80},{80,64},{96,112},{112,96},{1... | collective-permute-start | bytes 2359304 | tf_op jit(solution)/shard_map/ppermute | solution.py:248
  62.8 6.3 %collective-permute-start.13 = (bf16[128,3072]{1,0:T(8,128)(2,1)S(1)}, bf16[128,3072]{1,0:T(8,128)(2,1)S(1)}, u32[]{:S(2)}, u32[]{:S(2)}) collective-permute-start(bf16[128,3072]{1,0:T(8,128)(2,1)S(1)} %collective-permute-done.rest_1_), channel_id=1, source_target_pairs={{0,16},{16,0},{32,48},{48,32},{64,80},{80,64},{96,112},{112,96},{1... | collective-permute-start | bytes 2359304 | tf_op jit(solution)/shard_map/ppermute | solution.py:248
  64.7 4.4 %collective-permute-start.14 = (bf16[128,3072]{1,0:T(8,128)(2,1)S(1)}, bf16[128,3072]{1,0:T(8,128)(2,1)S(1)}, u32[]{:S(2)}, u32[]{:S(2)}) collective-permute-start(bf16[128,3072]{1,0:T(8,128)(2,1)S(1)} %collective-permute-done.1.rest_2_), channel_id=1, source_target_pairs={{0,16},{16,0},{32,48},{48,32},{64,80},{80,64},{96,112},{112,96},{1... | collective-permute-start | bytes 2359304 | tf_op jit(solution)/shard_map/ppermute | solution.py:248
  66.0 1.3 %collective-permute-start.11 = (f32[8,128]{1,0:T(8,128)S(1)}, f32[8,128]{1,0:T(8,128)S(1)}, u32[]{:S(2)}, u32[]{:S(2)}) collective-permute-start(f32[8,128]{1,0:T(8,128)S(1)} %max.30), channel_id=1, source_target_pairs={{0,16},{16,0},{32,48},{48,32},{64,80},{80,64},{96,112},{112,96},{1... | collective-permute-start | bytes 12296 | tf_op jit(solution)/shard_map/ppermute | solution.py:248
  66.0 1.9 %collective-permute-start.15 = (bf16[64,3072]{1,0:T(8,128)(2,1)S(1)}, bf16[64,3072]{1,0:T(8,128)(2,1)S(1)}, u32[]{:S(2)}, u32[]{:S(2)}) collective-permute-start(bf16[64,3072]{1,0:T(8,128)(2,1)S(1)} %collective-permute-done.5.rest_3_), channel_id=1, source_target_pairs={{0,16},{16,0},{32,48},{48,32},{64,80},{80,64},{96,112},{112,96},{1... | collective-permute-start | bytes 1179656 | tf_op jit(solution)/shard_map/ppermute | solution.py:248
  67.3 1.7 %collective-permute-start.16 = (bf16[64,3072]{1,0:T(8,128)(2,1)S(1)}, bf16[64,3072]{1,0:T(8,128)(2,1)S(1)}, u32[]{:S(2)}, u32[]{:S(2)}) collective-permute-start(bf16[64,3072]{1,0:T(8,128)(2,1)S(1)} %collective-permute-done.6.rest_4_), channel_id=1, source_target_pairs={{0,16},{16,0},{32,48},{48,32},{64,80},{80,64},{96,112},{112,96},{1... | collective-permute-start | bytes 1179656 | tf_op jit(solution)/shard_map/ppermute | solution.py:248
  75.9 9.4 %collective-permute-start.19 = (f32[1,5120]{1,0:T(1,128)S(1)}, f32[1,5120]{1,0:T(1,128)S(1)}, u32[]{:S(2)}, u32[]{:S(2)}) collective-permute-start(f32[1,5120]{1,0:T(1,128)S(1)} %get-tuple-element.34), channel_id=1, source_target_pairs={{0,96},{16,112},{32,64},{48,80},{64,32},{80,48},{96,0},{112,16},{1... | collective-permute-start | bytes 61448 | tf_op jit(solution)/shard_map/ppermute | solution.py:248
  78.8 6.5 %collective-permute-start.18 = (f32[1,5120]{1,0:T(1,128)S(1)}, f32[1,5120]{1,0:T(1,128)S(1)}, u32[]{:S(2)}, u32[]{:S(2)}) collective-permute-start(f32[1,5120]{1,0:T(1,128)S(1)} %get-tuple-element.34), channel_id=1, source_target_pairs={{0,64},{16,80},{32,96},{48,112},{64,0},{80,16},{96,32},{112,48},{1... | collective-permute-start | bytes 61448 | tf_op jit(solution)/shard_map/ppermute | solution.py:248
  78.8 6.5 %collective-permute-start.17 = (f32[1,5120]{1,0:T(1,128)S(1)}, f32[1,5120]{1,0:T(1,128)S(1)}, u32[]{:S(2)}, u32[]{:S(2)}) collective-permute-start(f32[1,5120]{1,0:T(1,128)S(1)} %get-tuple-element.34), channel_id=1, source_target_pairs={{0,32},{16,48},{32,0},{48,16},{64,96},{80,112},{96,64},{112,80},{1... | collective-permute-start | bytes 61448 | tf_op jit(solution)/shard_map/ppermute | solution.py:248
  85.3 25.7 %all-to-all-start.1 = ((bf16[8,2,3,128,128]{4,3,2,1,0:T(8,128)(2,1)}), bf16[8,2,3,128,128]{4,3,2,1,0:T(8,128)(2,1)S(1)}, u32[]{:S(2)}, u32[]{:S(2)}) async-start(bf16[8,2,3,128,128]{4,3,2,1,0:T(8,128)(2,1)} %attend_backward.1), calls=%async_computation.1 | async-start | bytes 3145728 | tf_op jit(solution)/shard_map/all_to_all | solution.py:317
  89.5 3.8 %collective-permute-start.20 = (f32[1,5120]{1,0:T(1,128)S(1)}, f32[1,5120]{1,0:T(1,128)S(1)}, u32[]{:S(2)}, u32[]{:S(2)}) collective-permute-start(f32[1,5120]{1,0:T(1,128)S(1)} %add_add_fusion), channel_id=1, source_target_pairs={{0,1},{1,0},{2,3},{3,2},{4,5},{5,4},{6,7},{7,6},{8,9},{9,8},{10,11... | collective-permute-start | bytes 61448 | tf_op jit(solution)/shard_map/ppermute | solution.py:248
  93.3 5.4 %collective-permute-start.21 = (f32[1,5120]{1,0:T(1,128)S(1)}, f32[1,5120]{1,0:T(1,128)S(1)}, u32[]{:S(2)}, u32[]{:S(2)}) collective-permute-start(f32[1,5120]{1,0:T(1,128)S(1)} %add.31), channel_id=1, source_target_pairs={{0,2},{1,3},{2,0},{3,1},{4,6},{5,7},{6,4},{7,5},{8,10},{9,11},{10,... | collective-permute-start | bytes 61448 | tf_op jit(solution)/shard_map/ppermute | solution.py:248
  98.7 3.9 %collective-permute-start.22 = (f32[1,5120]{1,0:T(1,128)S(1)}, f32[1,5120]{1,0:T(1,128)S(1)}, u32[]{:S(2)}, u32[]{:S(2)}) collective-permute-start(f32[1,5120]{1,0:T(1,128)S(1)} %add.32), channel_id=1, source_target_pairs={{0,4},{1,5},{2,6},{3,7},{4,0},{5,1},{6,2},{7,3},{8,12},{9,13},{10,... | collective-permute-start | bytes 61448 | tf_op jit(solution)/shard_map/ppermute | solution.py:248
  102.6 5.4 %collective-permute-start.23 = (f32[1,5120]{1,0:T(1,128)S(1)}, f32[1,5120]{1,0:T(1,128)S(1)}, u32[]{:S(2)}, u32[]{:S(2)}) collective-permute-start(f32[1,5120]{1,0:T(1,128)S(1)} %add.33), channel_id=1, source_target_pairs={{0,8},{1,9},{2,10},{3,11},{4,12},{5,13},{6,14},{7,15},{8,0},{9,1},... | collective-permute-start | bytes 61448 | tf_op jit(solution)/shard_map/ppermute | solution.py:248
  108.0 1.3 %collective-permute-start.24 = (f32[1,5120]{1,0:T(1,128)S(1)}, f32[1,5120]{1,0:T(1,128)S(1)}, u32[]{:S(2)}, u32[]{:S(2)}) collective-permute-start(f32[1,5120]{1,0:T(1,128)S(1)} %add.34), channel_id=1, source_target_pairs={{0,16},{16,0},{32,48},{48,32},{64,80},{80,64},{96,112},{112,96},{1... | collective-permute-start | bytes 61448 | tf_op jit(solution)/shard_map/ppermute | solution.py:248

commit v5 on v4

--- a/solution.py
+++ b/solution.py
@@ -43,51 +43,43 @@
 
 
 def forward_kernel(y_ref, weight_max_ref, p_ref, out_ref, message_ref):
-    keys = y_ref[:, 0, 1].reshape(LEN, HEAD_DIM)
-    values = y_ref[:, 0, 2].reshape(LEN, HEAD_DIM)
-    queries = y_ref[:, 0, 0].reshape(LEN, HEAD_DIM)
-    scores = dot(keys, queries, NT)
-    row_top = jnp.max(scores, axis=0, keepdims=True)
-    exponent = jnp.exp2((scores - row_top) * EXP2_SCALE)
-    total = jnp.sum(exponent, axis=0, keepdims=True)
-    weights = (exponent * (1.0 / total)).astype(jnp.bfloat16)
-    p_ref[0] = weights
-    mixed = dot(values, weights, TN).astype(jnp.bfloat16)
-    out_ref[0] = mixed
-    top = jnp.max(jnp.abs(mixed.astype(jnp.float32)), axis=1, keepdims=True)
-    act_row = to_row(top)
-    bound = jnp.max(
-        jnp.sqrt((act_row + epsilon) * (weight_max_ref[0] + epsilon)), axis=1, keepdims=True
-    )
-    head = pl.program_id(0)
-
-    @pl.when(head == 0)
-    def _():
-        message_ref[...] = jnp.zeros_like(message_ref)
-
-    message_ref[pl.ds(head, 1)] = act_row
-    message_ref[2:3] = jnp.maximum(message_ref[2:3], bound)
+    scores = []
+    for head in range(LOCAL_HEADS):
+        queries = y_ref[:, head, 0].reshape(LEN, HEAD_DIM)
+        keys = y_ref[:, head, 1].reshape(LEN, HEAD_DIM)
+        scores.append(dot(keys, queries, NT))
+    message_ref[...] = jnp.zeros_like(message_ref)
+    for head in range(LOCAL_HEADS):
+        row_top = jnp.max(scores[head], axis=0, keepdims=True)
+        exponent = jnp.exp2((scores[head] - row_top) * EXP2_SCALE)
+        total = jnp.sum(exponent, axis=0, keepdims=True)
+        weights = (exponent * (1.0 / total)).astype(jnp.bfloat16)
+        p_ref[head] = weights
+        values = y_ref[:, head, 2].reshape(LEN, HEAD_DIM)
+        mixed = dot(values, weights, TN).astype(jnp.bfloat16)
+        out_ref[head] = mixed
+        act_row = to_row(jnp.max(jnp.abs(mixed.astype(jnp.float32)), axis=1, keepdims=True))
+        bound = jnp.max(
+            jnp.sqrt((act_row + epsilon) * (weight_max_ref[head] + epsilon)),
+            axis=1,
+            keepdims=True,
+        )
+        message_ref[head : head + 1] = act_row
+        message_ref[2:3] = jnp.maximum(message_ref[2:3], bound)
 
 
 def forward(heads, weight_max):
+    vmem = pl.BlockSpec(memory_space=pltpu.VMEM)
     return pl.pallas_call(
         forward_kernel,
-        grid=(LOCAL_HEADS,),
-        in_specs=[
-            pl.BlockSpec((SEQ, 1, 3, TOKENS, HEAD_DIM), lambda h: (0, h, 0, 0, 0)),
-            pl.BlockSpec((1, 1, 128), lambda h: (h, 0, 0)),
-        ],
-        out_specs=[
-            pl.BlockSpec((1, LEN, LEN), lambda h: (h, 0, 0)),
-            pl.BlockSpec((1, HEAD_DIM, LEN), lambda h: (h, 0, 0)),
-            pl.BlockSpec((8, 128), lambda h: (0, 0)),
-        ],
+        in_specs=[vmem] * 2,
+        out_specs=[vmem] * 3,
         out_shape=[
             jax.ShapeDtypeStruct((LOCAL_HEADS, LEN, LEN), jnp.bfloat16),
             jax.ShapeDtypeStruct((LOCAL_HEADS, HEAD_DIM, LEN), jnp.bfloat16),
             jax.ShapeDtypeStruct((8, 128), jnp.float32),
         ],
-        compiler_params=pltpu.CompilerParams(vmem_limit_bytes=VMEM_LIMIT),
+        compiler_params=pltpu.CompilerParams(vmem_limit_bytes=28 * MIB),
         cost_estimate=pl.CostEstimate(
             flops=2 * 2 * LOCAL_HEADS * LEN * LEN * HEAD_DIM,
             bytes_accessed=6 * MIB,
@@ -103,21 +95,16 @@
 
 def projection_kernel(place_ref, message_ref, bound_ref, clip_ref, out_ref, own_ref, *rest):
     pieces = rest[:10]
-    grad_ref, vec_ref, cot_ref, wq_ref, tanh_ref, quant_ref, sem = rest[10:]
+    grad_ref, vec_ref, cot_ref, wq_ref, tanh_ref, quant_ref = rest[10:]
     place = place_ref[0]
     depth = place // 2
     core = place % 2
-    copies = []
     for k, piece in enumerate(pieces):
         kind, sibling = k % 5, k // 5
         rows = TOKENS if kind < 3 else HALF
         source = (depth + (0, 3, 1, 2, 2)[kind]) % 4
         first = (source * 2 + (core + sibling) % 2) * TOKENS + (HALF if kind == 4 else 0)
-        copy = pltpu.make_async_copy(
-            piece, cot_ref.at[pl.ds(pl.multiple_of(first, HALF), rows)], sem.at[k]
-        )
-        copy.start()
-        copies.append(copy)
+        cot_ref[pl.ds(pl.multiple_of(first, HALF), rows)] = piece[...]
     act_clip = act_fraction * bound_ref[2:3, 0:1]
     act_column = jnp.concatenate(
         [to_column(message_ref[0:1]), to_column(message_ref[1:2])], axis=0
@@ -137,8 +124,6 @@
         wq_ref[:, columns] = (clip * tanh).astype(jnp.bfloat16)
     inverse = 1.0 / smooth
     inner = inverse / act_clip
-    for copy in copies:
-        copy.wait()
     act_part = None
     for t in range(NUM_BLOCKS):
         tokens = slice(t * BLOCK, (t + 1) * BLOCK)
@@ -170,10 +155,9 @@
 
 def projection(place, message, bound, clip, out, own_rows, pieces):
     vmem = pl.BlockSpec(memory_space=pltpu.VMEM)
-    hbm = pl.BlockSpec(memory_space=pl.ANY)
     return pl.pallas_call(
         projection_kernel,
-        in_specs=[pl.BlockSpec(memory_space=pltpu.SMEM), vmem, vmem, vmem, vmem, vmem] + [hbm] * 10,
+        in_specs=[pl.BlockSpec(memory_space=pltpu.SMEM), vmem, vmem, vmem, vmem, vmem]+ [vmem] * 10,
         out_specs=[vmem, vmem],
         out_shape=[
             jax.ShapeDtypeStruct((LOCAL_HEADS, HEAD_DIM, LEN), jnp.bfloat16),
@@ -184,7 +168,6 @@
             pltpu.VMEM((CHANNELS, D), jnp.bfloat16),
             pltpu.VMEM((CHANNELS, D), jnp.float32),
             pltpu.VMEM((CHANNELS, LEN), jnp.bfloat16),
-            pltpu.SemaphoreType.DMA((10,)),
         ],
         compiler_params=pltpu.CompilerParams(vmem_limit_bytes=VMEM_LIMIT),
         cost_estimate=pl.CostEstimate(
@@ -196,45 +179,60 @@
     )(place, message, bound, clip, out, own_rows, *pieces)
 
 
-def backward_kernel(y_ref, p_ref, out_ref, grad_ref, z_ref, ds_ref):
-    keys = y_ref[:, 0, 1].reshape(LEN, HEAD_DIM)
-    values = y_ref[:, 0, 2].reshape(LEN, HEAD_DIM)
-    for b in range(LEN // WIDTH):
-        columns = pl.ds(b * WIDTH, WIDTH)
-        grad_out = grad_ref[0, :, columns]
-        delta = jnp.sum(
-            grad_out.astype(jnp.float32) * out_ref[0, :, columns].astype(jnp.float32),
-            axis=0,
-            keepdims=True,
+def backward_kernel(y_ref, p_ref, out_ref, grad_ref, result_ref, z_ref, ds_ref, sem):
+    copies = []
+
+    def send(head, which):
+        copy = pltpu.make_async_copy(
+            z_ref.at[:, head, which], result_ref.at[:, head, which], sem.at[head, which]
         )
-        grad_weights = dot(values, grad_out, NN)
-        weights = p_ref[0, :, columns].astype(jnp.float32)
-        ds_ref[:, columns] = (weights * (grad_weights - delta)).astype(jnp.bfloat16)
-    queries = y_ref[:, 0, 0].reshape(LEN, HEAD_DIM)
-    grad_query = (dot(keys, ds_ref[...], TN) * SCALE).astype(jnp.bfloat16)
-    z_ref[:, 0, 0] = grad_query.T.reshape(SEQ, TOKENS, HEAD_DIM)
-    grad_value = dot(p_ref[0], grad_ref[0], NT)
-    z_ref[:, 0, 2] = grad_value.astype(jnp.bfloat16).reshape(SEQ, TOKENS, HEAD_DIM)
-    grad_key = dot(ds_ref[...], queries, NN) * SCALE
-    z_ref[:, 0, 1] = grad_key.astype(jnp.bfloat16).reshape(SEQ, TOKENS, HEAD_DIM)
+        copy.start()
+        copies.append(copy)
+
+    for head in range(LOCAL_HEADS):
+        values = y_ref[:, head, 2].reshape(LEN, HEAD_DIM)
+        grad_value = dot(p_ref[head], grad_ref[head], NT)
+        z_ref[:, head, 2] = grad_value.astype(jnp.bfloat16).reshape(SEQ, TOKENS, HEAD_DIM)
+        send(head, 2)
+        for b in range(LEN // WIDTH):
+            columns = pl.ds(b * WIDTH, WIDTH)
+            grad_out = grad_ref[head, :, columns]
+            delta = jnp.sum(
+                grad_out.astype(jnp.float32) * out_ref[head, :, columns].astype(jnp.float32),
+                axis=0,
+                keepdims=True,
+            )
+            grad_weights = dot(values, grad_out, NN)
+            weights = p_ref[head, :, columns].astype(jnp.float32)
+            ds_ref[head, :, columns] = (weights * (grad_weights - delta)).astype(jnp.bfloat16)
+    for head in range(LOCAL_HEADS):
+        queries = y_ref[:, head, 0].reshape(LEN, HEAD_DIM)
+        keys = y_ref[:, head, 1].reshape(LEN, HEAD_DIM)
+        grad_query = (dot(keys, ds_ref[head], TN) * SCALE).astype(jnp.bfloat16)
+        z_ref[:, head, 0] = grad_query.T.reshape(SEQ, TOKENS, HEAD_DIM)
+        send(head, 0)
+        grad_key = dot(ds_ref[head], queries, NN) * SCALE
+        z_ref[:, head, 1] = grad_key.astype(jnp.bfloat16).reshape(SEQ, TOKENS, HEAD_DIM)
+        send(head, 1)
+    for copy in copies:
+        copy.wait()
 
 
 def backward(heads, weights, out, grad_out):
+    vmem = pl.BlockSpec(memory_space=pltpu.VMEM)
     return pl.pallas_call(
         backward_kernel,
-        grid=(LOCAL_HEADS,),
-        in_specs=[
-            pl.BlockSpec((SEQ, 1, 3, TOKENS, HEAD_DIM), lambda h: (0, h, 0, 0, 0)),
-            pl.BlockSpec((1, LEN, LEN), lambda h: (h, 0, 0)),
-            pl.BlockSpec((1, HEAD_DIM, LEN), lambda h: (h, 0, 0)),
-            pl.BlockSpec((1, HEAD_DIM, LEN), lambda h: (h, 0, 0)),
-        ],
-        out_specs=pl.BlockSpec((SEQ, 1, 3, TOKENS, HEAD_DIM), lambda h: (0, h, 0, 0, 0)),
+        in_specs=[vmem] * 4,
+        out_specs=pl.BlockSpec(memory_space=pl.ANY),
         out_shape=jax.ShapeDtypeStruct(
             (SEQ, LOCAL_HEADS, 3, TOKENS, HEAD_DIM), jnp.bfloat16
         ),
-        scratch_shapes=[pltpu.VMEM((LEN, LEN), jnp.bfloat16)],
-        compiler_params=pltpu.CompilerParams(vmem_limit_bytes=VMEM_LIMIT),
+        scratch_shapes=[
+            pltpu.VMEM((SEQ, LOCAL_HEADS, 3, TOKENS, HEAD_DIM), jnp.bfloat16),
+            pltpu.VMEM((LOCAL_HEADS, LEN, LEN), jnp.bfloat16),
+            pltpu.SemaphoreType.DMA((LOCAL_HEADS, 3)),
+        ],
+        compiler_params=pltpu.CompilerParams(vmem_limit_bytes=28 * MIB),
         cost_estimate=pl.CostEstimate(
             flops=4 * 2 * LOCAL_HEADS * LEN * LEN * HEAD_DIM,
             bytes_accessed=8 * MIB,

time: 114 us -> 112 us (0.982)
  Pallas kernels: 16.5 us -> 13.6 us
    pallas_call x1, Pallas kernels: 6.82 us -> 5.09 us  [projection(): pl.pallas_call(projection_kernel, in_specs=[pl.BlockSpec(memory_space=plt...]
    pallas_call x2, Pallas kernels: 9.73 us -> 8.49 us  [the longest x1 5.03 us: backward(): pl.pallas_call(backward_kernel, in_specs=[vmem] * 4, out_specs=pl.BlockSp...]
  transfers between devices with their start and end apart: 27 -> 27, of which waited for: 17 -> 17; matrix products, arithmetic and copies ran while one was open for 3% -> 3% of each run, Pallas kernels for 9% -> 8%
where the time goes in v5:
time: 112 us; the launch traced here: 111 us
  waiting for transfers between devices  45.1 us (40%)
  starting transfers between devices  43.3 us (39%)
  Pallas kernels  13.6 us (12%)
  local copies, waits for them, and re-layouts  7.89 us (7%)
    ppermute x21, starting transfers between devices, exchange(): return lax.ppermute(tensor, axis, [(i, i ^ bits) for i in range(size)])  28.4 us
    ppermute x21, waiting for transfers between devices, exchange(): return lax.ppermute(tensor, axis, [(i, i ^ bits) for i in range(size)])  19.9 us
    all_to_all x1, waiting for transfers between devices, per_device(): heads = lax.all_to_all(send, 'seq', split_axis=0, concat_axis=0, tiled=True)  19.7 us
    all_to_all x1, starting transfers between devices, per_device(): heads = lax.all_to_all(send, 'seq', split_axis=0, concat_axis=0, tiled=True)  5.4 us
    ppermute x4, starting transfers between devices, shift_depth(): lax.ppermute(tensor, 'seq', [(i, (i + 2 * steps) % SEQ) for i in range(SE...  5.26 us
    unnamed x6, local copies, waits for them, and re-layouts  5.12 us
    pallas_call x1, Pallas kernels, projection(): pl.pallas_call(projection_kernel, in_specs=[pl.BlockSpec(memory_space=plt...  5.09 us
    pallas_call x1, Pallas kernels, backward(): pl.pallas_call(backward_kernel, in_specs=[vmem] * 4, out_specs=pl.BlockSp...  5.03 us
  transfers between devices with their start and end apart: 27, of which 17 were waited for; matrix products, arithmetic and copies ran while one was open for 3% of the time, Pallas kernels for 8%

profile of v5, /device:TPU:0, one launch (start us, length us, event | category | flops | bytes accessed | tf_op | source)
XLA Modules:
  0.0 111.3 jit_solution(10072233565750067710)
XLA Ops:
  0.6 3.0 %copy.7 = bf16[1,3,128,16,128]{4,2,1,3,0:T(8,128)(2,1)} copy(bf16[1,3,128,16,128]{4,3,2,1,0:T(8,128)(2,1)} %param.4) | data formatting | bytes 3145728 | tf_op args[0]
  3.6 5.4 %all-to-all-start = ((bf16[8,2,3,128,128]{4,3,2,1,0:T(8,128)(2,1)}), bf16[8,2,3,128,128]{4,3,2,1,0:T(8,128)(2,1)S(1)}, u32[]{:S(2)}, u32[]{:S(2)}) async-start(bf16[8,2,3,128,128]{4,3,2,1,0:T(8,128)(2,1)} %bitcast.1), calls=%async_computation | async-start | bytes 3145728 | tf_op jit(solution)/shard_map/all_to_all | solution.py:287
  9.0 1.5 %constant_dynamic-slice_fusion.own_ref = bf16[256,3072]{1,0:T(8,128)(2,1)S(1)} fusion(bf16[2048,3072]{1,0:T(8,128)(2,1)} %param.6, s32[]{:T(128)S(6)} %select_n.10), kind=kLoop, calls=%fused_computation.5 | loop fusion | bytes 3145732 | tf_op jit(solution)/shard_map/dynamic_slice | solution.py:284
  10.5 0.4 abs_reduce_fusion
  10.9 19.7 %all-to-all-done.y_ref = bf16[8,2,3,128,128]{4,3,2,1,0:T(8,128)(2,1)S(1)} async-done(((bf16[8,2,3,128,128]{4,3,2,1,0:T(8,128)(2,1)}), bf16[8,2,3,128,128]{4,3,2,1,0:T(8,128)(2,1)S(1)}, u32[]{:S(2)}, u32[]{:S(2)}) %all-to-all-start) | async-done | bytes 1572896 | tf_op jit(solution)/shard_map/all_to_all | solution.py:287
  30.6 1.2 %collective-permute-start.1 = (bf16[128,3072]{1,0:T(8,128)(2,1)}, bf16[128,3072]{1,0:T(8,128)(2,1)S(1)}, u32[]{:S(2)}, u32[]{:S(2)}) collective-permute-start(bf16[128,3072]{1,0:T(8,128)(2,1)} %bitcast.12), channel_id=1, source_target_pairs={{0,96},{16,112},{32,0},{48,16},{64,32},{80,48},{96,64},{112,80},{1... | collective-permute-start | bytes 2359304 | tf_op jit(solution)/shard_map/ppermute | solution.py:267
  31.7 0.9 collective-permute-start
  32.6 3.5 %attend_forward.1 = (bf16[2,1024,1024]{2,1,0:T(8,128)(2,1)S(1)}, bf16[2,128,1024]{2,1,0:T(8,128)(2,1)S(1)}, f32[8,128]{1,0:T(8,128)S(1)}) custom-call(bf16[8,2,3,128,128]{4,3,2,1,0:T(8,128)(2,1)S(1)} %all-to-all-done.y_ref, f32[2,1,128]{2,1,0:T(1,128)S(1)} %bitcast.17), custom_call_target="tpu_custom_call" | custom-call | flops 1073741824 | bytes 6291456 | tf_op jit(solution)/shard_map/attend_forward/pallas_call | solution.py:73
  36.1 1.5 %collective-permute-start.2 = (f32[8,128]{1,0:T(8,128)S(1)}, f32[8,128]{1,0:T(8,128)S(1)}, u32[]{:S(2)}, u32[]{:S(2)}) collective-permute-start(f32[8,128]{1,0:T(8,128)S(1)} %get-tuple-element.24), channel_id=1, source_target_pairs={{0,1},{1,0},{2,3},{3,2},{4,5},{5,4},{6,7},{7,6},{8,9},{9,8},{10,11... | collective-permute-start | bytes 12296 | tf_op jit(solution)/shard_map/ppermute | solution.py:246
  37.6 2.1 %collective-permute-done.2 = f32[8,128]{1,0:T(8,128)S(1)} collective-permute-done((f32[8,128]{1,0:T(8,128)S(1)}, f32[8,128]{1,0:T(8,128)S(1)}, u32[]{:S(2)}, u32[]{:S(2)}) %collective-permute-start.2) | collective-permute-done | bytes 4128 | tf_op jit(solution)/shard_map/ppermute | solution.py:246
  39.7 3.0 %collective-permute-start.3 = (f32[8,128]{1,0:T(8,128)S(1)}, f32[8,128]{1,0:T(8,128)S(1)}, u32[]{:S(2)}, u32[]{:S(2)}) collective-permute-start(f32[8,128]{1,0:T(8,128)S(1)} %max.24), channel_id=1, source_target_pairs={{0,2},{1,3},{2,0},{3,1},{4,6},{5,7},{6,4},{7,5},{8,10},{9,11},{10,... | collective-permute-start | bytes 12296 | tf_op jit(solution)/shard_map/ppermute | solution.py:246
  42.8 2.1 %collective-permute-done.3 = f32[8,128]{1,0:T(8,128)S(1)} collective-permute-done((f32[8,128]{1,0:T(8,128)S(1)}, f32[8,128]{1,0:T(8,128)S(1)}, u32[]{:S(2)}, u32[]{:S(2)}) %collective-permute-start.3) | collective-permute-done | bytes 4128 | tf_op jit(solution)/shard_map/ppermute | solution.py:246
  44.8 1.6 %collective-permute-start.4 = (f32[8,128]{1,0:T(8,128)S(1)}, f32[8,128]{1,0:T(8,128)S(1)}, u32[]{:S(2)}, u32[]{:S(2)}) collective-permute-start(f32[8,128]{1,0:T(8,128)S(1)} %max.25), channel_id=1, source_target_pairs={{0,4},{1,5},{2,6},{3,7},{4,0},{5,1},{6,2},{7,3},{8,12},{9,13},{10,... | collective-permute-start | bytes 12296 | tf_op jit(solution)/shard_map/ppermute | solution.py:246
  46.4 2.0 %collective-permute-done.4 = f32[8,128]{1,0:T(8,128)S(1)} collective-permute-done((f32[8,128]{1,0:T(8,128)S(1)}, f32[8,128]{1,0:T(8,128)S(1)}, u32[]{:S(2)}, u32[]{:S(2)}) %collective-permute-start.4) | collective-permute-done | bytes 4128 | tf_op jit(solution)/shard_map/ppermute | solution.py:246
  48.5 1.4 %collective-permute-done.1.rest_2_ = bf16[128,3072]{1,0:T(8,128)(2,1)S(1)} collective-permute-done((bf16[128,3072]{1,0:T(8,128)(2,1)}, bf16[128,3072]{1,0:T(8,128)(2,1)S(1)}, u32[]{:S(2)}, u32[]{:S(2)}) %collective-permute-start.1) | collective-permute-done | bytes 786464 | tf_op jit(solution)/shard_map/ppermute | solution.py:267
  49.9 2.1 %collective-permute-done.rest_1_ = bf16[128,3072]{1,0:T(8,128)(2,1)S(1)} collective-permute-done((bf16[128,3072]{1,0:T(8,128)(2,1)}, bf16[128,3072]{1,0:T(8,128)(2,1)S(1)}, u32[]{:S(2)}, u32[]{:S(2)}) %collective-permute-start) | collective-permute-done | bytes 786464 | tf_op jit(solution)/shard_map/ppermute | solution.py:267
  52.0 0.4 collective-permute-start.9
  52.4 1.4 %collective-permute-start.8 = (f32[8,128]{1,0:T(8,128)S(1)}, f32[8,128]{1,0:T(8,128)S(1)}, u32[]{:S(2)}, u32[]{:S(2)}) collective-permute-start(f32[8,128]{1,0:T(8,128)S(1)} %max.26), channel_id=1, source_target_pairs={{0,64},{16,80},{32,96},{48,112},{64,0},{80,16},{96,32},{112,48},{1... | collective-permute-start | bytes 12296 | tf_op jit(solution)/shard_map/ppermute | solution.py:246
  53.8 2.4 %collective-permute-start.7 = (f32[8,128]{1,0:T(8,128)S(1)}, f32[8,128]{1,0:T(8,128)S(1)}, u32[]{:S(2)}, u32[]{:S(2)}) collective-permute-start(f32[8,128]{1,0:T(8,128)S(1)} %max.26), channel_id=1, source_target_pairs={{0,32},{16,48},{32,0},{48,16},{64,96},{80,112},{96,64},{112,80},{1... | collective-permute-start | bytes 12296 | tf_op jit(solution)/shard_map/ppermute | solution.py:246
  56.2 3.2 %collective-permute-start.6 = (bf16[64,3072]{1,0:T(8,128)(2,1)S(1)}, bf16[64,3072]{1,0:T(8,128)(2,1)S(1)}, u32[]{:S(2)}, u32[]{:S(2)}) collective-permute-start(bf16[64,3072]{1,0:T(8,128)(2,1)S(1)} %slice.19), channel_id=1, source_target_pairs={{0,96},{16,112},{32,0},{48,16},{64,32},{80,48},{96,64},{112,80},{1... | collective-permute-start | bytes 1179656 | tf_op jit(solution)/shard_map/ppermute | solution.py:267
  59.5 3.2 %collective-permute-start.10 = (f32[8,128]{1,0:T(8,128)S(1)}, f32[8,128]{1,0:T(8,128)S(1)}, u32[]{:S(2)}, u32[]{:S(2)}) collective-permute-start(f32[8,128]{1,0:T(8,128)S(1)} %maximum_select_fusion.1), channel_id=1, source_target_pairs={{0,8},{1,9},{2,10},{3,11},{4,12},{5,13},{6,14},{7,15},{8,0},{9,1},... | collective-permute-start | bytes 12296 | tf_op jit(solution)/shard_map/ppermute | solution.py:246
  62.8 0.5 collective-permute-start.13
  63.3 1.4 %collective-permute-done.10 = f32[8,128]{1,0:T(8,128)S(1)} collective-permute-done((f32[8,128]{1,0:T(8,128)S(1)}, f32[8,128]{1,0:T(8,128)S(1)}, u32[]{:S(2)}, u32[]{:S(2)}) %collective-permute-start.10) | collective-permute-done | bytes 4128 | tf_op jit(solution)/shard_map/ppermute | solution.py:246
  64.7 1.4 %collective-permute-done.5.rest_3_ = bf16[64,3072]{1,0:T(8,128)(2,1)S(1)} collective-permute-done((bf16[64,3072]{1,0:T(8,128)(2,1)S(1)}, bf16[64,3072]{1,0:T(8,128)(2,1)S(1)}, u32[]{:S(2)}, u32[]{:S(2)}) %collective-permute-start.5) | collective-permute-done | bytes 393248 | tf_op jit(solution)/shard_map/ppermute | solution.py:267
  66.0 0.5 collective-permute-start.15
  66.6 0.7 collective-permute-done.11
  67.3 0.1 collective-permute-start.16
  67.5 0.4 collective-permute-done.15.rest_8_
  67.9 1.1 %collective-permute-done.16.rest_9_ = bf16[64,3072]{1,0:T(8,128)(2,1)S(1)} collective-permute-done((bf16[64,3072]{1,0:T(8,128)(2,1)S(1)}, bf16[64,3072]{1,0:T(8,128)(2,1)S(1)}, u32[]{:S(2)}, u32[]{:S(2)}) %collective-permute-start.16) | collective-permute-done | bytes 393248 | tf_op jit(solution)/shard_map/ppermute | solution.py:246
  69.0 5.1 %projection_backward.1 = (bf16[2,128,1024]{2,1,0:T(8,128)(2,1)S(1)}, f32[1,5120]{1,0:T(1,128)S(1)}) custom-call(s32[1]{0:T(128)} %bitcast.4.place_ref, f32[8,128]{1,0:T(8,128)S(1)} %maximum_select_fusion.message_ref.bound_ref, f32[8,128]{1,0:T(8,128)S(1)} %maximum_select_fusion.message_ref.bound_ref, f32[1,3072]{1,0:T(1,128)S(1)} %bitcast.16, ...), custom_call_target="tpu_custom_call" | custom-call | flops 3221225472 | bytes 9437184 | tf_op jit(solution)/shard_map/projection_backward/pallas_call | solution.py:158
  74.1 2.9 %collective-permute-start.19 = (f32[1,5120]{1,0:T(1,128)S(1)}, f32[1,5120]{1,0:T(1,128)S(1)}, u32[]{:S(2)}, u32[]{:S(2)}) collective-permute-start(f32[1,5120]{1,0:T(1,128)S(1)} %get-tuple-element.34), channel_id=1, source_target_pairs={{0,96},{16,112},{32,64},{48,80},{64,32},{80,48},{96,0},{112,16},{1... | collective-permute-start | bytes 61448 | tf_op jit(solution)/shard_map/ppermute | solution.py:246
  77.0 1.2 %collective-permute-start.17 = (f32[1,5120]{1,0:T(1,128)S(1)}, f32[1,5120]{1,0:T(1,128)S(1)}, u32[]{:S(2)}, u32[]{:S(2)}) collective-permute-start(f32[1,5120]{1,0:T(1,128)S(1)} %get-tuple-element.34), channel_id=1, source_target_pairs={{0,32},{16,48},{32,0},{48,16},{64,96},{80,112},{96,64},{112,80},{1... | collective-permute-start | bytes 61448 | tf_op jit(solution)/shard_map/ppermute | solution.py:246
  78.3 5.0 %attend_backward.1 = bf16[8,2,3,128,128]{4,3,2,1,0:T(8,128)(2,1)} custom-call(bf16[8,2,3,128,128]{4,3,2,1,0:T(8,128)(2,1)S(1)} %all-to-all-done.y_ref, bf16[2,1024,1024]{2,1,0:T(8,128)(2,1)S(1)} %get-tuple-element.21.p_ref, bf16[2,128,1024]{2,1,0:T(8,128)(2,1)S(1)} %get-tuple-element.22.out_ref, bf16[2,128,1024]{2,1,0:T(8,128)(2,1)S(1)} %get-tuple-element.33.grad_ref), custom_call_target="tpu_custom_call" | custom-call | flops 2147483648 | bytes 8388608 | tf_op jit(solution)/shard_map/attend_backward/pallas_call | solution.py:223
  83.4 4.2 %all-to-all-start.1 = ((bf16[8,2,3,128,128]{4,3,2,1,0:T(8,128)(2,1)}), bf16[8,2,3,128,128]{4,3,2,1,0:T(8,128)(2,1)S(1)}, u32[]{:S(2)}, u32[]{:S(2)}) async-start(bf16[8,2,3,128,128]{4,3,2,1,0:T(8,128)(2,1)} %attend_backward.1), calls=%async_computation.1 | async-start | bytes 3145728 | tf_op jit(solution)/shard_map/all_to_all | solution.py:315
  87.5 1.5 %collective-permute-start.20 = (f32[1,5120]{1,0:T(1,128)S(1)}, f32[1,5120]{1,0:T(1,128)S(1)}, u32[]{:S(2)}, u32[]{:S(2)}) collective-permute-start(f32[1,5120]{1,0:T(1,128)S(1)} %add_add_fusion), channel_id=1, source_target_pairs={{0,1},{1,0},{2,3},{3,2},{4,5},{5,4},{6,7},{7,6},{8,9},{9,8},{10,11... | collective-permute-start | bytes 61448 | tf_op jit(solution)/shard_map/ppermute | solution.py:246
  89.0 2.3 %collective-permute-done.20 = f32[1,5120]{1,0:T(1,128)S(1)} collective-permute-done((f32[1,5120]{1,0:T(1,128)S(1)}, f32[1,5120]{1,0:T(1,128)S(1)}, u32[]{:S(2)}, u32[]{:S(2)}) %collective-permute-start.20) | collective-permute-done | bytes 20512 | tf_op jit(solution)/shard_map/ppermute | solution.py:246
  91.3 3.1 %collective-permute-start.21 = (f32[1,5120]{1,0:T(1,128)S(1)}, f32[1,5120]{1,0:T(1,128)S(1)}, u32[]{:S(2)}, u32[]{:S(2)}) collective-permute-start(f32[1,5120]{1,0:T(1,128)S(1)} %add.31), channel_id=1, source_target_pairs={{0,2},{1,3},{2,0},{3,1},{4,6},{5,7},{6,4},{7,5},{8,10},{9,11},{10,... | collective-permute-start | bytes 61448 | tf_op jit(solution)/shard_map/ppermute | solution.py:246
  94.4 2.3 %collective-permute-done.21 = f32[1,5120]{1,0:T(1,128)S(1)} collective-permute-done((f32[1,5120]{1,0:T(1,128)S(1)}, f32[1,5120]{1,0:T(1,128)S(1)}, u32[]{:S(2)}, u32[]{:S(2)}) %collective-permute-start.21) | collective-permute-done | bytes 20512 | tf_op jit(solution)/shard_map/ppermute | solution.py:246
  96.7 1.7 %collective-permute-start.22 = (f32[1,5120]{1,0:T(1,128)S(1)}, f32[1,5120]{1,0:T(1,128)S(1)}, u32[]{:S(2)}, u32[]{:S(2)}) collective-permute-start(f32[1,5120]{1,0:T(1,128)S(1)} %add.32), channel_id=1, source_target_pairs={{0,4},{1,5},{2,6},{3,7},{4,0},{5,1},{6,2},{7,3},{8,12},{9,13},{10,... | collective-permute-start | bytes 61448 | tf_op jit(solution)/shard_map/ppermute | solution.py:246
  98.4 2.2 %collective-permute-done.22 = f32[1,5120]{1,0:T(1,128)S(1)} collective-permute-done((f32[1,5120]{1,0:T(1,128)S(1)}, f32[1,5120]{1,0:T(1,128)S(1)}, u32[]{:S(2)}, u32[]{:S(2)}) %collective-permute-start.22) | collective-permute-done | bytes 20512 | tf_op jit(solution)/shard_map/ppermute | solution.py:246
  100.6 3.3 %collective-permute-start.23 = (f32[1,5120]{1,0:T(1,128)S(1)}, f32[1,5120]{1,0:T(1,128)S(1)}, u32[]{:S(2)}, u32[]{:S(2)}) collective-permute-start(f32[1,5120]{1,0:T(1,128)S(1)} %add.33), channel_id=1, source_target_pairs={{0,8},{1,9},{2,10},{3,11},{4,12},{5,13},{6,14},{7,15},{8,0},{9,1},... | collective-permute-start | bytes 61448 | tf_op jit(solution)/shard_map/ppermute | solution.py:246
  103.9 2.1 %collective-permute-done.23 = f32[1,5120]{1,0:T(1,128)S(1)} collective-permute-done((f32[1,5120]{1,0:T(1,128)S(1)}, f32[1,5120]{1,0:T(1,128)S(1)}, u32[]{:S(2)}, u32[]{:S(2)}) %collective-permute-start.23) | collective-permute-done | bytes 20512 | tf_op jit(solution)/shard_map/ppermute | solution.py:246
  106.0 0.1 collective-permute-start.24
  106.1 1.2 %collective-permute-done.24 = f32[1,5120]{1,0:T(1,128)S(1)} collective-permute-done((f32[1,5120]{1,0:T(1,128)S(1)}, f32[1,5120]{1,0:T(1,128)S(1)}, u32[]{:S(2)}, u32[]{:S(2)}) %collective-permute-start.24) | collective-permute-done | bytes 20512 | tf_op jit(solution)/shard_map/ppermute | solution.py:246
  107.3 0.6 slice.24
  107.9 0.6 slice.25
  108.5 0.6 all-to-all-done.1
  109.1 2.2 %copy.8 = bf16[1,3,128,16,128]{4,3,2,1,0:T(8,128)(2,1)} copy(bf16[1,3,128,16,128]{4,2,1,3,0:T(8,128)(2,1)S(1)} %bitcast.18) | data formatting | bytes 3145728
  (35 shorter events, 0.5 us)
Async XLA Ops:
  3.6 27.0 %all-to-all-start = ((bf16[8,2,3,128,128]{4,3,2,1,0:T(8,128)(2,1)}), bf16[8,2,3,128,128]{4,3,2,1,0:T(8,128)(2,1)S(1)}, u32[]{:S(2)}, u32[]{:S(2)}) async-start(bf16[8,2,3,128,128]{4,3,2,1,0:T(8,128)(2,1)} %bitcast.1), calls=%async_computation | async-start | bytes 3145728 | tf_op jit(solution)/shard_map/all_to_all | solution.py:287
  30.6 19.3 %collective-permute-start.1 = (bf16[128,3072]{1,0:T(8,128)(2,1)}, bf16[128,3072]{1,0:T(8,128)(2,1)S(1)}, u32[]{:S(2)}, u32[]{:S(2)}) collective-permute-start(bf16[128,3072]{1,0:T(8,128)(2,1)} %bitcast.12), channel_id=1, source_target_pairs={{0,96},{16,112},{32,0},{48,16},{64,32},{80,48},{96,64},{112,80},{1... | collective-permute-start | bytes 2359304 | tf_op jit(solution)/shard_map/ppermute | solution.py:267
  31.7 20.2 %collective-permute-start = (bf16[128,3072]{1,0:T(8,128)(2,1)}, bf16[128,3072]{1,0:T(8,128)(2,1)S(1)}, u32[]{:S(2)}, u32[]{:S(2)}) collective-permute-start(bf16[128,3072]{1,0:T(8,128)(2,1)} %bitcast.13), channel_id=1, source_target_pairs={{0,32},{16,48},{32,64},{48,80},{64,96},{80,112},{96,0},{112,16},{1... | collective-permute-start | bytes 2359304 | tf_op jit(solution)/shard_map/ppermute | solution.py:267
  36.1 26.7 %copy-start = (bf16[1,128,3072]{2,1,0:T(8,128)(2,1)S(1)}, bf16[1,128,3072]{2,1,0:T(8,128)(2,1)}, u32[]{:S(2)}) copy-start(bf16[1,128,3072]{2,1,0:T(8,128)(2,1)} %param.5) | copy-start | bytes 2359300
  36.1 33.0 %copy-start.1 = (f32[3072]{0:T(1024)S(1)}, f32[3072]{0:T(1024)}, u32[]{:S(2)}) copy-start(f32[3072]{0:T(1024)} %param.7) | copy-start | bytes 36868
  36.1 3.7 %collective-permute-start.2 = (f32[8,128]{1,0:T(8,128)S(1)}, f32[8,128]{1,0:T(8,128)S(1)}, u32[]{:S(2)}, u32[]{:S(2)}) collective-permute-start(f32[8,128]{1,0:T(8,128)S(1)} %get-tuple-element.24), channel_id=1, source_target_pairs={{0,1},{1,0},{2,3},{3,2},{4,5},{5,4},{6,7},{7,6},{8,9},{9,8},{10,11... | collective-permute-start | bytes 12296 | tf_op jit(solution)/shard_map/ppermute | solution.py:246
  39.7 5.1 %collective-permute-start.3 = (f32[8,128]{1,0:T(8,128)S(1)}, f32[8,128]{1,0:T(8,128)S(1)}, u32[]{:S(2)}, u32[]{:S(2)}) collective-permute-start(f32[8,128]{1,0:T(8,128)S(1)} %max.24), channel_id=1, source_target_pairs={{0,2},{1,3},{2,0},{3,1},{4,6},{5,7},{6,4},{7,5},{8,10},{9,11},{10,... | collective-permute-start | bytes 12296 | tf_op jit(solution)/shard_map/ppermute | solution.py:246
  44.8 3.6 %collective-permute-start.4 = (f32[8,128]{1,0:T(8,128)S(1)}, f32[8,128]{1,0:T(8,128)S(1)}, u32[]{:S(2)}, u32[]{:S(2)}) collective-permute-start(f32[8,128]{1,0:T(8,128)S(1)} %max.25), channel_id=1, source_target_pairs={{0,4},{1,5},{2,6},{3,7},{4,0},{5,1},{6,2},{7,3},{8,12},{9,13},{10,... | collective-permute-start | bytes 12296 | tf_op jit(solution)/shard_map/ppermute | solution.py:246
  52.0 7.4 %collective-permute-start.9 = (f32[8,128]{1,0:T(8,128)S(1)}, f32[8,128]{1,0:T(8,128)S(1)}, u32[]{:S(2)}, u32[]{:S(2)}) collective-permute-start(f32[8,128]{1,0:T(8,128)S(1)} %max.26), channel_id=1, source_target_pairs={{0,96},{16,112},{32,64},{48,80},{64,32},{80,48},{96,0},{112,16},{1... | collective-permute-start | bytes 12296 | tf_op jit(solution)/shard_map/ppermute | solution.py:246
  52.4 7.1 %collective-permute-start.8 = (f32[8,128]{1,0:T(8,128)S(1)}, f32[8,128]{1,0:T(8,128)S(1)}, u32[]{:S(2)}, u32[]{:S(2)}) collective-permute-start(f32[8,128]{1,0:T(8,128)S(1)} %max.26), channel_id=1, source_target_pairs={{0,64},{16,80},{32,96},{48,112},{64,0},{80,16},{96,32},{112,48},{1... | collective-permute-start | bytes 12296 | tf_op jit(solution)/shard_map/ppermute | solution.py:246
  53.8 5.6 %collective-permute-start.7 = (f32[8,128]{1,0:T(8,128)S(1)}, f32[8,128]{1,0:T(8,128)S(1)}, u32[]{:S(2)}, u32[]{:S(2)}) collective-permute-start(f32[8,128]{1,0:T(8,128)S(1)} %max.26), channel_id=1, source_target_pairs={{0,32},{16,48},{32,0},{48,16},{64,96},{80,112},{96,64},{112,80},{1... | collective-permute-start | bytes 12296 | tf_op jit(solution)/shard_map/ppermute | solution.py:246
  56.2 9.8 %collective-permute-start.5 = (bf16[64,3072]{1,0:T(8,128)(2,1)S(1)}, bf16[64,3072]{1,0:T(8,128)(2,1)S(1)}, u32[]{:S(2)}, u32[]{:S(2)}) collective-permute-start(bf16[64,3072]{1,0:T(8,128)(2,1)S(1)} %slice.18), channel_id=1, source_target_pairs={{0,32},{16,48},{32,64},{48,80},{64,96},{80,112},{96,0},{112,16},{1... | collective-permute-start | bytes 1179656 | tf_op jit(solution)/shard_map/ppermute | solution.py:267
  56.2 9.8 %collective-permute-start.6 = (bf16[64,3072]{1,0:T(8,128)(2,1)S(1)}, bf16[64,3072]{1,0:T(8,128)(2,1)S(1)}, u32[]{:S(2)}, u32[]{:S(2)}) collective-permute-start(bf16[64,3072]{1,0:T(8,128)(2,1)S(1)} %slice.19), channel_id=1, source_target_pairs={{0,96},{16,112},{32,0},{48,16},{64,32},{80,48},{96,64},{112,80},{1... | collective-permute-start | bytes 1179656 | tf_op jit(solution)/shard_map/ppermute | solution.py:267
  59.5 5.1 %collective-permute-start.10 = (f32[8,128]{1,0:T(8,128)S(1)}, f32[8,128]{1,0:T(8,128)S(1)}, u32[]{:S(2)}, u32[]{:S(2)}) collective-permute-start(f32[8,128]{1,0:T(8,128)S(1)} %maximum_select_fusion.1), channel_id=1, source_target_pairs={{0,8},{1,9},{2,10},{3,11},{4,12},{5,13},{6,14},{7,15},{8,0},{9,1},... | collective-permute-start | bytes 12296 | tf_op jit(solution)/shard_map/ppermute | solution.py:246
  62.8 4.8 %collective-permute-start.12 = (bf16[128,3072]{1,0:T(8,128)(2,1)S(1)}, bf16[128,3072]{1,0:T(8,128)(2,1)S(1)}, u32[]{:S(2)}, u32[]{:S(2)}) collective-permute-start(bf16[128,3072]{1,0:T(8,128)(2,1)S(1)} %bitcast.14), channel_id=1, source_target_pairs={{0,16},{16,0},{32,48},{48,32},{64,80},{80,64},{96,112},{112,96},{1... | collective-permute-start | bytes 2359304 | tf_op jit(solution)/shard_map/ppermute | solution.py:246
  62.8 6.3 %collective-permute-start.13 = (bf16[128,3072]{1,0:T(8,128)(2,1)S(1)}, bf16[128,3072]{1,0:T(8,128)(2,1)S(1)}, u32[]{:S(2)}, u32[]{:S(2)}) collective-permute-start(bf16[128,3072]{1,0:T(8,128)(2,1)S(1)} %collective-permute-done.rest_1_), channel_id=1, source_target_pairs={{0,16},{16,0},{32,48},{48,32},{64,80},{80,64},{96,112},{112,96},{1... | collective-permute-start | bytes 2359304 | tf_op jit(solution)/shard_map/ppermute | solution.py:246
  64.7 4.4 %collective-permute-start.14 = (bf16[128,3072]{1,0:T(8,128)(2,1)S(1)}, bf16[128,3072]{1,0:T(8,128)(2,1)S(1)}, u32[]{:S(2)}, u32[]{:S(2)}) collective-permute-start(bf16[128,3072]{1,0:T(8,128)(2,1)S(1)} %collective-permute-done.1.rest_2_), channel_id=1, source_target_pairs={{0,16},{16,0},{32,48},{48,32},{64,80},{80,64},{96,112},{112,96},{1... | collective-permute-start | bytes 2359304 | tf_op jit(solution)/shard_map/ppermute | solution.py:246
  66.0 1.3 %collective-permute-start.11 = (f32[8,128]{1,0:T(8,128)S(1)}, f32[8,128]{1,0:T(8,128)S(1)}, u32[]{:S(2)}, u32[]{:S(2)}) collective-permute-start(f32[8,128]{1,0:T(8,128)S(1)} %max.30), channel_id=1, source_target_pairs={{0,16},{16,0},{32,48},{48,32},{64,80},{80,64},{96,112},{112,96},{1... | collective-permute-start | bytes 12296 | tf_op jit(solution)/shard_map/ppermute | solution.py:246
  66.0 1.9 %collective-permute-start.15 = (bf16[64,3072]{1,0:T(8,128)(2,1)S(1)}, bf16[64,3072]{1,0:T(8,128)(2,1)S(1)}, u32[]{:S(2)}, u32[]{:S(2)}) collective-permute-start(bf16[64,3072]{1,0:T(8,128)(2,1)S(1)} %collective-permute-done.5.rest_3_), channel_id=1, source_target_pairs={{0,16},{16,0},{32,48},{48,32},{64,80},{80,64},{96,112},{112,96},{1... | collective-permute-start | bytes 1179656 | tf_op jit(solution)/shard_map/ppermute | solution.py:246
  67.3 1.7 %collective-permute-start.16 = (bf16[64,3072]{1,0:T(8,128)(2,1)S(1)}, bf16[64,3072]{1,0:T(8,128)(2,1)S(1)}, u32[]{:S(2)}, u32[]{:S(2)}) collective-permute-start(bf16[64,3072]{1,0:T(8,128)(2,1)S(1)} %collective-permute-done.6.rest_4_), channel_id=1, source_target_pairs={{0,16},{16,0},{32,48},{48,32},{64,80},{80,64},{96,112},{112,96},{1... | collective-permute-start | bytes 1179656 | tf_op jit(solution)/shard_map/ppermute | solution.py:246
  74.1 9.2 %collective-permute-start.19 = (f32[1,5120]{1,0:T(1,128)S(1)}, f32[1,5120]{1,0:T(1,128)S(1)}, u32[]{:S(2)}, u32[]{:S(2)}) collective-permute-start(f32[1,5120]{1,0:T(1,128)S(1)} %get-tuple-element.34), channel_id=1, source_target_pairs={{0,96},{16,112},{32,64},{48,80},{64,32},{80,48},{96,0},{112,16},{1... | collective-permute-start | bytes 61448 | tf_op jit(solution)/shard_map/ppermute | solution.py:246
  77.0 6.3 %collective-permute-start.18 = (f32[1,5120]{1,0:T(1,128)S(1)}, f32[1,5120]{1,0:T(1,128)S(1)}, u32[]{:S(2)}, u32[]{:S(2)}) collective-permute-start(f32[1,5120]{1,0:T(1,128)S(1)} %get-tuple-element.34), channel_id=1, source_target_pairs={{0,64},{16,80},{32,96},{48,112},{64,0},{80,16},{96,32},{112,48},{1... | collective-permute-start | bytes 61448 | tf_op jit(solution)/shard_map/ppermute | solution.py:246
  77.0 6.3 %collective-permute-start.17 = (f32[1,5120]{1,0:T(1,128)S(1)}, f32[1,5120]{1,0:T(1,128)S(1)}, u32[]{:S(2)}, u32[]{:S(2)}) collective-permute-start(f32[1,5120]{1,0:T(1,128)S(1)} %get-tuple-element.34), channel_id=1, source_target_pairs={{0,32},{16,48},{32,0},{48,16},{64,96},{80,112},{96,64},{112,80},{1... | collective-permute-start | bytes 61448 | tf_op jit(solution)/shard_map/ppermute | solution.py:246
  83.4 25.7 %all-to-all-start.1 = ((bf16[8,2,3,128,128]{4,3,2,1,0:T(8,128)(2,1)}), bf16[8,2,3,128,128]{4,3,2,1,0:T(8,128)(2,1)S(1)}, u32[]{:S(2)}, u32[]{:S(2)}) async-start(bf16[8,2,3,128,128]{4,3,2,1,0:T(8,128)(2,1)} %attend_backward.1), calls=%async_computation.1 | async-start | bytes 3145728 | tf_op jit(solution)/shard_map/all_to_all | solution.py:315
  87.5 3.8 %collective-permute-start.20 = (f32[1,5120]{1,0:T(1,128)S(1)}, f32[1,5120]{1,0:T(1,128)S(1)}, u32[]{:S(2)}, u32[]{:S(2)}) collective-permute-start(f32[1,5120]{1,0:T(1,128)S(1)} %add_add_fusion), channel_id=1, source_target_pairs={{0,1},{1,0},{2,3},{3,2},{4,5},{5,4},{6,7},{7,6},{8,9},{9,8},{10,11... | collective-permute-start | bytes 61448 | tf_op jit(solution)/shard_map/ppermute | solution.py:246
  91.3 5.4 %collective-permute-start.21 = (f32[1,5120]{1,0:T(1,128)S(1)}, f32[1,5120]{1,0:T(1,128)S(1)}, u32[]{:S(2)}, u32[]{:S(2)}) collective-permute-start(f32[1,5120]{1,0:T(1,128)S(1)} %add.31), channel_id=1, source_target_pairs={{0,2},{1,3},{2,0},{3,1},{4,6},{5,7},{6,4},{7,5},{8,10},{9,11},{10,... | collective-permute-start | bytes 61448 | tf_op jit(solution)/shard_map/ppermute | solution.py:246
  96.7 3.9 %collective-permute-start.22 = (f32[1,5120]{1,0:T(1,128)S(1)}, f32[1,5120]{1,0:T(1,128)S(1)}, u32[]{:S(2)}, u32[]{:S(2)}) collective-permute-start(f32[1,5120]{1,0:T(1,128)S(1)} %add.32), channel_id=1, source_target_pairs={{0,4},{1,5},{2,6},{3,7},{4,0},{5,1},{6,2},{7,3},{8,12},{9,13},{10,... | collective-permute-start | bytes 61448 | tf_op jit(solution)/shard_map/ppermute | solution.py:246
  100.6 5.4 %collective-permute-start.23 = (f32[1,5120]{1,0:T(1,128)S(1)}, f32[1,5120]{1,0:T(1,128)S(1)}, u32[]{:S(2)}, u32[]{:S(2)}) collective-permute-start(f32[1,5120]{1,0:T(1,128)S(1)} %add.33), channel_id=1, source_target_pairs={{0,8},{1,9},{2,10},{3,11},{4,12},{5,13},{6,14},{7,15},{8,0},{9,1},... | collective-permute-start | bytes 61448 | tf_op jit(solution)/shard_map/ppermute | solution.py:246
  106.0 1.3 %collective-permute-start.24 = (f32[1,5120]{1,0:T(1,128)S(1)}, f32[1,5120]{1,0:T(1,128)S(1)}, u32[]{:S(2)}, u32[]{:S(2)}) collective-permute-start(f32[1,5120]{1,0:T(1,128)S(1)} %add.34), channel_id=1, source_target_pairs={{0,16},{16,0},{32,48},{48,32},{64,80},{80,64},{96,112},{112,96},{1... | collective-permute-start | bytes 61448 | tf_op jit(solution)/shard_map/ppermute | solution.py:246

commit v6 on v5

--- a/solution.py
+++ b/solution.py
@@ -93,7 +93,7 @@
 WIDTH = 512
 
 
-def projection_kernel(place_ref, message_ref, bound_ref, clip_ref, out_ref, own_ref, *rest):
+def projection_kernel(place_ref, message_ref, bound_ref, weight_max_ref, clip_ref, out_ref, own_ref, *rest):
     pieces = rest[:10]
     grad_ref, vec_ref, cot_ref, wq_ref, tanh_ref, quant_ref = rest[10:]
     place = place_ref[0]
@@ -109,11 +109,9 @@
     act_column = jnp.concatenate(
         [to_column(message_ref[0:1]), to_column(message_ref[1:2])], axis=0
     )
-    weight_max = None
-    for j in range(D // WIDTH):
-        weight = own_ref[:, j * WIDTH : (j + 1) * WIDTH]
-        top = jnp.max(jnp.abs(weight.astype(jnp.float32)), axis=1, keepdims=True)
-        weight_max = top if weight_max is None else jnp.maximum(weight_max, top)
+    weight_max = jnp.concatenate(
+        [to_column(weight_max_ref[0]), to_column(weight_max_ref[1])], axis=0
+    )
     smooth = jnp.sqrt((act_column + epsilon) / (weight_max + epsilon))
     for j in range(D // WIDTH):
         columns = slice(j * WIDTH, (j + 1) * WIDTH)
@@ -153,11 +151,11 @@
     vec_ref[:, pl.ds(pl.multiple_of(place * CHANNELS, CHANNELS), CHANNELS)] = to_row(smooth_part)
 
 
-def projection(place, message, bound, clip, out, own_rows, pieces):
+def projection(place, message, bound, weight_max, clip, out, own_rows, pieces):
     vmem = pl.BlockSpec(memory_space=pltpu.VMEM)
     return pl.pallas_call(
         projection_kernel,
-        in_specs=[pl.BlockSpec(memory_space=pltpu.SMEM), vmem, vmem, vmem, vmem, vmem]+ [vmem] * 10,
+        in_specs=[pl.BlockSpec(memory_space=pltpu.SMEM), vmem, vmem, vmem, vmem, vmem, vmem]+ [vmem] * 10,
         out_specs=[vmem, vmem],
         out_shape=[
             jax.ShapeDtypeStruct((LOCAL_HEADS, HEAD_DIM, LEN), jnp.bfloat16),
@@ -176,7 +174,7 @@
             transcendentals=CHANNELS * (D + LEN),
         ),
         name="projection_backward",
-    )(place, message, bound, clip, out, own_rows, *pieces)
+    )(place, message, bound, weight_max, clip, out, own_rows, *pieces)
 
 
 def backward_kernel(y_ref, p_ref, out_ref, grad_ref, result_ref, z_ref, ds_ref, sem):
@@ -309,7 +307,7 @@
     message = jnp.where(is_bound, pair, message)
     pieces = [own, before, behind, far_low, far_high, own_swapped]
     pieces += [swap_cores(piece) for piece in (before, behind, far_low, far_high)]
-    grad_out, vector = projection(place_vector, message, message, clip, out, own_rows, pieces)
+    grad_out, vector = projection(place_vector, message, message, weight_max, clip, out, own_rows, pieces)
     back = backward(heads, weights, out, grad_out)
     back, vector = lax.optimization_barrier((back, total_over_depth(vector)))
     received = lax.all_to_all(back, "seq", split_axis=0, concat_axis=0, tiled=True)

time: 112 us -> 112 us (level)
  no operation moved by 1% of the time
where the time goes in v6:
time: 112 us; the launch traced here: 111 us
  waiting for transfers between devices  45.1 us (40%)
  starting transfers between devices  43.3 us (39%)
  Pallas kernels  13.2 us (12%)
  local copies, waits for them, and re-layouts  7.89 us (7%)
    ppermute x21, starting transfers between devices, exchange(): return lax.ppermute(tensor, axis, [(i, i ^ bits) for i in range(size)])  28.5 us
    ppermute x21, waiting for transfers between devices, exchange(): return lax.ppermute(tensor, axis, [(i, i ^ bits) for i in range(size)])  19.9 us
    all_to_all x1, waiting for transfers between devices, per_device(): heads = lax.all_to_all(send, 'seq', split_axis=0, concat_axis=0, tiled=True)  19.7 us
    all_to_all x1, starting transfers between devices, per_device(): heads = lax.all_to_all(send, 'seq', split_axis=0, concat_axis=0, tiled=True)  5.4 us
    ppermute x4, starting transfers between devices, shift_depth(): lax.ppermute(tensor, 'seq', [(i, (i + 2 * steps) % SEQ) for i in range(SE...  5.26 us
    unnamed x6, local copies, waits for them, and re-layouts  5.12 us
    pallas_call x1, Pallas kernels, backward(): pl.pallas_call(backward_kernel, in_specs=[vmem] * 4, out_specs=pl.BlockSp...  5.02 us
    ppermute x4, waiting for transfers between devices, shift_depth(): lax.ppermute(tensor, 'seq', [(i, (i + 2 * steps) % SEQ) for i in range(SE...  4.87 us
  transfers between devices with their start and end apart: 27, of which 17 were waited for; matrix products, arithmetic and copies ran while one was open for 3% of the time, Pallas kernels for 8%

profile of v6, /device:TPU:0, one launch (start us, length us, event | category | flops | bytes accessed | tf_op | source)
XLA Modules:
  0.0 110.9 jit_solution(2637742899280952934)
XLA Ops:
  0.6 3.0 %copy.7 = bf16[1,3,128,16,128]{4,2,1,3,0:T(8,128)(2,1)} copy(bf16[1,3,128,16,128]{4,3,2,1,0:T(8,128)(2,1)} %param.4) | data formatting | bytes 3145728 | tf_op args[0]
  3.6 5.4 %all-to-all-start = ((bf16[8,2,3,128,128]{4,3,2,1,0:T(8,128)(2,1)}), bf16[8,2,3,128,128]{4,3,2,1,0:T(8,128)(2,1)S(1)}, u32[]{:S(2)}, u32[]{:S(2)}) async-start(bf16[8,2,3,128,128]{4,3,2,1,0:T(8,128)(2,1)} %bitcast.1), calls=%async_computation | async-start | bytes 3145728 | tf_op jit(solution)/shard_map/all_to_all | solution.py:285
  9.0 1.5 %constant_dynamic-slice_fusion.own_ref = bf16[256,3072]{1,0:T(8,128)(2,1)S(1)} fusion(bf16[2048,3072]{1,0:T(8,128)(2,1)} %param.6, s32[]{:T(128)S(6)} %select_n.10), kind=kLoop, calls=%fused_computation.5 | loop fusion | bytes 3145732 | tf_op jit(solution)/shard_map/dynamic_slice | solution.py:282
  10.5 0.4 abs_reduce_fusion
  10.9 19.7 %all-to-all-done.y_ref = bf16[8,2,3,128,128]{4,3,2,1,0:T(8,128)(2,1)S(1)} async-done(((bf16[8,2,3,128,128]{4,3,2,1,0:T(8,128)(2,1)}), bf16[8,2,3,128,128]{4,3,2,1,0:T(8,128)(2,1)S(1)}, u32[]{:S(2)}, u32[]{:S(2)}) %all-to-all-start) | async-done | bytes 1572896 | tf_op jit(solution)/shard_map/all_to_all | solution.py:285
  30.6 1.2 %collective-permute-start.1 = (bf16[128,3072]{1,0:T(8,128)(2,1)}, bf16[128,3072]{1,0:T(8,128)(2,1)S(1)}, u32[]{:S(2)}, u32[]{:S(2)}) collective-permute-start(bf16[128,3072]{1,0:T(8,128)(2,1)} %bitcast.12), channel_id=1, source_target_pairs={{0,96},{16,112},{32,0},{48,16},{64,32},{80,48},{96,64},{112,80},{1... | collective-permute-start | bytes 2359304 | tf_op jit(solution)/shard_map/ppermute | solution.py:265
  31.7 0.9 collective-permute-start
  32.6 3.5 %attend_forward.1 = (bf16[2,1024,1024]{2,1,0:T(8,128)(2,1)S(1)}, bf16[2,128,1024]{2,1,0:T(8,128)(2,1)S(1)}, f32[8,128]{1,0:T(8,128)S(1)}) custom-call(bf16[8,2,3,128,128]{4,3,2,1,0:T(8,128)(2,1)S(1)} %all-to-all-done.y_ref, f32[2,1,128]{2,1,0:T(1,128)S(1)} %bitcast.17), custom_call_target="tpu_custom_call" | custom-call | flops 1073741824 | bytes 6291456 | tf_op jit(solution)/shard_map/attend_forward/pallas_call | solution.py:73
  36.1 1.5 %collective-permute-start.2 = (f32[8,128]{1,0:T(8,128)S(1)}, f32[8,128]{1,0:T(8,128)S(1)}, u32[]{:S(2)}, u32[]{:S(2)}) collective-permute-start(f32[8,128]{1,0:T(8,128)S(1)} %get-tuple-element.24), channel_id=1, source_target_pairs={{0,1},{1,0},{2,3},{3,2},{4,5},{5,4},{6,7},{7,6},{8,9},{9,8},{10,11... | collective-permute-start | bytes 12296 | tf_op jit(solution)/shard_map/ppermute | solution.py:244
  37.6 2.1 %collective-permute-done.2 = f32[8,128]{1,0:T(8,128)S(1)} collective-permute-done((f32[8,128]{1,0:T(8,128)S(1)}, f32[8,128]{1,0:T(8,128)S(1)}, u32[]{:S(2)}, u32[]{:S(2)}) %collective-permute-start.2) | collective-permute-done | bytes 4128 | tf_op jit(solution)/shard_map/ppermute | solution.py:244
  39.7 3.0 %collective-permute-start.3 = (f32[8,128]{1,0:T(8,128)S(1)}, f32[8,128]{1,0:T(8,128)S(1)}, u32[]{:S(2)}, u32[]{:S(2)}) collective-permute-start(f32[8,128]{1,0:T(8,128)S(1)} %max.24), channel_id=1, source_target_pairs={{0,2},{1,3},{2,0},{3,1},{4,6},{5,7},{6,4},{7,5},{8,10},{9,11},{10,... | collective-permute-start | bytes 12296 | tf_op jit(solution)/shard_map/ppermute | solution.py:244
  42.8 2.1 %collective-permute-done.3 = f32[8,128]{1,0:T(8,128)S(1)} collective-permute-done((f32[8,128]{1,0:T(8,128)S(1)}, f32[8,128]{1,0:T(8,128)S(1)}, u32[]{:S(2)}, u32[]{:S(2)}) %collective-permute-start.3) | collective-permute-done | bytes 4128 | tf_op jit(solution)/shard_map/ppermute | solution.py:244
  44.8 1.6 %collective-permute-start.4 = (f32[8,128]{1,0:T(8,128)S(1)}, f32[8,128]{1,0:T(8,128)S(1)}, u32[]{:S(2)}, u32[]{:S(2)}) collective-permute-start(f32[8,128]{1,0:T(8,128)S(1)} %max.25), channel_id=1, source_target_pairs={{0,4},{1,5},{2,6},{3,7},{4,0},{5,1},{6,2},{7,3},{8,12},{9,13},{10,... | collective-permute-start | bytes 12296 | tf_op jit(solution)/shard_map/ppermute | solution.py:244
  46.4 2.0 %collective-permute-done.4 = f32[8,128]{1,0:T(8,128)S(1)} collective-permute-done((f32[8,128]{1,0:T(8,128)S(1)}, f32[8,128]{1,0:T(8,128)S(1)}, u32[]{:S(2)}, u32[]{:S(2)}) %collective-permute-start.4) | collective-permute-done | bytes 4128 | tf_op jit(solution)/shard_map/ppermute | solution.py:244
  48.5 1.4 %collective-permute-done.1.rest_2_ = bf16[128,3072]{1,0:T(8,128)(2,1)S(1)} collective-permute-done((bf16[128,3072]{1,0:T(8,128)(2,1)}, bf16[128,3072]{1,0:T(8,128)(2,1)S(1)}, u32[]{:S(2)}, u32[]{:S(2)}) %collective-permute-start.1) | collective-permute-done | bytes 786464 | tf_op jit(solution)/shard_map/ppermute | solution.py:265
  49.9 2.1 %collective-permute-done.rest_1_ = bf16[128,3072]{1,0:T(8,128)(2,1)S(1)} collective-permute-done((bf16[128,3072]{1,0:T(8,128)(2,1)}, bf16[128,3072]{1,0:T(8,128)(2,1)S(1)}, u32[]{:S(2)}, u32[]{:S(2)}) %collective-permute-start) | collective-permute-done | bytes 786464 | tf_op jit(solution)/shard_map/ppermute | solution.py:265
  52.0 0.4 collective-permute-start.9
  52.4 1.4 %collective-permute-start.8 = (f32[8,128]{1,0:T(8,128)S(1)}, f32[8,128]{1,0:T(8,128)S(1)}, u32[]{:S(2)}, u32[]{:S(2)}) collective-permute-start(f32[8,128]{1,0:T(8,128)S(1)} %max.26), channel_id=1, source_target_pairs={{0,64},{16,80},{32,96},{48,112},{64,0},{80,16},{96,32},{112,48},{1... | collective-permute-start | bytes 12296 | tf_op jit(solution)/shard_map/ppermute | solution.py:244
  53.8 2.4 %collective-permute-start.7 = (f32[8,128]{1,0:T(8,128)S(1)}, f32[8,128]{1,0:T(8,128)S(1)}, u32[]{:S(2)}, u32[]{:S(2)}) collective-permute-start(f32[8,128]{1,0:T(8,128)S(1)} %max.26), channel_id=1, source_target_pairs={{0,32},{16,48},{32,0},{48,16},{64,96},{80,112},{96,64},{112,80},{1... | collective-permute-start | bytes 12296 | tf_op jit(solution)/shard_map/ppermute | solution.py:244
  56.2 3.2 %collective-permute-start.6 = (bf16[64,3072]{1,0:T(8,128)(2,1)S(1)}, bf16[64,3072]{1,0:T(8,128)(2,1)S(1)}, u32[]{:S(2)}, u32[]{:S(2)}) collective-permute-start(bf16[64,3072]{1,0:T(8,128)(2,1)S(1)} %slice.19), channel_id=1, source_target_pairs={{0,96},{16,112},{32,0},{48,16},{64,32},{80,48},{96,64},{112,80},{1... | collective-permute-start | bytes 1179656 | tf_op jit(solution)/shard_map/ppermute | solution.py:265
  59.5 3.2 %collective-permute-start.10 = (f32[8,128]{1,0:T(8,128)S(1)}, f32[8,128]{1,0:T(8,128)S(1)}, u32[]{:S(2)}, u32[]{:S(2)}) collective-permute-start(f32[8,128]{1,0:T(8,128)S(1)} %maximum_select_fusion.1), channel_id=1, source_target_pairs={{0,8},{1,9},{2,10},{3,11},{4,12},{5,13},{6,14},{7,15},{8,0},{9,1},... | collective-permute-start | bytes 12296 | tf_op jit(solution)/shard_map/ppermute | solution.py:244
  62.8 0.5 collective-permute-start.13
  63.3 1.4 %collective-permute-done.10 = f32[8,128]{1,0:T(8,128)S(1)} collective-permute-done((f32[8,128]{1,0:T(8,128)S(1)}, f32[8,128]{1,0:T(8,128)S(1)}, u32[]{:S(2)}, u32[]{:S(2)}) %collective-permute-start.10) | collective-permute-done | bytes 4128 | tf_op jit(solution)/shard_map/ppermute | solution.py:244
  64.7 1.4 %collective-permute-done.5.rest_3_ = bf16[64,3072]{1,0:T(8,128)(2,1)S(1)} collective-permute-done((bf16[64,3072]{1,0:T(8,128)(2,1)S(1)}, bf16[64,3072]{1,0:T(8,128)(2,1)S(1)}, u32[]{:S(2)}, u32[]{:S(2)}) %collective-permute-start.5) | collective-permute-done | bytes 393248 | tf_op jit(solution)/shard_map/ppermute | solution.py:265
  66.0 0.5 collective-permute-start.15
  66.6 0.7 collective-permute-done.11
  67.3 0.1 collective-permute-start.16
  67.5 0.4 collective-permute-done.15.rest_8_
  67.9 1.1 %collective-permute-done.16.rest_9_ = bf16[64,3072]{1,0:T(8,128)(2,1)S(1)} collective-permute-done((bf16[64,3072]{1,0:T(8,128)(2,1)S(1)}, bf16[64,3072]{1,0:T(8,128)(2,1)S(1)}, u32[]{:S(2)}, u32[]{:S(2)}) %collective-permute-start.16) | collective-permute-done | bytes 393248 | tf_op jit(solution)/shard_map/ppermute | solution.py:244
  69.0 4.7 %projection_backward.1 = (bf16[2,128,1024]{2,1,0:T(8,128)(2,1)S(1)}, f32[1,5120]{1,0:T(1,128)S(1)}) custom-call(s32[1]{0:T(128)} %bitcast.4.place_ref, f32[8,128]{1,0:T(8,128)S(1)} %maximum_select_fusion.message_ref.bound_ref, f32[8,128]{1,0:T(8,128)S(1)} %maximum_select_fusion.message_ref.bound_ref, f32[2,1,128]{2,1,0:T(1,128)S(1)} %bitcast.18, ...), custom_call_target="tpu_custom_call" | custom-call | flops 3221225472 | bytes 9437184 | tf_op jit(solution)/shard_map/projection_backward/pallas_call | solution.py:156
  73.8 2.9 %collective-permute-start.19 = (f32[1,5120]{1,0:T(1,128)S(1)}, f32[1,5120]{1,0:T(1,128)S(1)}, u32[]{:S(2)}, u32[]{:S(2)}) collective-permute-start(f32[1,5120]{1,0:T(1,128)S(1)} %get-tuple-element.34), channel_id=1, source_target_pairs={{0,96},{16,112},{32,64},{48,80},{64,32},{80,48},{96,0},{112,16},{1... | collective-permute-start | bytes 61448 | tf_op jit(solution)/shard_map/ppermute | solution.py:244
  76.7 1.2 %collective-permute-start.17 = (f32[1,5120]{1,0:T(1,128)S(1)}, f32[1,5120]{1,0:T(1,128)S(1)}, u32[]{:S(2)}, u32[]{:S(2)}) collective-permute-start(f32[1,5120]{1,0:T(1,128)S(1)} %get-tuple-element.34), channel_id=1, source_target_pairs={{0,32},{16,48},{32,0},{48,16},{64,96},{80,112},{96,64},{112,80},{1... | collective-permute-start | bytes 61448 | tf_op jit(solution)/shard_map/ppermute | solution.py:244
  77.9 5.0 %attend_backward.1 = bf16[8,2,3,128,128]{4,3,2,1,0:T(8,128)(2,1)} custom-call(bf16[8,2,3,128,128]{4,3,2,1,0:T(8,128)(2,1)S(1)} %all-to-all-done.y_ref, bf16[2,1024,1024]{2,1,0:T(8,128)(2,1)S(1)} %get-tuple-element.21.p_ref, bf16[2,128,1024]{2,1,0:T(8,128)(2,1)S(1)} %get-tuple-element.22.out_ref, bf16[2,128,1024]{2,1,0:T(8,128)(2,1)S(1)} %get-tuple-element.33.grad_ref), custom_call_target="tpu_custom_call" | custom-call | flops 2147483648 | bytes 8388608 | tf_op jit(solution)/shard_map/attend_backward/pallas_call | solution.py:221
  83.0 4.2 %all-to-all-start.1 = ((bf16[8,2,3,128,128]{4,3,2,1,0:T(8,128)(2,1)}), bf16[8,2,3,128,128]{4,3,2,1,0:T(8,128)(2,1)S(1)}, u32[]{:S(2)}, u32[]{:S(2)}) async-start(bf16[8,2,3,128,128]{4,3,2,1,0:T(8,128)(2,1)} %attend_backward.1), calls=%async_computation.1 | async-start | bytes 3145728 | tf_op jit(solution)/shard_map/all_to_all | solution.py:313
  87.2 1.5 %collective-permute-start.20 = (f32[1,5120]{1,0:T(1,128)S(1)}, f32[1,5120]{1,0:T(1,128)S(1)}, u32[]{:S(2)}, u32[]{:S(2)}) collective-permute-start(f32[1,5120]{1,0:T(1,128)S(1)} %add_add_fusion), channel_id=1, source_target_pairs={{0,1},{1,0},{2,3},{3,2},{4,5},{5,4},{6,7},{7,6},{8,9},{9,8},{10,11... | collective-permute-start | bytes 61448 | tf_op jit(solution)/shard_map/ppermute | solution.py:244
  88.7 2.3 %collective-permute-done.20 = f32[1,5120]{1,0:T(1,128)S(1)} collective-permute-done((f32[1,5120]{1,0:T(1,128)S(1)}, f32[1,5120]{1,0:T(1,128)S(1)}, u32[]{:S(2)}, u32[]{:S(2)}) %collective-permute-start.20) | collective-permute-done | bytes 20512 | tf_op jit(solution)/shard_map/ppermute | solution.py:244
  91.0 3.1 %collective-permute-start.21 = (f32[1,5120]{1,0:T(1,128)S(1)}, f32[1,5120]{1,0:T(1,128)S(1)}, u32[]{:S(2)}, u32[]{:S(2)}) collective-permute-start(f32[1,5120]{1,0:T(1,128)S(1)} %add.31), channel_id=1, source_target_pairs={{0,2},{1,3},{2,0},{3,1},{4,6},{5,7},{6,4},{7,5},{8,10},{9,11},{10,... | collective-permute-start | bytes 61448 | tf_op jit(solution)/shard_map/ppermute | solution.py:244
  94.1 2.2 %collective-permute-done.21 = f32[1,5120]{1,0:T(1,128)S(1)} collective-permute-done((f32[1,5120]{1,0:T(1,128)S(1)}, f32[1,5120]{1,0:T(1,128)S(1)}, u32[]{:S(2)}, u32[]{:S(2)}) %collective-permute-start.21) | collective-permute-done | bytes 20512 | tf_op jit(solution)/shard_map/ppermute | solution.py:244
  96.4 1.7 %collective-permute-start.22 = (f32[1,5120]{1,0:T(1,128)S(1)}, f32[1,5120]{1,0:T(1,128)S(1)}, u32[]{:S(2)}, u32[]{:S(2)}) collective-permute-start(f32[1,5120]{1,0:T(1,128)S(1)} %add.32), channel_id=1, source_target_pairs={{0,4},{1,5},{2,6},{3,7},{4,0},{5,1},{6,2},{7,3},{8,12},{9,13},{10,... | collective-permute-start | bytes 61448 | tf_op jit(solution)/shard_map/ppermute | solution.py:244
  98.0 2.2 %collective-permute-done.22 = f32[1,5120]{1,0:T(1,128)S(1)} collective-permute-done((f32[1,5120]{1,0:T(1,128)S(1)}, f32[1,5120]{1,0:T(1,128)S(1)}, u32[]{:S(2)}, u32[]{:S(2)}) %collective-permute-start.22) | collective-permute-done | bytes 20512 | tf_op jit(solution)/shard_map/ppermute | solution.py:244
  100.3 3.3 %collective-permute-start.23 = (f32[1,5120]{1,0:T(1,128)S(1)}, f32[1,5120]{1,0:T(1,128)S(1)}, u32[]{:S(2)}, u32[]{:S(2)}) collective-permute-start(f32[1,5120]{1,0:T(1,128)S(1)} %add.33), channel_id=1, source_target_pairs={{0,8},{1,9},{2,10},{3,11},{4,12},{5,13},{6,14},{7,15},{8,0},{9,1},... | collective-permute-start | bytes 61448 | tf_op jit(solution)/shard_map/ppermute | solution.py:244
  103.5 2.1 %collective-permute-done.23 = f32[1,5120]{1,0:T(1,128)S(1)} collective-permute-done((f32[1,5120]{1,0:T(1,128)S(1)}, f32[1,5120]{1,0:T(1,128)S(1)}, u32[]{:S(2)}, u32[]{:S(2)}) %collective-permute-start.23) | collective-permute-done | bytes 20512 | tf_op jit(solution)/shard_map/ppermute | solution.py:244
  105.7 0.1 collective-permute-start.24
  105.7 1.2 %collective-permute-done.24 = f32[1,5120]{1,0:T(1,128)S(1)} collective-permute-done((f32[1,5120]{1,0:T(1,128)S(1)}, f32[1,5120]{1,0:T(1,128)S(1)}, u32[]{:S(2)}, u32[]{:S(2)}) %collective-permute-start.24) | collective-permute-done | bytes 20512 | tf_op jit(solution)/shard_map/ppermute | solution.py:244
  107.0 0.6 slice.24
  107.6 0.6 slice.25
  108.2 0.6 all-to-all-done.1
  108.8 2.2 %copy.8 = bf16[1,3,128,16,128]{4,3,2,1,0:T(8,128)(2,1)} copy(bf16[1,3,128,16,128]{4,2,1,3,0:T(8,128)(2,1)S(1)} %bitcast.19) | data formatting | bytes 3145728
  (35 shorter events, 0.5 us)
Async XLA Ops:
  3.6 27.0 %all-to-all-start = ((bf16[8,2,3,128,128]{4,3,2,1,0:T(8,128)(2,1)}), bf16[8,2,3,128,128]{4,3,2,1,0:T(8,128)(2,1)S(1)}, u32[]{:S(2)}, u32[]{:S(2)}) async-start(bf16[8,2,3,128,128]{4,3,2,1,0:T(8,128)(2,1)} %bitcast.1), calls=%async_computation | async-start | bytes 3145728 | tf_op jit(solution)/shard_map/all_to_all | solution.py:285
  30.6 19.3 %collective-permute-start.1 = (bf16[128,3072]{1,0:T(8,128)(2,1)}, bf16[128,3072]{1,0:T(8,128)(2,1)S(1)}, u32[]{:S(2)}, u32[]{:S(2)}) collective-permute-start(bf16[128,3072]{1,0:T(8,128)(2,1)} %bitcast.12), channel_id=1, source_target_pairs={{0,96},{16,112},{32,0},{48,16},{64,32},{80,48},{96,64},{112,80},{1... | collective-permute-start | bytes 2359304 | tf_op jit(solution)/shard_map/ppermute | solution.py:265
  31.7 20.2 %collective-permute-start = (bf16[128,3072]{1,0:T(8,128)(2,1)}, bf16[128,3072]{1,0:T(8,128)(2,1)S(1)}, u32[]{:S(2)}, u32[]{:S(2)}) collective-permute-start(bf16[128,3072]{1,0:T(8,128)(2,1)} %bitcast.13), channel_id=1, source_target_pairs={{0,32},{16,48},{32,64},{48,80},{64,96},{80,112},{96,0},{112,16},{1... | collective-permute-start | bytes 2359304 | tf_op jit(solution)/shard_map/ppermute | solution.py:265
  36.1 26.7 %copy-start = (bf16[1,128,3072]{2,1,0:T(8,128)(2,1)S(1)}, bf16[1,128,3072]{2,1,0:T(8,128)(2,1)}, u32[]{:S(2)}) copy-start(bf16[1,128,3072]{2,1,0:T(8,128)(2,1)} %param.5) | copy-start | bytes 2359300
  36.1 33.0 %copy-start.1 = (f32[3072]{0:T(1024)S(1)}, f32[3072]{0:T(1024)}, u32[]{:S(2)}) copy-start(f32[3072]{0:T(1024)} %param.7) | copy-start | bytes 36868
  36.1 3.7 %collective-permute-start.2 = (f32[8,128]{1,0:T(8,128)S(1)}, f32[8,128]{1,0:T(8,128)S(1)}, u32[]{:S(2)}, u32[]{:S(2)}) collective-permute-start(f32[8,128]{1,0:T(8,128)S(1)} %get-tuple-element.24), channel_id=1, source_target_pairs={{0,1},{1,0},{2,3},{3,2},{4,5},{5,4},{6,7},{7,6},{8,9},{9,8},{10,11... | collective-permute-start | bytes 12296 | tf_op jit(solution)/shard_map/ppermute | solution.py:244
  39.7 5.1 %collective-permute-start.3 = (f32[8,128]{1,0:T(8,128)S(1)}, f32[8,128]{1,0:T(8,128)S(1)}, u32[]{:S(2)}, u32[]{:S(2)}) collective-permute-start(f32[8,128]{1,0:T(8,128)S(1)} %max.24), channel_id=1, source_target_pairs={{0,2},{1,3},{2,0},{3,1},{4,6},{5,7},{6,4},{7,5},{8,10},{9,11},{10,... | collective-permute-start | bytes 12296 | tf_op jit(solution)/shard_map/ppermute | solution.py:244
  44.8 3.6 %collective-permute-start.4 = (f32[8,128]{1,0:T(8,128)S(1)}, f32[8,128]{1,0:T(8,128)S(1)}, u32[]{:S(2)}, u32[]{:S(2)}) collective-permute-start(f32[8,128]{1,0:T(8,128)S(1)} %max.25), channel_id=1, source_target_pairs={{0,4},{1,5},{2,6},{3,7},{4,0},{5,1},{6,2},{7,3},{8,12},{9,13},{10,... | collective-permute-start | bytes 12296 | tf_op jit(solution)/shard_map/ppermute | solution.py:244
  52.0 7.4 %collective-permute-start.9 = (f32[8,128]{1,0:T(8,128)S(1)}, f32[8,128]{1,0:T(8,128)S(1)}, u32[]{:S(2)}, u32[]{:S(2)}) collective-permute-start(f32[8,128]{1,0:T(8,128)S(1)} %max.26), channel_id=1, source_target_pairs={{0,96},{16,112},{32,64},{48,80},{64,32},{80,48},{96,0},{112,16},{1... | collective-permute-start | bytes 12296 | tf_op jit(solution)/shard_map/ppermute | solution.py:244
  52.4 7.1 %collective-permute-start.8 = (f32[8,128]{1,0:T(8,128)S(1)}, f32[8,128]{1,0:T(8,128)S(1)}, u32[]{:S(2)}, u32[]{:S(2)}) collective-permute-start(f32[8,128]{1,0:T(8,128)S(1)} %max.26), channel_id=1, source_target_pairs={{0,64},{16,80},{32,96},{48,112},{64,0},{80,16},{96,32},{112,48},{1... | collective-permute-start | bytes 12296 | tf_op jit(solution)/shard_map/ppermute | solution.py:244
  53.8 5.6 %collective-permute-start.7 = (f32[8,128]{1,0:T(8,128)S(1)}, f32[8,128]{1,0:T(8,128)S(1)}, u32[]{:S(2)}, u32[]{:S(2)}) collective-permute-start(f32[8,128]{1,0:T(8,128)S(1)} %max.26), channel_id=1, source_target_pairs={{0,32},{16,48},{32,0},{48,16},{64,96},{80,112},{96,64},{112,80},{1... | collective-permute-start | bytes 12296 | tf_op jit(solution)/shard_map/ppermute | solution.py:244
  56.2 9.8 %collective-permute-start.5 = (bf16[64,3072]{1,0:T(8,128)(2,1)S(1)}, bf16[64,3072]{1,0:T(8,128)(2,1)S(1)}, u32[]{:S(2)}, u32[]{:S(2)}) collective-permute-start(bf16[64,3072]{1,0:T(8,128)(2,1)S(1)} %slice.18), channel_id=1, source_target_pairs={{0,32},{16,48},{32,64},{48,80},{64,96},{80,112},{96,0},{112,16},{1... | collective-permute-start | bytes 1179656 | tf_op jit(solution)/shard_map/ppermute | solution.py:265
  56.2 9.8 %collective-permute-start.6 = (bf16[64,3072]{1,0:T(8,128)(2,1)S(1)}, bf16[64,3072]{1,0:T(8,128)(2,1)S(1)}, u32[]{:S(2)}, u32[]{:S(2)}) collective-permute-start(bf16[64,3072]{1,0:T(8,128)(2,1)S(1)} %slice.19), channel_id=1, source_target_pairs={{0,96},{16,112},{32,0},{48,16},{64,32},{80,48},{96,64},{112,80},{1... | collective-permute-start | bytes 1179656 | tf_op jit(solution)/shard_map/ppermute | solution.py:265
  59.5 5.1 %collective-permute-start.10 = (f32[8,128]{1,0:T(8,128)S(1)}, f32[8,128]{1,0:T(8,128)S(1)}, u32[]{:S(2)}, u32[]{:S(2)}) collective-permute-start(f32[8,128]{1,0:T(8,128)S(1)} %maximum_select_fusion.1), channel_id=1, source_target_pairs={{0,8},{1,9},{2,10},{3,11},{4,12},{5,13},{6,14},{7,15},{8,0},{9,1},... | collective-permute-start | bytes 12296 | tf_op jit(solution)/shard_map/ppermute | solution.py:244
  62.8 4.8 %collective-permute-start.12 = (bf16[128,3072]{1,0:T(8,128)(2,1)S(1)}, bf16[128,3072]{1,0:T(8,128)(2,1)S(1)}, u32[]{:S(2)}, u32[]{:S(2)}) collective-permute-start(bf16[128,3072]{1,0:T(8,128)(2,1)S(1)} %bitcast.14), channel_id=1, source_target_pairs={{0,16},{16,0},{32,48},{48,32},{64,80},{80,64},{96,112},{112,96},{1... | collective-permute-start | bytes 2359304 | tf_op jit(solution)/shard_map/ppermute | solution.py:244
  62.8 6.3 %collective-permute-start.13 = (bf16[128,3072]{1,0:T(8,128)(2,1)S(1)}, bf16[128,3072]{1,0:T(8,128)(2,1)S(1)}, u32[]{:S(2)}, u32[]{:S(2)}) collective-permute-start(bf16[128,3072]{1,0:T(8,128)(2,1)S(1)} %collective-permute-done.rest_1_), channel_id=1, source_target_pairs={{0,16},{16,0},{32,48},{48,32},{64,80},{80,64},{96,112},{112,96},{1... | collective-permute-start | bytes 2359304 | tf_op jit(solution)/shard_map/ppermute | solution.py:244
  64.7 4.4 %collective-permute-start.14 = (bf16[128,3072]{1,0:T(8,128)(2,1)S(1)}, bf16[128,3072]{1,0:T(8,128)(2,1)S(1)}, u32[]{:S(2)}, u32[]{:S(2)}) collective-permute-start(bf16[128,3072]{1,0:T(8,128)(2,1)S(1)} %collective-permute-done.1.rest_2_), channel_id=1, source_target_pairs={{0,16},{16,0},{32,48},{48,32},{64,80},{80,64},{96,112},{112,96},{1... | collective-permute-start | bytes 2359304 | tf_op jit(solution)/shard_map/ppermute | solution.py:244
  66.0 1.3 %collective-permute-start.11 = (f32[8,128]{1,0:T(8,128)S(1)}, f32[8,128]{1,0:T(8,128)S(1)}, u32[]{:S(2)}, u32[]{:S(2)}) collective-permute-start(f32[8,128]{1,0:T(8,128)S(1)} %max.30), channel_id=1, source_target_pairs={{0,16},{16,0},{32,48},{48,32},{64,80},{80,64},{96,112},{112,96},{1... | collective-permute-start | bytes 12296 | tf_op jit(solution)/shard_map/ppermute | solution.py:244
  66.0 1.9 %collective-permute-start.15 = (bf16[64,3072]{1,0:T(8,128)(2,1)S(1)}, bf16[64,3072]{1,0:T(8,128)(2,1)S(1)}, u32[]{:S(2)}, u32[]{:S(2)}) collective-permute-start(bf16[64,3072]{1,0:T(8,128)(2,1)S(1)} %collective-permute-done.5.rest_3_), channel_id=1, source_target_pairs={{0,16},{16,0},{32,48},{48,32},{64,80},{80,64},{96,112},{112,96},{1... | collective-permute-start | bytes 1179656 | tf_op jit(solution)/shard_map/ppermute | solution.py:244
  67.3 1.7 %collective-permute-start.16 = (bf16[64,3072]{1,0:T(8,128)(2,1)S(1)}, bf16[64,3072]{1,0:T(8,128)(2,1)S(1)}, u32[]{:S(2)}, u32[]{:S(2)}) collective-permute-start(bf16[64,3072]{1,0:T(8,128)(2,1)S(1)} %collective-permute-done.6.rest_4_), channel_id=1, source_target_pairs={{0,16},{16,0},{32,48},{48,32},{64,80},{80,64},{96,112},{112,96},{1... | collective-permute-start | bytes 1179656 | tf_op jit(solution)/shard_map/ppermute | solution.py:244
  73.8 9.2 %collective-permute-start.19 = (f32[1,5120]{1,0:T(1,128)S(1)}, f32[1,5120]{1,0:T(1,128)S(1)}, u32[]{:S(2)}, u32[]{:S(2)}) collective-permute-start(f32[1,5120]{1,0:T(1,128)S(1)} %get-tuple-element.34), channel_id=1, source_target_pairs={{0,96},{16,112},{32,64},{48,80},{64,32},{80,48},{96,0},{112,16},{1... | collective-permute-start | bytes 61448 | tf_op jit(solution)/shard_map/ppermute | solution.py:244
  76.7 6.3 %collective-permute-start.18 = (f32[1,5120]{1,0:T(1,128)S(1)}, f32[1,5120]{1,0:T(1,128)S(1)}, u32[]{:S(2)}, u32[]{:S(2)}) collective-permute-start(f32[1,5120]{1,0:T(1,128)S(1)} %get-tuple-element.34), channel_id=1, source_target_pairs={{0,64},{16,80},{32,96},{48,112},{64,0},{80,16},{96,32},{112,48},{1... | collective-permute-start | bytes 61448 | tf_op jit(solution)/shard_map/ppermute | solution.py:244
  76.7 6.3 %collective-permute-start.17 = (f32[1,5120]{1,0:T(1,128)S(1)}, f32[1,5120]{1,0:T(1,128)S(1)}, u32[]{:S(2)}, u32[]{:S(2)}) collective-permute-start(f32[1,5120]{1,0:T(1,128)S(1)} %get-tuple-element.34), channel_id=1, source_target_pairs={{0,32},{16,48},{32,0},{48,16},{64,96},{80,112},{96,64},{112,80},{1... | collective-permute-start | bytes 61448 | tf_op jit(solution)/shard_map/ppermute | solution.py:244
  83.0 25.7 %all-to-all-start.1 = ((bf16[8,2,3,128,128]{4,3,2,1,0:T(8,128)(2,1)}), bf16[8,2,3,128,128]{4,3,2,1,0:T(8,128)(2,1)S(1)}, u32[]{:S(2)}, u32[]{:S(2)}) async-start(bf16[8,2,3,128,128]{4,3,2,1,0:T(8,128)(2,1)} %attend_backward.1), calls=%async_computation.1 | async-start | bytes 3145728 | tf_op jit(solution)/shard_map/all_to_all | solution.py:313
  87.2 3.8 %collective-permute-start.20 = (f32[1,5120]{1,0:T(1,128)S(1)}, f32[1,5120]{1,0:T(1,128)S(1)}, u32[]{:S(2)}, u32[]{:S(2)}) collective-permute-start(f32[1,5120]{1,0:T(1,128)S(1)} %add_add_fusion), channel_id=1, source_target_pairs={{0,1},{1,0},{2,3},{3,2},{4,5},{5,4},{6,7},{7,6},{8,9},{9,8},{10,11... | collective-permute-start | bytes 61448 | tf_op jit(solution)/shard_map/ppermute | solution.py:244
  91.0 5.4 %collective-permute-start.21 = (f32[1,5120]{1,0:T(1,128)S(1)}, f32[1,5120]{1,0:T(1,128)S(1)}, u32[]{:S(2)}, u32[]{:S(2)}) collective-permute-start(f32[1,5120]{1,0:T(1,128)S(1)} %add.31), channel_id=1, source_target_pairs={{0,2},{1,3},{2,0},{3,1},{4,6},{5,7},{6,4},{7,5},{8,10},{9,11},{10,... | collective-permute-start | bytes 61448 | tf_op jit(solution)/shard_map/ppermute | solution.py:244
  96.4 3.9 %collective-permute-start.22 = (f32[1,5120]{1,0:T(1,128)S(1)}, f32[1,5120]{1,0:T(1,128)S(1)}, u32[]{:S(2)}, u32[]{:S(2)}) collective-permute-start(f32[1,5120]{1,0:T(1,128)S(1)} %add.32), channel_id=1, source_target_pairs={{0,4},{1,5},{2,6},{3,7},{4,0},{5,1},{6,2},{7,3},{8,12},{9,13},{10,... | collective-permute-start | bytes 61448 | tf_op jit(solution)/shard_map/ppermute | solution.py:244
  100.3 5.4 %collective-permute-start.23 = (f32[1,5120]{1,0:T(1,128)S(1)}, f32[1,5120]{1,0:T(1,128)S(1)}, u32[]{:S(2)}, u32[]{:S(2)}) collective-permute-start(f32[1,5120]{1,0:T(1,128)S(1)} %add.33), channel_id=1, source_target_pairs={{0,8},{1,9},{2,10},{3,11},{4,12},{5,13},{6,14},{7,15},{8,0},{9,1},... | collective-permute-start | bytes 61448 | tf_op jit(solution)/shard_map/ppermute | solution.py:244
  105.7 1.3 %collective-permute-start.24 = (f32[1,5120]{1,0:T(1,128)S(1)}, f32[1,5120]{1,0:T(1,128)S(1)}, u32[]{:S(2)}, u32[]{:S(2)}) collective-permute-start(f32[1,5120]{1,0:T(1,128)S(1)} %add.34), channel_id=1, source_target_pairs={{0,16},{16,0},{32,48},{48,32},{64,80},{80,64},{96,112},{112,96},{1... | collective-permute-start | bytes 61448 | tf_op jit(solution)/shard_map/ppermute | solution.py:244
